TPU v7x, 256 devices: a whole 4x4x8 slice. The times are simulated.
256 devices in a mesh: rep: 8 (over x, z_hi), fsdp: 32 (over z_lo, y, core).
Axes of the slice: x: 4, y: 4, z: 8 (z_hi: 2, z_lo: 4; z = z_hi * 4 + z_lo), core: 2. Of those that a mesh axis runs over, the one named last changes fastest.
Arguments:
- inputs: bfloat16 [32768, 8192], P(('rep', 'fsdp')), may hold values from -24 to 24
- cotangent: bfloat16 [32768, 512], P(('rep', 'fsdp')), may hold values from -6 to 6
- value_weight: bfloat16 [65536, 512], P(('rep', 'fsdp')), may hold values from -0.0625 to 0.0625
- norm_gain: float32 [65536], P('rep'), may hold values from 0.1 to 1.9
- outer_delta: float32 [65536, 1024], P(('rep', 'fsdp')), may hold values from -4 to 4
- outer_params: float32 [8192, 1024], P('fsdp', 'rep'), may hold values from -6 to 6
- outer_moment: float32 [8192, 1024], P('fsdp', 'rep'), may hold values from -4 to 4
Outputs:
- values: float32 [32768, 512], P(('rep', 'fsdp'))
- input_grad: float32 [32768, 8192], P(('rep', 'fsdp'))
- weight_grad: float32 [65536, 512], P(('rep', 'fsdp'))
- gain_grad: float32 [65536], P(('rep', 'fsdp'))
- new_params: float32 [8192, 1024], P('fsdp', 'rep')
- new_moment: float32 [8192, 1024], P('fsdp', 'rep')
All inputs are finite; a program needn't handle non-finite values.
Results may differ from a plain program's by a relative error of at most 0.0029.
Values may be sent and summed in bfloat16 or wider, within the bound.
No kernel may reach another device: no remote copies, remote signals or barrier semaphores. Data moves between devices by JAX's collectives and lax.ppermute only.
A program may use at most 128 MiB of HBM per device.

v0:
```python
import math

import jax
import jax.numpy as jnp
from jax import lax
from jax.sharding import PartitionSpec as P


def outer_update(average, params, moment):
    new_moment = 0.9 * moment + average
    new_params = params - 0.7 * (average + 0.9 * new_moment)
    return (new_params, new_moment)


def shards(inputs, cotangent, value_weight, norm_gain, outer_delta, outer_params, outer_moment):
    rows = inputs.shape[0]
    groups = lax.axis_size("rep")
    floats = inputs.astype(jnp.float32)
    scale = lax.rsqrt(jnp.mean(floats * floats, axis=-1, keepdims=True) + 1e-05)
    normed = floats * scale
    hidden = (normed * norm_gain).astype(jnp.bfloat16)
    gathered = lax.all_gather(value_weight, "fsdp", axis=0, tiled=True)
    values = jnp.dot(hidden, gathered, preferred_element_type=jnp.float32)
    hidden_grad = lax.dot_general(
        cotangent, gathered, (((1,), (1,)), ((), ())), preferred_element_type=jnp.float32
    )
    scaled = hidden_grad * norm_gain
    input_grad = scale * (scaled - normed * jnp.mean(scaled * normed, axis=-1, keepdims=True))
    weight_term = lax.dot_general(
        hidden, cotangent, (((0,), (0,)), ((), ())), preferred_element_type=jnp.float32
    )
    gain_term = jnp.sum(hidden_grad * normed, axis=0)
    weight_sum, gain_sum = (
        lax.psum_scatter(weight_term, "fsdp", scatter_dimension=0, tiled=True),
        lax.psum_scatter(gain_term, "fsdp", scatter_dimension=0, tiled=True),
    )
    scale_grad = 1.0 / math.sqrt(rows * lax.axis_size("fsdp"))
    count = outer_params.shape[1]
    total = lax.psum(outer_delta, "rep")
    first = lax.axis_index("rep") * count
    own_cols = lax.dynamic_slice_in_dim(total, first, count, 1)
    new_params, new_moment = outer_update(own_cols / groups, outer_params, outer_moment)
    return (
        values,
        input_grad,
        weight_sum * scale_grad,
        gain_sum * scale_grad,
        new_params,
        new_moment,
    )


def solution(mesh):
    in_specs = (
        P(("rep", "fsdp"), None),
        P(("rep", "fsdp"), None),
        P(("rep", "fsdp"), None),
        P("rep"),
        P(("rep", "fsdp"), None),
        P("fsdp", "rep"),
        P("fsdp", "rep"),
    )
    out_specs = (
        P(("rep", "fsdp"), None),
        P(("rep", "fsdp"), None),
        P(("rep", "fsdp"), None),
        P(("rep", "fsdp")),
        P("fsdp", "rep"),
        P("fsdp", "rep"),
    )
    return jax.shard_map(shards, mesh=mesh, in_specs=in_specs, out_specs=out_specs, check_vma=False)
```

profile of v0, /device:TPU:2, one launch (start us, length us, event | category | flops | bytes accessed | tf_op | source)
XLA Modules:
  0.0 340.0 jit_solution(4454484413418516107)
XLA Ops:
  8.0 0.0 copy-start
  8.0 0.0 copy-start.1
  8.0 0.0 all-reduce.3.cloned.1.call-start
  8.1 0.7 all-reduce.3.cloned.1.call-update
  8.8 0.0 all-gather.2.cloned.1.call-start
  8.8 0.5 all-gather.2.cloned.1.call-update
  9.3 0.0 reduce-scatter.2.cloned.1.call-start
  9.4 2.1 fusion.9
  11.5 0.0 copy-done
  11.5 0.0 copy-done.1
  11.5 8.9 %fusion.10 = f32[8192,512]{1,0:T(8,128)} fusion(bf16[128,512]{1,0:T(8,128)(2,1)S(1)} %copy-done, bf16[128,8192]{1,0:T(8,128)(2,1)S(1)} %copy-done.1, f32[8192]{0:T(1024)} %param.10, f32[128]{0:T(128)S(1)} %add_rsqrt_fusion), kind=kOutput, calls=%fused_computation.12 | convolution fusion | flops 1077936128 | bytes 19038720 | tf_op jit(solution)/shard_map/dot_general | solution.py:29
  20.4 0.0 copy-start.6
  20.4 0.0 copy-start.4
  20.4 0.0 copy-start.5
  20.4 0.0 copy-start.3
  20.4 0.0 reduce-scatter.2.cloned.1.call-update
  20.5 0.6 copy-done.6
  21.1 0.6 dynamic-slice
  22.3 141.2 %all-reduce.3.cloned.1.call-done = f32[256,1024]{1,0:T(8,128)} async-done(((f32[256,1024]{1,0:T(8,128)}), f32[256,1024]{1,0:T(8,128)}) %all-reduce.3.cloned.1.call-update) | async-done | bytes 1048592 | tf_op jit(solution)/shard_map/psum | solution.py:39
  163.6 0.0 copy-done.4
  163.6 0.0 copy-done.5
  163.6 1.6 multiply_subtract_fusion
  165.2 0.0 all-gather.2.cloned.1.call-done
  165.2 0.0 copy-done.3
  165.2 8.3 %fusion.8 = (f32[8192]{0:T(1024)S(1)}, f32[128]{0:T(128)S(1)}, f32[128,8192]{1,0:T(8,128)}) fusion(bf16[128,8192]{1,0:T(8,128)(2,1)S(1)} %copy-done.1, f32[128]{0:T(128)S(1)} %add_rsqrt_fusion, f32[8192]{0:T(1024)S(1)} %copy-done.3, bf16[128,512]{1,0:T(8,128)(2,1)S(1)} %copy-done, bf16[8192,512]{1,0:T(8,128)(2,1)} %all-gather.2.cloned.1.call-done), kind=kOutput, calls=%fused_computation.10 | convolution fusion | flops 1081073536 | bytes 14877696 | tf_op jit(solution)/shard_map/dot_general | solution.py:24
  173.5 133.7 %all-reduce = f32[8192]{0:T(1024)S(1)} all-reduce(f32[8192]{0:T(1024)S(1)} %get-tuple-element.6), channel_id=3, replica_groups=mesh['rep'=8,'fsdp'=32] {'fsdp'}, use_global_device_ids=true, to_apply=%region_4.0.clone | all-reduce | flops 8192 | bytes 65536
  307.2 0.6 dynamic-slice_multiply_fusion.1
  307.8 0.0 copy-start.2
  307.8 5.7 %fusion.12 = f32[128,512]{1,0:T(8,128)} fusion(bf16[8192,512]{1,0:T(8,128)(2,1)} %all-gather.2.cloned.1.call-done, bf16[128,8192]{1,0:T(8,128)(2,1)S(1)} %copy-done.1, f32[8192]{0:T(1024)S(1)} %copy-done.3, f32[128]{0:T(128)S(1)} %add_rsqrt_fusion), kind=kOutput, calls=%fused_computation.13 | convolution fusion | flops 1077936128 | bytes 10781184 | tf_op jit(solution)/shard_map/dot_general | solution.py:23
  313.5 0.0 copy-done.2
  313.5 2.9 fusion.7
  316.4 14.3 %reduce-scatter.2.cloned.1.call-done = f32[256,512]{1,0:T(8,128)} async-done(((f32[8192,512]{1,0:T(8,128)}), f32[256,512]{1,0:T(8,128)}) %reduce-scatter.2.cloned.1.call-update) | async-done | bytes 524304 | tf_op jit(solution)/shard_map/reduce_scatter | solution.py:34
  330.7 1.9 broadcast_multiply_fusion
  (2 shorter events, 0.0 us)
Async XLA Ops:
  8.0 3.5 %copy-start = (bf16[128,512]{1,0:T(8,128)(2,1)S(1)}, bf16[128,512]{1,0:T(8,128)(2,1)}, u32[]{:S(2)}) copy-start(bf16[128,512]{1,0:T(8,128)(2,1)} %param.8) | copy-start | bytes 393220
  8.0 3.5 %copy-start.1 = (bf16[128,8192]{1,0:T(8,128)(2,1)S(1)}, bf16[128,8192]{1,0:T(8,128)(2,1)}, u32[]{:S(2)}) copy-start(bf16[128,8192]{1,0:T(8,128)(2,1)} %param.7) | copy-start | bytes 6291460
  8.0 155.6 %all-reduce.3.cloned.1.call-start = ((), (), s32[]{:S(2)}) async-start(), calls=%async_computation.3 | async-start | bytes 2097152 | tf_op jit(solution)/shard_map/psum | solution.py:39
  8.8 156.5 %all-gather.2.cloned.1.call-start = ((), (), s32[]{:S(2)}) async-start(), calls=%async_computation.1 | async-start | bytes 8650752 | tf_op jit(solution)/shard_map/all_gather | solution.py:22
  9.3 321.4 %reduce-scatter.2.cloned.1.call-start = ((), (), s32[]{:S(2)}) async-start(), calls=%async_computation.2 | async-start | bytes 17301504 | tf_op jit(solution)/shard_map/reduce_scatter | solution.py:34
  20.4 0.7 copy-start.6
  20.4 143.2 %copy-start.4 = (f32[256,128]{1,0:T(8,128)S(1)}, f32[256,128]{1,0:T(8,128)}, u32[]{:S(2)}) copy-start(f32[256,128]{1,0:T(8,128)} %param.12) | copy-start | bytes 393220
  20.4 143.2 %copy-start.5 = (f32[256,128]{1,0:T(8,128)S(1)}, f32[256,128]{1,0:T(8,128)}, u32[]{:S(2)}) copy-start(f32[256,128]{1,0:T(8,128)} %param.13) | copy-start | bytes 393220
  20.4 144.8 %copy-start.3 = (f32[8192]{0:T(1024)S(1)}, f32[8192]{0:T(1024)}, u32[]{:S(2)}) copy-start(f32[8192]{0:T(1024)} %param.10) | copy-start | bytes 98308
  307.8 5.7 %copy-start.2 = (f32[128,8192]{1,0:T(8,128)S(1)}, f32[128,8192]{1,0:T(8,128)}, u32[]{:S(2)}) copy-start(f32[128,8192]{1,0:T(8,128)} %get-tuple-element.10) | copy-start | bytes 12582916
Sparse Core Ops, SparseCore 0:
  11.5 152.0 all-reduce.2
Sparse Core Ops, SparseCore 1:
  11.1 123.6 all-gather.1
  137.1 193.5 reduce-scatter.1
where the time goes:
time: 340 us
  waiting for transfers between devices  157 us (46%)
  blocking collectives  134 us (39%)
  matrix products  22.9 us (7%)
  between operations  16.2 us (5%)
  other arithmetic  9.18 us (3%)
    psum x1, waiting for transfers between devices, shards(): total = lax.psum(outer_delta, 'rep')  141 us
    unnamed x1, blocking collectives  134 us
    reduce_scatter x1, waiting for transfers between devices, shards(): lax.psum_scatter(weight_term, 'fsdp', scatter_dimension=0, tiled=True)  14.3 us
    dot_general x1, matrix products, shards(): lax.dot_general(hidden, cotangent, (((0,), (0,)), ((), ())), preferred_el...  8.93 us
    dot_general x1, matrix products, shards(): lax.dot_general(cotangent, gathered, (((1,), (1,)), ((), ())), preferred_...  8.29 us
  transfers between devices with their start and end apart: 3, of which 2 were waited for; matrix products, arithmetic and copies ran while one was open for 9% of the time, Pallas kernels for 0%

commit v1 on v0

v1 whole, which is shorter than its diff:
```python
import functools
import math

import jax
import jax.numpy as jnp
from jax import lax
from jax.experimental import pallas as pl
from jax.experimental.pallas import tpu as pltpu
from jax.sharding import PartitionSpec as P

F32 = jnp.float32
BF16 = jnp.bfloat16

NZ, NY, NC, NX = 4, 4, 2, 4
PLANE = NY * NC
OFFSETS = [(dy, dc) for dy in range(NY) for dc in range(NC)]
SENDS = [(1, 0), (3, 0), (1, 1), (3, 1), (2, 0), (2, 1), (0, 1)]


def split_index(index):
    return index // PLANE, (index // NC) % NY, index % NC


def fsdp_perm(dz, dy, dc):
    pairs = []
    for source in range(NZ * PLANE):
        z, y, c = split_index(source)
        target = ((z + dz) % NZ) * PLANE + ((y + dy) % NY) * NC + (c ^ dc)
        pairs.append((source, target))
    return pairs


def rep_perm(dx, dh):
    return [
        (x * 2 + h, ((x + dx) % NX) * 2 + (h ^ dh)) for x in range(NX) for h in range(2)
    ]


def send(array, dz=0, dy=0, dc=0):
    return lax.ppermute(array, "fsdp", fsdp_perm(dz % NZ, dy % NY, dc))


def vmem_params(mib=48):
    return pltpu.CompilerParams(vmem_limit_bytes=mib * 2**20)


def feature_start(position, dz, dy, dc, rows):
    z, y, c = position
    owner = ((z + dz) % NZ) * PLANE + ((y + dy) % NY) * NC + (c ^ dc)
    return pl.multiple_of(owner * rows, rows)


def norm_kernel(place, x_ref, gain_ref, scale_ref, *out_refs):
    position = (place[0], place[1], place[2])
    floats = x_ref[...].astype(F32)
    mean = jnp.mean(floats * floats, axis=-1, keepdims=True)
    scale = lax.rsqrt(mean + 1e-05)
    scale_ref[...] = scale
    rows = x_ref.shape[1] // (NZ * PLANE)
    for (dy, dc), out in zip(OFFSETS, out_refs):
        for dz in range(NZ):
            at = pl.ds(feature_start(position, dz, dy, dc, rows), rows)
            normed = x_ref[:, at].astype(F32) * scale
            out[:, dz * rows : (dz + 1) * rows] = (normed * gain_ref[:, at]).astype(BF16)


def make_hidden(place, inputs, gain):
    tokens, width = inputs.shape
    step = 32
    block = width // PLANE
    return pl.pallas_call(
        norm_kernel,
        grid=(tokens // step,),
        in_specs=[
            pl.BlockSpec(memory_space=pltpu.SMEM),
            pl.BlockSpec((step, width), lambda i: (i, 0)),
            pl.BlockSpec((1, width), lambda i: (0, 0)),
        ],
        out_specs=[pl.BlockSpec((step, 1), lambda i: (i, 0))]
        + [pl.BlockSpec((step, block), lambda i: (i, 0))] * PLANE,
        out_shape=[jax.ShapeDtypeStruct((tokens, 1), F32)]
        + [jax.ShapeDtypeStruct((tokens, block), BF16)] * PLANE,
        compiler_params=vmem_params(),
        cost_estimate=pl.CostEstimate(
            flops=6 * tokens * width, bytes_accessed=4 * tokens * width, transcendentals=0
        ),
        name="norm",
    )(place, inputs, gain)


def hidden_grad_kernel(*refs):
    cots, weights, outs = refs[:PLANE], refs[PLANE : PLANE + NZ], refs[PLANE + NZ :]
    for cot, out in zip(cots, outs):
        for dz, weight in enumerate(weights):
            rows = weight.shape[0]
            out[:, dz * rows : (dz + 1) * rows] = lax.dot_general(
                cot[...], weight[...], (((1,), (1,)), ((), ())), preferred_element_type=F32
            ).astype(BF16)


def make_hidden_grad(cots, weights):
    tokens, inner = cots[0].shape
    block = NZ * weights[0].shape[0]
    return pl.pallas_call(
        hidden_grad_kernel,
        out_shape=[jax.ShapeDtypeStruct((tokens, block), BF16)] * PLANE,
        compiler_params=vmem_params(),
        cost_estimate=pl.CostEstimate(
            flops=2 * PLANE * tokens * inner * block,
            bytes_accessed=2 * PLANE * tokens * (inner + block) + 2 * block * inner,
            transcendentals=0,
        ),
        name="hidden_grad",
    )(*cots, *weights)


def weight_kernel(*refs):
    hiddens, cots, outs = refs[:PLANE], refs[PLANE : 2 * PLANE], refs[2 * PLANE :]
    cot = jnp.concatenate([ref[...] for ref in cots], axis=0)
    rows = outs[0].shape[0]
    for dz, out in enumerate(outs):
        hidden = jnp.concatenate(
            [ref[:, dz * rows : (dz + 1) * rows] for ref in hiddens], axis=0
        )
        out[...] = lax.dot_general(
            hidden, cot, (((0,), (0,)), ((), ())), preferred_element_type=F32
        ).astype(out.dtype)


def make_weight_terms(hiddens, cots):
    tokens, block = hiddens[0].shape
    inner = cots[0].shape[1]
    rows = block // NZ
    return pl.pallas_call(
        weight_kernel,
        out_shape=[
            jax.ShapeDtypeStruct((rows, inner), F32 if dz == 0 else BF16) for dz in range(NZ)
        ],
        compiler_params=vmem_params(),
        cost_estimate=pl.CostEstimate(
            flops=2 * PLANE * tokens * inner * block,
            bytes_accessed=2 * PLANE * tokens * (inner + block) + 3 * block * inner,
            transcendentals=0,
        ),
        name="weight_terms",
    )(*hiddens, *cots)


def values_kernel(*refs):
    hiddens, weights, outs = refs[:PLANE], refs[PLANE : PLANE + NZ], refs[PLANE + NZ :]
    weight = jnp.concatenate([ref[...] for ref in weights], axis=0)
    for (dy, dc), hidden in zip(OFFSETS, hiddens):
        outs[dc][dy] = jnp.dot(hidden[...], weight, preferred_element_type=F32)


def make_value_terms(hiddens, weights):
    tokens, block = hiddens[0].shape
    inner = weights[0].shape[1]
    return pl.pallas_call(
        values_kernel,
        out_shape=[jax.ShapeDtypeStruct((NY, tokens, inner), F32)] * NC,
        compiler_params=vmem_params(),
        cost_estimate=pl.CostEstimate(
            flops=2 * PLANE * tokens * inner * block,
            bytes_accessed=2 * PLANE * tokens * (2 * inner + block) + 2 * block * inner,
            transcendentals=0,
        ),
        name="value_terms",
    )(*hiddens, *weights)


def input_grad_kernel(place, x_ref, gain_ref, scale_ref, *refs):
    grads, out_ref = refs[:PLANE], refs[PLANE]
    position = (place[0], place[1], place[2])
    width = x_ref.shape[1]
    rows = width // (NZ * PLANE)
    scale = scale_ref[...]
    total = jnp.zeros((x_ref.shape[0], rows), F32)
    for (dy, dc), grad in zip(OFFSETS, grads):
        for dz in range(NZ):
            at = pl.ds(feature_start(position, dz, dy, dc, rows), rows)
            scaled = grad[:, dz * rows : (dz + 1) * rows].astype(F32) * gain_ref[:, at]
            total += scaled * (x_ref[:, at].astype(F32) * scale)
    mean = jnp.sum(total, axis=-1, keepdims=True) * (1.0 / width)
    for (dy, dc), grad in zip(OFFSETS, grads):
        for dz in range(NZ):
            at = pl.ds(feature_start(position, dz, dy, dc, rows), rows)
            scaled = grad[:, dz * rows : (dz + 1) * rows].astype(F32) * gain_ref[:, at]
            normed = x_ref[:, at].astype(F32) * scale
            out_ref[:, at] = scale * (scaled - normed * mean)


def make_input_grad(place, inputs, gain, scale, grads):
    tokens, width = inputs.shape
    step = 32
    block = width // PLANE
    return pl.pallas_call(
        input_grad_kernel,
        grid=(tokens // step,),
        in_specs=[
            pl.BlockSpec(memory_space=pltpu.SMEM),
            pl.BlockSpec((step, width), lambda i: (i, 0)),
            pl.BlockSpec((1, width), lambda i: (0, 0)),
            pl.BlockSpec((step, 1), lambda i: (i, 0)),
        ]
        + [pl.BlockSpec((step, block), lambda i: (i, 0))] * PLANE,
        out_specs=pl.BlockSpec((step, width), lambda i: (i, 0)),
        out_shape=jax.ShapeDtypeStruct((tokens, width), F32),
        compiler_params=vmem_params(),
        cost_estimate=pl.CostEstimate(
            flops=12 * tokens * width, bytes_accessed=8 * tokens * width, transcendentals=0
        ),
        name="input_grad",
    )(place, inputs, gain, scale, *grads)


def outer_step(delta, params, moment):
    groups = lax.axis_size("rep")
    rep = lax.axis_index("rep")
    x, half = rep // 2, rep % 2
    count = params.shape[1]
    parts = []
    for dx in (1, 3, 2):
        piece = lax.dynamic_slice_in_dim(delta, ((x + dx) % NX) * 2 * count, 2 * count, 1)
        parts.append(lax.ppermute(piece, "rep", rep_perm(dx, 0)))
    total = lax.dynamic_slice_in_dim(delta, x * 2 * count, 2 * count, 1)
    for part in parts:
        total = total + part
    other = lax.dynamic_slice_in_dim(total, (1 - half) * count, count, 1)
    mine = lax.dynamic_slice_in_dim(total, half * count, count, 1)
    average = (mine + lax.ppermute(other, "rep", rep_perm(0, 1))) / groups
    new_moment = 0.9 * moment + average
    new_params = params - 0.7 * (average + 0.9 * new_moment)
    return new_params, new_moment


def shards(inputs, cotangent, value_weight, norm_gain, outer_delta, outer_params, outer_moment):
    index = lax.axis_index("fsdp")
    z, y, c = split_index(index)
    place = jnp.stack([z, y, c]).astype(jnp.int32)
    gain = norm_gain.reshape(1, -1)
    rows = value_weight.shape[0]

    same = [cotangent] + [send(cotangent, dy=dy) for dy in (1, 2, 3)]
    weights = [value_weight] + [send(value_weight, dz=-dz) for dz in (1, 2, 3)]
    swapped = send(jnp.stack(same), dc=1)
    cots = []
    for dy in range(NY):
        cots += [same[dy], swapped[dy]]

    scale, *mine = make_hidden(place, inputs, gain)
    own_blocks = dict(zip(OFFSETS, mine))
    got = {(0, 0): own_blocks[0, 0]}
    for dy, dc in SENDS:
        got[dy, dc] = send(own_blocks[dy, dc], dy=dy, dc=dc)
    hiddens = [got[offset] for offset in OFFSETS]

    grads = dict(zip(OFFSETS, make_hidden_grad(cots, weights)))
    back = {(0, 0): grads[0, 0]}
    for dy, dc in SENDS:
        back[dy, dc] = send(grads[dy, dc], dy=-dy, dc=dc)
    input_grad = make_input_grad(
        place, inputs, gain, scale, [back[offset] for offset in OFFSETS]
    )

    terms = make_weight_terms(hiddens, cots)
    weight_sum = terms[0]
    for dz in (1, 2, 3):
        weight_sum = weight_sum + send(terms[dz], dz=dz).astype(F32)
    scale_grad = 1.0 / math.sqrt(inputs.shape[0] * lax.axis_size("fsdp"))
    weight_grad = weight_sum * scale_grad
    own_gain = lax.dynamic_slice_in_dim(norm_gain, index * rows, rows, 0)
    gain_grad = jnp.sum(weight_grad * value_weight.astype(F32), axis=1) / own_gain

    keep, give = make_value_terms(hiddens, weights)
    pair = keep + send(give, dc=1)
    values = pair[0]
    for dy in (1, 2, 3):
        values = values + send(pair[dy].astype(BF16), dy=-dy).astype(F32)

    new_params, new_moment = outer_step(outer_delta, outer_params, outer_moment)
    return values, input_grad, weight_grad, gain_grad, new_params, new_moment


def solution(mesh):
    rows = P(("rep", "fsdp"), None)
    in_specs = (rows, rows, rows, P("rep"), rows, P("fsdp", "rep"), P("fsdp", "rep"))
    out_specs = (rows, rows, rows, P(("rep", "fsdp")), P("fsdp", "rep"), P("fsdp", "rep"))
    return jax.shard_map(shards, mesh=mesh, in_specs=in_specs, out_specs=out_specs, check_vma=False)
```

time: 340 us -> 147 us (0.43)
  the two profiles are of different devices: /device:TPU:2 before, /device:TPU:166 now
where the time goes in v1:
time: 147 us; the launch traced here: 146 us
  waiting for transfers between devices  52.5 us (36%)
  starting transfers between devices  37.5 us (26%)
  local copies, waits for them, and re-layouts  30.3 us (21%)
  Pallas kernels  15.3 us (10%)
  other arithmetic  9.66 us (7%)
    ppermute x28, waiting for transfers between devices, send(): return lax.ppermute(array, 'fsdp', fsdp_perm(dz % NZ, dy % NY, dc))  40.6 us
    ppermute x28, starting transfers between devices, send(): return lax.ppermute(array, 'fsdp', fsdp_perm(dz % NZ, dy % NY, dc))  34.6 us
    unnamed x122, local copies, waits for them, and re-layouts  27.9 us
    ppermute x1, waiting for transfers between devices, outer_step(): average = (mine + lax.ppermute(other, 'rep', rep_perm(0, 1))) / groups  11.9 us
    pallas_call x1, Pallas kernels, make_input_grad(): pl.pallas_call(input_grad_kernel, grid=(tokens // step,), in_specs=[pl.Bl...  4.8 us
    pallas_call x1, Pallas kernels, make_hidden_grad(): pl.pallas_call(hidden_grad_kernel, out_shape=[jax.ShapeDtypeStruct((token...  3.52 us
  transfers between devices with their start and end apart: 32, of which 14 were waited for; matrix products, arithmetic and copies ran while one was open for 7% of the time, Pallas kernels for 10%

profile of v1, /device:TPU:166, one launch (start us, length us, event | category | flops | bytes accessed | tf_op | source)
XLA Modules:
  0.0 146.3 jit_solution(17954101113339672212)
XLA Ops:
  0.6 1.1 collective-permute-start.9
  1.7 2.4 %collective-permute-start.8 = (bf16[256,512]{1,0:T(8,128)(2,1)}, bf16[256,512]{1,0:T(8,128)(2,1)S(1)}, u32[]{:S(2)}, u32[]{:S(2)}) collective-permute-start(bf16[256,512]{1,0:T(8,128)(2,1)} %refs_8_.4), channel_id=1, source_target_pairs={{0,16},{1,17},{2,18},{3,19},{4,20},{5,21},{6,22},{7,23},{8,24},{9,... | collective-permute-start | bytes 786440 | tf_op jit(solution)/shard_map/ppermute | solution.py:40
  4.1 3.0 %collective-permute-start.16 = (bf16[128,512]{1,0:T(8,128)(2,1)}, bf16[128,512]{1,0:T(8,128)(2,1)S(1)}, u32[]{:S(2)}, u32[]{:S(2)}) collective-permute-start(bf16[128,512]{1,0:T(8,128)(2,1)} %refs_8_.5), channel_id=1, source_target_pairs={{0,6},{1,7},{2,0},{3,1},{4,2},{5,3},{6,4},{7,5},{8,14},{9,15},{10,... | collective-permute-start | bytes 393224 | tf_op jit(solution)/shard_map/ppermute | solution.py:40
  7.7 1.0 collective-permute-start.14
  8.8 1.6 %copy-done = bf16[128,8192]{1,0:T(8,128)(2,1)S(1)} copy-done((bf16[128,8192]{1,0:T(8,128)(2,1)S(1)}, bf16[128,8192]{1,0:T(8,128)(2,1)}, u32[]{:S(2)}) %copy-start) | copy-done | bytes 2097176
  11.1 2.8 %norm.1 = (f32[128,1]{1,0:T(8,128)S(1)}, bf16[128,1024]{1,0:T(8,128)(2,1)S(1)}, bf16[128,1024]{1,0:T(8,128)(2,1)S(1)}, bf16[128,1024]{1,0:T(8,128)(2,1)S(1)}, bf...) custom-call(s32[3]{0:T(128)S(1)} %pad_add_fusion.place, ...), custom_call_target="tpu_custom_call" | custom-call | flops 6291456 | bytes 4194304 | tf_op jit(solution)/shard_map/norm/pallas_call | solution.py:71
  14.7 1.3 collective-permute-done.14.refs_2_.refs_10_
  16.2 1.8 %pad_maximum_fusion = bf16[4,128,512]{2,1,0:T(8,128)(2,1)} fusion(bf16[1,128,512]{2,1,0:T(8,128)(2,1)S(1)} %bitcast.33, bf16[1,128,512]{2,1,0:T(8,128)(2,1)S(1)} %bitcast.34, bf16[1,128,512]{2,1,0:T(8,128)(2,1)S(1)} %bitcast.35, bf16[1,128,512]{2,1,0:T(8,128)(2,1)} %bitcast.32), kind=kLoop, calls=%fused_computation | loop fusion | flops 786432 | bytes 1048576 | tf_op jit(solution)/shard_map/stack | solution.py:246
  18.0 6.5 %collective-permute-done.8.refs_10_ = bf16[256,512]{1,0:T(8,128)(2,1)S(1)} collective-permute-done((bf16[256,512]{1,0:T(8,128)(2,1)}, bf16[256,512]{1,0:T(8,128)(2,1)S(1)}, u32[]{:S(2)}, u32[]{:S(2)}) %collective-permute-start.8) | collective-permute-done | bytes 262176 | tf_op jit(solution)/shard_map/ppermute | solution.py:40
  24.5 2.6 %collective-permute-done.7.refs_9_ = bf16[256,512]{1,0:T(8,128)(2,1)S(1)} collective-permute-done((bf16[256,512]{1,0:T(8,128)(2,1)}, bf16[256,512]{1,0:T(8,128)(2,1)S(1)}, u32[]{:S(2)}, u32[]{:S(2)}) %collective-permute-start.7) | collective-permute-done | bytes 262176 | tf_op jit(solution)/shard_map/ppermute | solution.py:40
  27.8 3.2 %collective-permute-start.3 = (bf16[128,1024]{1,0:T(8,128)(2,1)}, bf16[128,1024]{1,0:T(8,128)(2,1)S(1)}, u32[]{:S(2)}, u32[]{:S(2)}) collective-permute-start(bf16[128,1024]{1,0:T(8,128)(2,1)} %get-tuple-element.33), channel_id=1, source_target_pairs={{0,4},{1,5},{2,6},{3,7},{4,0},{5,1},{6,2},{7,3},{8,12},{9,13},{10,... | collective-permute-start | bytes 786440 | tf_op jit(solution)/shard_map/ppermute | solution.py:40
  31.0 2.5 %collective-permute-start.5 = (bf16[128,1024]{1,0:T(8,128)(2,1)}, bf16[128,1024]{1,0:T(8,128)(2,1)S(1)}, u32[]{:S(2)}, u32[]{:S(2)}) collective-permute-start(bf16[128,1024]{1,0:T(8,128)(2,1)} %get-tuple-element.35), channel_id=1, source_target_pairs={{0,6},{1,7},{2,0},{3,1},{4,2},{5,3},{6,4},{7,5},{8,14},{9,15},{10,... | collective-permute-start | bytes 786440 | tf_op jit(solution)/shard_map/ppermute | solution.py:40
  33.5 1.0 collective-permute-start.6
  34.5 1.2 constant_dynamic-slice_fusion.3
  35.7 2.9 %collective-permute-done.3.refs_4_ = bf16[128,1024]{1,0:T(8,128)(2,1)S(1)} collective-permute-done((bf16[128,1024]{1,0:T(8,128)(2,1)}, bf16[128,1024]{1,0:T(8,128)(2,1)S(1)}, u32[]{:S(2)}, u32[]{:S(2)}) %collective-permute-start.3) | collective-permute-done | bytes 262176 | tf_op jit(solution)/shard_map/ppermute | solution.py:40
  39.8 2.6 %collective-permute-done.4.refs_5_ = bf16[128,1024]{1,0:T(8,128)(2,1)S(1)} collective-permute-done((bf16[128,1024]{1,0:T(8,128)(2,1)}, bf16[128,1024]{1,0:T(8,128)(2,1)S(1)}, u32[]{:S(2)}, u32[]{:S(2)}) %collective-permute-start.4) | collective-permute-done | bytes 262176 | tf_op jit(solution)/shard_map/ppermute | solution.py:40
  43.2 1.4 collective-permute-start.30
  44.6 5.7 %collective-permute-done.5.refs_6_ = bf16[128,1024]{1,0:T(8,128)(2,1)S(1)} collective-permute-done((bf16[128,1024]{1,0:T(8,128)(2,1)}, bf16[128,1024]{1,0:T(8,128)(2,1)S(1)}, u32[]{:S(2)}, u32[]{:S(2)}) %collective-permute-start.5) | collective-permute-done | bytes 262176 | tf_op jit(solution)/shard_map/ppermute | solution.py:40
  51.8 2.0 %collective-permute-done.6.refs_7_ = bf16[128,1024]{1,0:T(8,128)(2,1)S(1)} collective-permute-done((bf16[128,1024]{1,0:T(8,128)(2,1)}, bf16[128,1024]{1,0:T(8,128)(2,1)S(1)}, u32[]{:S(2)}, u32[]{:S(2)}) %collective-permute-start.6) | collective-permute-done | bytes 262176 | tf_op jit(solution)/shard_map/ppermute | solution.py:40
  54.5 0.9 copy-done.45
  55.5 0.9 copy-done.48
  56.4 0.9 copy-done.51
  58.3 0.9 copy-done.57
  59.3 2.2 %value_terms.1 = (f32[4,128,512]{2,1,0:T(8,128)S(1)}, f32[4,128,512]{2,1,0:T(8,128)}) custom-call(bf16[128,1024]{1,0:T(8,128)(2,1)S(1)} %get-tuple-element.29.refs_0_, bf16[128,1024]{1,0:T(8,128)(2,1)S(1)} %collective-permute-done.refs_1_, bf16[128,1024]{1,0:T(8,128)(2,1)S(1)} %collective-permute-done.1.refs_2_, ...), custom_call_target="tpu_custom_call" | custom-call | flops 1073741824 | bytes 5242880 | tf_op jit(solution)/shard_map/value_terms/pallas_call | solution.py:159
  62.4 1.1 slice_bitcast_fusion.1
  68.2 0.9 copy-done.33
  69.1 0.9 copy-done.35
  70.2 3.5 %hidden_grad.1 = (bf16[128,1024]{1,0:T(8,128)(2,1)S(1)}, bf16[128,1024]{1,0:T(8,128)(2,1)S(1)}, bf16[128,1024]{1,0:T(8,128)(2,1)S(1)}, bf16[128,1024]{1,0:T(8,12...) custom-call(bf16[128,512]{1,0:T(8,128)(2,1)S(1)} %copy-done.21, ...), custom_call_target="tpu_custom_call" | custom-call | flops 1073741824 | bytes 4194304 | tf_op jit(solution)/shard_map/hidden_grad/pallas_call | solution.py:104
  73.8 3.2 %collective-permute-start.19 = (bf16[128,1024]{1,0:T(8,128)(2,1)S(1)}, bf16[128,1024]{1,0:T(8,128)(2,1)S(1)}, u32[]{:S(2)}, u32[]{:S(2)}) collective-permute-start(bf16[128,1024]{1,0:T(8,128)(2,1)S(1)} %get-tuple-element.42), channel_id=1, source_target_pairs={{0,6},{1,7},{2,0},{3,1},{4,2},{5,3},{6,4},{7,5},{8,14},{9,15},{10,... | collective-permute-start | bytes 786440 | tf_op jit(solution)/shard_map/ppermute | solution.py:40
  77.0 1.0 add_add_fusion
  78.3 11.9 %collective-permute-done.31 = f32[256,128]{1,0:T(8,128)S(1)} collective-permute-done((f32[256,128]{1,0:T(8,128)S(1)}, f32[256,128]{1,0:T(8,128)S(1)}, u32[]{:S(2)}, u32[]{:S(2)}) %collective-permute-start.31) | collective-permute-done | bytes 131104 | tf_op jit(solution)/shard_map/ppermute | solution.py:231
  91.5 1.4 collective-permute-start.22
  94.4 1.5 %collective-permute-start.24 = (bf16[128,1024]{1,0:T(8,128)(2,1)}, bf16[128,1024]{1,0:T(8,128)(2,1)}, u32[]{:S(2)}, u32[]{:S(2)}) collective-permute-start(bf16[128,1024]{1,0:T(8,128)(2,1)} %get-tuple-element.47), channel_id=1, source_target_pairs={{0,3},{1,2},{2,5},{3,4},{4,7},{5,6},{6,1},{7,0},{8,11},{9,10},{10,... | collective-permute-start | bytes 786440 | tf_op jit(solution)/shard_map/ppermute | solution.py:40
  96.0 2.0 %weight_terms.1 = (f32[256,512]{1,0:T(8,128)S(1)}, bf16[256,512]{1,0:T(8,128)(2,1)}, bf16[256,512]{1,0:T(8,128)(2,1)}, bf16[256,512]{1,0:T(8,128)(2,1)}) custom-call(bf16[128,1024]{1,0:T(8,128)(2,1)S(1)} %copy-done.37, bf16[128,1024]{1,0:T(8,128)(2,1)S(1)} %copy-done.39, bf16[128,1024]{1,0:T(8,128)(2,1)S(1)} %copy-done.41, bf16[128,1024]{1,0:T(8,128)(2,1)S(1)} %copy-done.43, ...), custom_call_target="tpu_custom_call" | custom-call | flops 1073741824 | bytes 4718592 | tf_op jit(solution)/shard_map/weight_terms/pallas_call | solution.py:134
  98.8 2.3 %collective-permute-done.21.refs_4_ = bf16[128,1024]{1,0:T(8,128)(2,1)S(1)} collective-permute-done((bf16[128,1024]{1,0:T(8,128)(2,1)S(1)}, bf16[128,1024]{1,0:T(8,128)(2,1)S(1)}, u32[]{:S(2)}, u32[]{:S(2)}) %collective-permute-start.21) | collective-permute-done | bytes 262176 | tf_op jit(solution)/shard_map/ppermute | solution.py:40
  101.8 1.2 collective-permute-done.22.refs_5_
  103.7 2.5 %collective-permute-start.26 = (bf16[256,512]{1,0:T(8,128)(2,1)}, bf16[256,512]{1,0:T(8,128)(2,1)}, u32[]{:S(2)}, u32[]{:S(2)}) collective-permute-start(bf16[256,512]{1,0:T(8,128)(2,1)} %get-tuple-element.50), channel_id=1, source_target_pairs={{0,16},{1,17},{2,18},{3,19},{4,20},{5,21},{6,22},{7,23},{8,24},{9,... | collective-permute-start | bytes 786440 | tf_op jit(solution)/shard_map/ppermute | solution.py:40
  106.2 4.1 %collective-permute-done.23.refs_6_ = bf16[128,1024]{1,0:T(8,128)(2,1)S(1)} collective-permute-done((bf16[128,1024]{1,0:T(8,128)(2,1)S(1)}, bf16[128,1024]{1,0:T(8,128)(2,1)S(1)}, u32[]{:S(2)}, u32[]{:S(2)}) %collective-permute-start.23) | collective-permute-done | bytes 262176 | tf_op jit(solution)/shard_map/ppermute | solution.py:40
  111.0 1.8 %multiply_subtract_fusion = (f32[256,128]{1,0:T(8,128)}, f32[256,128]{1,0:T(8,128)}) fusion(f32[256,128]{1,0:T(8,128)} %param.12, f32[256,128]{1,0:T(8,128)} %copy-done.60, f32[256,256]{1,0:T(8,128)} %copy-done.59, s32[]{:T(128)S(6)} %select_n.72, f32[256,128]{1,0:T(8,128)} %param.13), kind=kLoop, calls=%fused_computation.15 | loop fusion | flops 262144 | bytes 786436 | tf_op jit(solution)/shard_map/sub | solution.py:233
  112.8 3.2 %collective-permute-done.24.refs_7_ = bf16[128,1024]{1,0:T(8,128)(2,1)} collective-permute-done((bf16[128,1024]{1,0:T(8,128)(2,1)}, bf16[128,1024]{1,0:T(8,128)(2,1)}, u32[]{:S(2)}, u32[]{:S(2)}) %collective-permute-start.24) | collective-permute-done | bytes 262176 | tf_op jit(solution)/shard_map/ppermute | solution.py:40
  116.1 0.9 copy-done.5
  117.0 0.9 copy-done.7
  121.8 4.8 %input_grad.1 = f32[128,8192]{1,0:T(8,128)} custom-call(s32[3]{0:T(128)S(1)} %pad_add_fusion.place, bf16[128,8192]{1,0:T(8,128)(2,1)S(1)} %copy-done.1, f32[1,8192]{1,0:T(1,128)S(1)} %bitcast.31, f32[128,1]{1,0:T(8,128)S(1)} %get-tuple-element.39.scale_ref, bf16[128,1024]{1,0:T(8,128)(2,1)S(1)} %get-tuple-element.40.refs_0_, ...), custom_call_target="tpu_custom_call" | custom-call | flops 12582912 | bytes 8388608 | tf_op jit(solution)/shard_map/input_grad/pallas_call | solution.py:197
  126.6 2.1 %multiply_reduce_fusion = (f32[256]{0:T(256)S(1)}, f32[256,512]{1,0:T(8,128)}) fusion(bf16[256,512]{1,0:T(8,128)(2,1)S(1)} %copy-done.18, bf16[256,512]{1,0:T(8,128)(2,1)} %collective-permute-done.27, bf16[256,512]{1,0:T(8,128)(2,1)} %collective-permute-done.26, f32[256,512]{1,0:T(8,128)S(1)} %copy-done.3, bf16[256,512]{1,0:T(8,128)(2,1)} %collective-permute-done.25), kind=kLoop, calls=%fused_computation.1 | loop fusion | flops 1310464 | bytes 2098176 | tf_op jit(solution)/shard_map/reduce_sum | solution.py:273
  128.7 1.5 %fusion.3 = (bf16[4,128,512]{2,1,0:T(8,128)(2,1)S(1)}, f32[4,128,512]{2,1,0:T(8,128)S(1)}) fusion(f32[4,128,512]{2,1,0:T(8,128)S(1)} %get-tuple-element.37, f32[4,128,512]{2,1,0:T(8,128)} %collective-permute-done.10), kind=kLoop, calls=%fused_computation.24 | loop fusion | flops 524288 | bytes 3670016 | tf_op jit(solution)/shard_map/convert.2
  130.2 6.1 %collective-permute-start.11 = (bf16[128,512]{1,0:T(8,128)(2,1)S(1)}, bf16[128,512]{1,0:T(8,128)(2,1)S(1)}, u32[]{:S(2)}, u32[]{:S(2)}) collective-permute-start(bf16[128,512]{1,0:T(8,128)(2,1)S(1)} %get-tuple-element.65), channel_id=1, source_target_pairs={{0,6},{1,7},{2,0},{3,1},{4,2},{5,3},{6,4},{7,5},{8,14},{9,15},{10,... | collective-permute-start | bytes 393224 | tf_op jit(solution)/shard_map/ppermute | solution.py:40
  136.3 3.1 %collective-permute-start.12 = (bf16[128,512]{1,0:T(8,128)(2,1)S(1)}, bf16[128,512]{1,0:T(8,128)(2,1)S(1)}, u32[]{:S(2)}, u32[]{:S(2)}) collective-permute-start(bf16[128,512]{1,0:T(8,128)(2,1)S(1)} %get-tuple-element.67), channel_id=1, source_target_pairs={{0,4},{1,5},{2,6},{3,7},{4,0},{5,1},{6,2},{7,3},{8,12},{9,13},{10,... | collective-permute-start | bytes 393224 | tf_op jit(solution)/shard_map/ppermute | solution.py:40
  140.0 5.5 %collective-permute-done.13 = bf16[128,512]{1,0:T(8,128)(2,1)S(1)} collective-permute-done((bf16[128,512]{1,0:T(8,128)(2,1)S(1)}, bf16[128,512]{1,0:T(8,128)(2,1)S(1)}, u32[]{:S(2)}, u32[]{:S(2)}) %collective-permute-start.13) | collective-permute-done | bytes 131104 | tf_op jit(solution)/shard_map/ppermute | solution.py:40
  (155 shorter events, 25.1 us)
Async XLA Ops:
  0.6 15.5 %collective-permute-start.9 = (bf16[256,512]{1,0:T(8,128)(2,1)}, bf16[256,512]{1,0:T(8,128)(2,1)S(1)}, u32[]{:S(2)}, u32[]{:S(2)}) collective-permute-start(bf16[256,512]{1,0:T(8,128)(2,1)} %refs_8_.4), channel_id=1, source_target_pairs={{0,8},{1,9},{2,10},{3,11},{4,12},{5,13},{6,14},{7,15},{8,16},{9,17... | collective-permute-start | bytes 786440 | tf_op jit(solution)/shard_map/ppermute | solution.py:40
  1.7 22.7 %collective-permute-start.8 = (bf16[256,512]{1,0:T(8,128)(2,1)}, bf16[256,512]{1,0:T(8,128)(2,1)S(1)}, u32[]{:S(2)}, u32[]{:S(2)}) collective-permute-start(bf16[256,512]{1,0:T(8,128)(2,1)} %refs_8_.4), channel_id=1, source_target_pairs={{0,16},{1,17},{2,18},{3,19},{4,20},{5,21},{6,22},{7,23},{8,24},{9,... | collective-permute-start | bytes 786440 | tf_op jit(solution)/shard_map/ppermute | solution.py:40
  4.1 9.8 %collective-permute-start.16 = (bf16[128,512]{1,0:T(8,128)(2,1)}, bf16[128,512]{1,0:T(8,128)(2,1)S(1)}, u32[]{:S(2)}, u32[]{:S(2)}) collective-permute-start(bf16[128,512]{1,0:T(8,128)(2,1)} %refs_8_.5), channel_id=1, source_target_pairs={{0,6},{1,7},{2,0},{3,1},{4,2},{5,3},{6,4},{7,5},{8,14},{9,15},{10,... | collective-permute-start | bytes 393224 | tf_op jit(solution)/shard_map/ppermute | solution.py:40
  7.1 7.6 %collective-permute-start.15 = (bf16[128,512]{1,0:T(8,128)(2,1)}, bf16[128,512]{1,0:T(8,128)(2,1)S(1)}, u32[]{:S(2)}, u32[]{:S(2)}) collective-permute-start(bf16[128,512]{1,0:T(8,128)(2,1)} %refs_8_.5), channel_id=1, source_target_pairs={{0,4},{1,5},{2,6},{3,7},{4,0},{5,1},{6,2},{7,3},{8,12},{9,13},{10,... | collective-permute-start | bytes 393224 | tf_op jit(solution)/shard_map/ppermute | solution.py:40
  7.7 8.3 %collective-permute-start.14 = (bf16[128,512]{1,0:T(8,128)(2,1)}, bf16[128,512]{1,0:T(8,128)(2,1)S(1)}, u32[]{:S(2)}, u32[]{:S(2)}) collective-permute-start(bf16[128,512]{1,0:T(8,128)(2,1)} %refs_8_.5), channel_id=1, source_target_pairs={{0,2},{1,3},{2,4},{3,5},{4,6},{5,7},{6,0},{7,1},{8,10},{9,11},{10,... | collective-permute-start | bytes 393224 | tf_op jit(solution)/shard_map/ppermute | solution.py:40
  11.1 43.4 %copy-start.16 = (bf16[256,512]{1,0:T(8,128)(2,1)S(1)}, bf16[256,512]{1,0:T(8,128)(2,1)}, u32[]{:S(2)}) copy-start(bf16[256,512]{1,0:T(8,128)(2,1)} %refs_8_.4) | copy-start | bytes 786436
  13.9 49.6 %copy-start.36 = (bf16[128,1024]{1,0:T(8,128)(2,1)}, bf16[128,1024]{1,0:T(8,128)(2,1)S(1)}, u32[]{:S(2)}) copy-start(bf16[128,1024]{1,0:T(8,128)(2,1)S(1)} %get-tuple-element.29.refs_0_) | copy-start | bytes 786436
  13.9 49.6 %copy-start.23 = (bf16[128,512]{1,0:T(8,128)(2,1)}, bf16[128,512]{1,0:T(8,128)(2,1)S(1)}, u32[]{:S(2)}) copy-start(bf16[128,512]{1,0:T(8,128)(2,1)S(1)} %collective-permute-done.16.refs_6_.refs_14_) | copy-start | bytes 393220
  13.9 13.1 %collective-permute-start.7 = (bf16[256,512]{1,0:T(8,128)(2,1)}, bf16[256,512]{1,0:T(8,128)(2,1)S(1)}, u32[]{:S(2)}, u32[]{:S(2)}) collective-permute-start(bf16[256,512]{1,0:T(8,128)(2,1)} %refs_8_.4), channel_id=1, source_target_pairs={{0,24},{1,25},{2,26},{3,27},{4,28},{5,29},{6,30},{7,31},{8,0},{9,1... | collective-permute-start | bytes 786440 | tf_op jit(solution)/shard_map/ppermute | solution.py:40
  14.7 48.9 %copy-start.26 = (bf16[128,512]{1,0:T(8,128)(2,1)}, bf16[128,512]{1,0:T(8,128)(2,1)S(1)}, u32[]{:S(2)}) copy-start(bf16[128,512]{1,0:T(8,128)(2,1)S(1)} %collective-permute-done.15.refs_4_.refs_12_) | copy-start | bytes 393220
  14.7 16.3 %collective-permute-start = (bf16[128,1024]{1,0:T(8,128)(2,1)S(1)}, bf16[128,1024]{1,0:T(8,128)(2,1)S(1)}, u32[]{:S(2)}, u32[]{:S(2)}) collective-permute-start(bf16[128,1024]{1,0:T(8,128)(2,1)S(1)} %get-tuple-element.30), channel_id=1, source_target_pairs={{0,1},{1,0},{2,3},{3,2},{4,5},{5,4},{6,7},{7,6},{8,9},{9,8},{10,11... | collective-permute-start | bytes 786440 | tf_op jit(solution)/shard_map/ppermute | solution.py:40
  16.0 47.5 %copy-start.29 = (bf16[128,512]{1,0:T(8,128)(2,1)}, bf16[128,512]{1,0:T(8,128)(2,1)S(1)}, u32[]{:S(2)}) copy-start(bf16[128,512]{1,0:T(8,128)(2,1)S(1)} %collective-permute-done.14.refs_2_.refs_10_) | copy-start | bytes 393220
  16.0 14.9 %collective-permute-start.1 = (bf16[128,1024]{1,0:T(8,128)(2,1)S(1)}, bf16[128,1024]{1,0:T(8,128)(2,1)S(1)}, u32[]{:S(2)}, u32[]{:S(2)}) collective-permute-start(bf16[128,1024]{1,0:T(8,128)(2,1)S(1)} %get-tuple-element.31), channel_id=1, source_target_pairs={{0,2},{1,3},{2,4},{3,5},{4,6},{5,7},{6,0},{7,1},{8,10},{9,11},{10,... | collective-permute-start | bytes 786440 | tf_op jit(solution)/shard_map/ppermute | solution.py:40
  16.1 47.4 %copy-start.32 = (bf16[256,512]{1,0:T(8,128)(2,1)}, bf16[256,512]{1,0:T(8,128)(2,1)S(1)}, u32[]{:S(2)}) copy-start(bf16[256,512]{1,0:T(8,128)(2,1)S(1)} %collective-permute-done.9.refs_11_) | copy-start | bytes 786436
  16.1 17.4 %collective-permute-start.2 = (bf16[128,1024]{1,0:T(8,128)(2,1)S(1)}, bf16[128,1024]{1,0:T(8,128)(2,1)S(1)}, u32[]{:S(2)}, u32[]{:S(2)}) collective-permute-start(bf16[128,1024]{1,0:T(8,128)(2,1)S(1)} %get-tuple-element.32), channel_id=1, source_target_pairs={{0,3},{1,2},{2,5},{3,4},{4,7},{5,6},{6,1},{7,0},{8,11},{9,10},{10,... | collective-permute-start | bytes 786440 | tf_op jit(solution)/shard_map/ppermute | solution.py:40
  24.5 39.1 %copy-start.34 = (bf16[256,512]{1,0:T(8,128)(2,1)}, bf16[256,512]{1,0:T(8,128)(2,1)S(1)}, u32[]{:S(2)}) copy-start(bf16[256,512]{1,0:T(8,128)(2,1)S(1)} %collective-permute-done.8.refs_10_) | copy-start | bytes 786436
  24.5 37.9 %collective-permute-start.17 = (bf16[4,128,512]{2,1,0:T(8,128)(2,1)}, bf16[4,128,512]{2,1,0:T(8,128)(2,1)}, u32[]{:S(2)}, u32[]{:S(2)}) collective-permute-start(bf16[4,128,512]{2,1,0:T(8,128)(2,1)} %pad_maximum_fusion), channel_id=1, source_target_pairs={{0,1},{1,0},{2,3},{3,2},{4,5},{5,4},{6,7},{7,6},{8,9},{9,8},{10,11... | collective-permute-start | bytes 1572872 | tf_op jit(solution)/shard_map/ppermute | solution.py:40
  27.8 10.9 %collective-permute-start.3 = (bf16[128,1024]{1,0:T(8,128)(2,1)}, bf16[128,1024]{1,0:T(8,128)(2,1)S(1)}, u32[]{:S(2)}, u32[]{:S(2)}) collective-permute-start(bf16[128,1024]{1,0:T(8,128)(2,1)} %get-tuple-element.33), channel_id=1, source_target_pairs={{0,4},{1,5},{2,6},{3,7},{4,0},{5,1},{6,2},{7,3},{8,12},{9,13},{10,... | collective-permute-start | bytes 786440 | tf_op jit(solution)/shard_map/ppermute | solution.py:40
  31.0 32.6 %copy-start.38 = (bf16[128,1024]{1,0:T(8,128)(2,1)}, bf16[128,1024]{1,0:T(8,128)(2,1)S(1)}, u32[]{:S(2)}) copy-start(bf16[128,1024]{1,0:T(8,128)(2,1)S(1)} %collective-permute-done.refs_1_) | copy-start | bytes 786436
  31.0 11.5 %collective-permute-start.4 = (bf16[128,1024]{1,0:T(8,128)(2,1)}, bf16[128,1024]{1,0:T(8,128)(2,1)S(1)}, u32[]{:S(2)}, u32[]{:S(2)}) collective-permute-start(bf16[128,1024]{1,0:T(8,128)(2,1)} %get-tuple-element.34), channel_id=1, source_target_pairs={{0,5},{1,4},{2,7},{3,6},{4,1},{5,0},{6,3},{7,2},{8,13},{9,12},{10,... | collective-permute-start | bytes 786440 | tf_op jit(solution)/shard_map/ppermute | solution.py:40
  31.0 32.6 %copy-start.40 = (bf16[128,1024]{1,0:T(8,128)(2,1)}, bf16[128,1024]{1,0:T(8,128)(2,1)S(1)}, u32[]{:S(2)}) copy-start(bf16[128,1024]{1,0:T(8,128)(2,1)S(1)} %collective-permute-done.1.refs_2_) | copy-start | bytes 786436
  31.0 19.3 %collective-permute-start.5 = (bf16[128,1024]{1,0:T(8,128)(2,1)}, bf16[128,1024]{1,0:T(8,128)(2,1)S(1)}, u32[]{:S(2)}, u32[]{:S(2)}) collective-permute-start(bf16[128,1024]{1,0:T(8,128)(2,1)} %get-tuple-element.35), channel_id=1, source_target_pairs={{0,6},{1,7},{2,0},{3,1},{4,2},{5,3},{6,4},{7,5},{8,14},{9,15},{10,... | collective-permute-start | bytes 786440 | tf_op jit(solution)/shard_map/ppermute | solution.py:40
  33.5 20.3 %collective-permute-start.6 = (bf16[128,1024]{1,0:T(8,128)(2,1)}, bf16[128,1024]{1,0:T(8,128)(2,1)S(1)}, u32[]{:S(2)}, u32[]{:S(2)}) collective-permute-start(bf16[128,1024]{1,0:T(8,128)(2,1)} %get-tuple-element.36), channel_id=1, source_target_pairs={{0,7},{1,6},{2,1},{3,0},{4,3},{5,2},{6,5},{7,4},{8,15},{9,14},{10,... | collective-permute-start | bytes 786440 | tf_op jit(solution)/shard_map/ppermute | solution.py:40
  39.4 34.4 %collective-permute-start.28 = (f32[256,256]{1,0:T(8,128)S(1)}, f32[256,256]{1,0:T(8,128)S(1)}, u32[]{:S(2)}, u32[]{:S(2)}) collective-permute-start(f32[256,256]{1,0:T(8,128)S(1)} %get-tuple-element.58), channel_id=1, source_target_pairs={{0,64},{32,96},{64,128},{96,160},{128,192},{160,224},{192,0},{224,... | collective-permute-start | bytes 786440 | tf_op jit(solution)/shard_map/ppermute | solution.py:225
  43.2 33.9 %collective-permute-start.30 = (f32[256,256]{1,0:T(8,128)S(1)}, f32[256,256]{1,0:T(8,128)S(1)}, u32[]{:S(2)}, u32[]{:S(2)}) collective-permute-start(f32[256,256]{1,0:T(8,128)S(1)} %get-tuple-element.59), channel_id=1, source_target_pairs={{0,128},{32,160},{64,192},{96,224},{128,0},{160,32},{192,64},{224,... | collective-permute-start | bytes 786440 | tf_op jit(solution)/shard_map/ppermute | solution.py:225
  51.0 26.0 %collective-permute-start.29 = (f32[256,256]{1,0:T(8,128)S(1)}, f32[256,256]{1,0:T(8,128)S(1)}, u32[]{:S(2)}, u32[]{:S(2)}) collective-permute-start(f32[256,256]{1,0:T(8,128)S(1)} %get-tuple-element.60), channel_id=1, source_target_pairs={{0,192},{32,224},{64,0},{96,32},{128,64},{160,96},{192,128},{224,1... | collective-permute-start | bytes 786440 | tf_op jit(solution)/shard_map/ppermute | solution.py:225
  59.3 36.6 %copy-start.55 = (bf16[128,1024]{1,0:T(8,128)(2,1)S(1)}, bf16[128,1024]{1,0:T(8,128)(2,1)}, u32[]{:S(2)}) copy-start(bf16[128,1024]{1,0:T(8,128)(2,1)} %copy-done.53) | copy-start | bytes 786436
  61.5 34.4 %copy-start.22 = (bf16[128,512]{1,0:T(8,128)(2,1)S(1)}, bf16[128,512]{1,0:T(8,128)(2,1)}, u32[]{:S(2)}) copy-start(bf16[128,512]{1,0:T(8,128)(2,1)} %refs_8_.5) | copy-start | bytes 393220
  61.5 34.4 %copy-start.46 = (bf16[128,1024]{1,0:T(8,128)(2,1)S(1)}, bf16[128,1024]{1,0:T(8,128)(2,1)}, u32[]{:S(2)}) copy-start(bf16[128,1024]{1,0:T(8,128)(2,1)} %copy-done.44) | copy-start | bytes 786436
  61.5 34.4 %copy-start.49 = (bf16[128,1024]{1,0:T(8,128)(2,1)S(1)}, bf16[128,1024]{1,0:T(8,128)(2,1)}, u32[]{:S(2)}) copy-start(bf16[128,1024]{1,0:T(8,128)(2,1)} %copy-done.47) | copy-start | bytes 786436
  61.5 34.4 %copy-start.52 = (bf16[128,1024]{1,0:T(8,128)(2,1)S(1)}, bf16[128,1024]{1,0:T(8,128)(2,1)}, u32[]{:S(2)}) copy-start(bf16[128,1024]{1,0:T(8,128)(2,1)} %copy-done.50) | copy-start | bytes 786436
  61.5 67.2 %collective-permute-start.10 = (f32[4,128,512]{2,1,0:T(8,128)}, f32[4,128,512]{2,1,0:T(8,128)}, u32[]{:S(2)}, u32[]{:S(2)}) collective-permute-start(f32[4,128,512]{2,1,0:T(8,128)} %get-tuple-element.38), channel_id=1, source_target_pairs={{0,1},{1,0},{2,3},{3,2},{4,5},{5,4},{6,7},{7,6},{8,9},{9,8},{10,11... | collective-permute-start | bytes 3145736 | tf_op jit(solution)/shard_map/ppermute | solution.py:40
  70.1 45.9 %copy-start.1 = (bf16[128,8192]{1,0:T(8,128)(2,1)S(1)}, bf16[128,8192]{1,0:T(8,128)(2,1)}, u32[]{:S(2)}) copy-start(bf16[128,8192]{1,0:T(8,128)(2,1)} %x_ref.3) | copy-start | bytes 6291460
  70.1 45.9 %copy-start.20 = (f32[8192]{0:T(1024)S(1)}, f32[8192]{0:T(1024)}, u32[]{:S(2)}) copy-start(f32[8192]{0:T(1024)} %param.10) | copy-start | bytes 98308
  73.7 17.2 %collective-permute-start.18 = (bf16[128,1024]{1,0:T(8,128)(2,1)S(1)}, bf16[128,1024]{1,0:T(8,128)(2,1)S(1)}, u32[]{:S(2)}, u32[]{:S(2)}) collective-permute-start(bf16[128,1024]{1,0:T(8,128)(2,1)S(1)} %get-tuple-element.41), channel_id=1, source_target_pairs={{0,1},{1,0},{2,3},{3,2},{4,5},{5,4},{6,7},{7,6},{8,9},{9,8},{10,11... | collective-permute-start | bytes 786440 | tf_op jit(solution)/shard_map/ppermute | solution.py:40
  73.8 19.2 %collective-permute-start.19 = (bf16[128,1024]{1,0:T(8,128)(2,1)S(1)}, bf16[128,1024]{1,0:T(8,128)(2,1)S(1)}, u32[]{:S(2)}, u32[]{:S(2)}) collective-permute-start(bf16[128,1024]{1,0:T(8,128)(2,1)S(1)} %get-tuple-element.42), channel_id=1, source_target_pairs={{0,6},{1,7},{2,0},{3,1},{4,2},{5,3},{6,4},{7,5},{8,14},{9,15},{10,... | collective-permute-start | bytes 786440 | tf_op jit(solution)/shard_map/ppermute | solution.py:40
  78.1 12.1 %collective-permute-start.31 = (f32[256,128]{1,0:T(8,128)S(1)}, f32[256,128]{1,0:T(8,128)S(1)}, u32[]{:S(2)}, u32[]{:S(2)}) collective-permute-start(f32[256,128]{1,0:T(8,128)S(1)} %constant_dynamic-slice_fusion), channel_id=1, source_target_pairs={{0,32},{32,0},{64,96},{96,64},{128,160},{160,128},{192,224},{224,1... | collective-permute-start | bytes 393224 | tf_op jit(solution)/shard_map/ppermute | solution.py:231
  78.3 15.4 %collective-permute-start.20 = (bf16[128,1024]{1,0:T(8,128)(2,1)S(1)}, bf16[128,1024]{1,0:T(8,128)(2,1)S(1)}, u32[]{:S(2)}, u32[]{:S(2)}) collective-permute-start(bf16[128,1024]{1,0:T(8,128)(2,1)S(1)} %get-tuple-element.43), channel_id=1, source_target_pairs={{0,7},{1,6},{2,1},{3,0},{4,3},{5,2},{6,5},{7,4},{8,15},{9,14},{10,... | collective-permute-start | bytes 786440 | tf_op jit(solution)/shard_map/ppermute | solution.py:40
  90.2 10.8 %collective-permute-start.21 = (bf16[128,1024]{1,0:T(8,128)(2,1)S(1)}, bf16[128,1024]{1,0:T(8,128)(2,1)S(1)}, u32[]{:S(2)}, u32[]{:S(2)}) collective-permute-start(bf16[128,1024]{1,0:T(8,128)(2,1)S(1)} %get-tuple-element.44), channel_id=1, source_target_pairs={{0,4},{1,5},{2,6},{3,7},{4,0},{5,1},{6,2},{7,3},{8,12},{9,13},{10,... | collective-permute-start | bytes 786440 | tf_op jit(solution)/shard_map/ppermute | solution.py:40
  91.5 11.5 %collective-permute-start.22 = (bf16[128,1024]{1,0:T(8,128)(2,1)S(1)}, bf16[128,1024]{1,0:T(8,128)(2,1)S(1)}, u32[]{:S(2)}, u32[]{:S(2)}) collective-permute-start(bf16[128,1024]{1,0:T(8,128)(2,1)S(1)} %get-tuple-element.45), channel_id=1, source_target_pairs={{0,5},{1,4},{2,7},{3,6},{4,1},{5,0},{6,3},{7,2},{8,13},{9,12},{10,... | collective-permute-start | bytes 786440 | tf_op jit(solution)/shard_map/ppermute | solution.py:40
  93.7 16.6 %collective-permute-start.23 = (bf16[128,1024]{1,0:T(8,128)(2,1)S(1)}, bf16[128,1024]{1,0:T(8,128)(2,1)S(1)}, u32[]{:S(2)}, u32[]{:S(2)}) collective-permute-start(bf16[128,1024]{1,0:T(8,128)(2,1)S(1)} %get-tuple-element.46), channel_id=1, source_target_pairs={{0,2},{1,3},{2,4},{3,5},{4,6},{5,7},{6,0},{7,1},{8,10},{9,11},{10,... | collective-permute-start | bytes 786440 | tf_op jit(solution)/shard_map/ppermute | solution.py:40
  94.4 21.7 %collective-permute-start.24 = (bf16[128,1024]{1,0:T(8,128)(2,1)}, bf16[128,1024]{1,0:T(8,128)(2,1)}, u32[]{:S(2)}, u32[]{:S(2)}) collective-permute-start(bf16[128,1024]{1,0:T(8,128)(2,1)} %get-tuple-element.47), channel_id=1, source_target_pairs={{0,3},{1,2},{2,5},{3,4},{4,7},{5,6},{6,1},{7,0},{8,11},{9,10},{10,... | collective-permute-start | bytes 786440 | tf_op jit(solution)/shard_map/ppermute | solution.py:40
  101.8 24.8 %collective-permute-start.25 = (bf16[256,512]{1,0:T(8,128)(2,1)}, bf16[256,512]{1,0:T(8,128)(2,1)}, u32[]{:S(2)}, u32[]{:S(2)}) collective-permute-start(bf16[256,512]{1,0:T(8,128)(2,1)} %get-tuple-element.49), channel_id=1, source_target_pairs={{0,8},{1,9},{2,10},{3,11},{4,12},{5,13},{6,14},{7,15},{8,16},{9,17... | collective-permute-start | bytes 786440 | tf_op jit(solution)/shard_map/ppermute | solution.py:40
  103.7 22.9 %collective-permute-start.26 = (bf16[256,512]{1,0:T(8,128)(2,1)}, bf16[256,512]{1,0:T(8,128)(2,1)}, u32[]{:S(2)}, u32[]{:S(2)}) collective-permute-start(bf16[256,512]{1,0:T(8,128)(2,1)} %get-tuple-element.50), channel_id=1, source_target_pairs={{0,16},{1,17},{2,18},{3,19},{4,20},{5,21},{6,22},{7,23},{8,24},{9,... | collective-permute-start | bytes 786440 | tf_op jit(solution)/shard_map/ppermute | solution.py:40
  111.0 15.6 %collective-permute-start.27 = (bf16[256,512]{1,0:T(8,128)(2,1)}, bf16[256,512]{1,0:T(8,128)(2,1)}, u32[]{:S(2)}, u32[]{:S(2)}) collective-permute-start(bf16[256,512]{1,0:T(8,128)(2,1)} %get-tuple-element.51), channel_id=1, source_target_pairs={{0,24},{1,25},{2,26},{3,27},{4,28},{5,29},{6,30},{7,31},{8,0},{9,1... | collective-permute-start | bytes 786440 | tf_op jit(solution)/shard_map/ppermute | solution.py:40
  130.2 9.8 %collective-permute-start.11 = (bf16[128,512]{1,0:T(8,128)(2,1)S(1)}, bf16[128,512]{1,0:T(8,128)(2,1)S(1)}, u32[]{:S(2)}, u32[]{:S(2)}) collective-permute-start(bf16[128,512]{1,0:T(8,128)(2,1)S(1)} %get-tuple-element.65), channel_id=1, source_target_pairs={{0,6},{1,7},{2,0},{3,1},{4,2},{5,3},{6,4},{7,5},{8,14},{9,15},{10,... | collective-permute-start | bytes 393224 | tf_op jit(solution)/shard_map/ppermute | solution.py:40
  136.3 9.2 %collective-permute-start.13 = (bf16[128,512]{1,0:T(8,128)(2,1)S(1)}, bf16[128,512]{1,0:T(8,128)(2,1)S(1)}, u32[]{:S(2)}, u32[]{:S(2)}) collective-permute-start(bf16[128,512]{1,0:T(8,128)(2,1)S(1)} %get-tuple-element.66), channel_id=1, source_target_pairs={{0,2},{1,3},{2,4},{3,5},{4,6},{5,7},{6,0},{7,1},{8,10},{9,11},{10,... | collective-permute-start | bytes 393224 | tf_op jit(solution)/shard_map/ppermute | solution.py:40
  136.3 9.2 %collective-permute-start.12 = (bf16[128,512]{1,0:T(8,128)(2,1)S(1)}, bf16[128,512]{1,0:T(8,128)(2,1)S(1)}, u32[]{:S(2)}, u32[]{:S(2)}) collective-permute-start(bf16[128,512]{1,0:T(8,128)(2,1)S(1)} %get-tuple-element.67), channel_id=1, source_target_pairs={{0,4},{1,5},{2,6},{3,7},{4,0},{5,1},{6,2},{7,3},{8,12},{9,13},{10,... | collective-permute-start | bytes 393224 | tf_op jit(solution)/shard_map/ppermute | solution.py:40
  (45 other events, 309.7 us)

commit v2 on v0

v2 whole, which is shorter than its diff:
```python
import math

import jax
import jax.numpy as jnp
from jax import lax
from jax.experimental import pallas as pl
from jax.experimental.pallas import tpu as pltpu
from jax.sharding import PartitionSpec as P

F32 = jnp.float32
BF16 = jnp.bfloat16

NZ, NY, NC = 4, 4, 2
PLANE = NY * NC
HALVES = (0, 2, 1, 3)


def place():
    index = lax.axis_index("fsdp")
    return index // PLANE, (index // NC) % NY, index % NC


def swap(array, axis, bits):
    size = lax.axis_size(axis)
    return lax.ppermute(array, axis, [(source, source ^ bits) for source in range(size)])


def exchange_plane(array):
    planes = [[z * PLANE + m for m in range(PLANE)] for z in range(NZ)]
    return lax.all_to_all(array, "fsdp", 0, 0, axis_index_groups=planes)


def after(value, *others):
    return lax.optimization_barrier((value, *others))[0]


def cost(flops, bytes_accessed):
    return pl.CostEstimate(flops=flops, bytes_accessed=bytes_accessed, transcendentals=0)


def feature_start(member, dz, rows):
    return pl.multiple_of((member + (place()[0] ^ dz) * PLANE) * rows, rows)


def norm_kernel(x_ref, gain_ref, scale_ref, out_ref):
    floats = x_ref[...].astype(F32)
    mean = jnp.mean(floats * floats, axis=-1, keepdims=True)
    scale = lax.rsqrt(mean + 1e-05)
    scale_ref[...] = scale
    rows = x_ref.shape[1] // (NZ * PLANE)
    for dz in range(NZ):
        for member in range(PLANE):
            at = pl.ds(feature_start(member, dz, rows), rows)
            normed = x_ref[:, at].astype(F32) * scale
            out_ref[member, :, dz * rows : (dz + 1) * rows] = (normed * gain_ref[:, at]).astype(
                BF16
            )


def make_hidden(inputs, gain):
    tokens, width = inputs.shape
    step = 32
    block = width // PLANE
    return pl.pallas_call(
        norm_kernel,
        grid=(tokens // step,),
        in_specs=[
            pl.BlockSpec((step, width), lambda i: (i, 0)),
            pl.BlockSpec((1, width), lambda i: (0, 0)),
        ],
        out_specs=[
            pl.BlockSpec((step, 1), lambda i: (i, 0)),
            pl.BlockSpec((PLANE, step, block), lambda i: (0, i, 0)),
        ],
        out_shape=[
            jax.ShapeDtypeStruct((tokens, 1), F32),
            jax.ShapeDtypeStruct((PLANE, tokens, block), BF16),
        ],
        cost_estimate=cost(6 * tokens * width, 4 * tokens * width),
        name="norm",
    )(inputs, gain)


def fill_plane(cot_ref, same_ref, other_ref):
    _, y, c = place()
    tokens = cot_ref.shape[0] // PLANE
    for member in range(PLANE):
        dy = y ^ (member // NC)
        first = pl.multiple_of(((dy // 2) + (dy % 2) * 2) * tokens, tokens)
        at = pl.ds(first, tokens)
        cot_ref[member * tokens : (member + 1) * tokens] = jnp.where(
            member % NC == c, same_ref[at], other_ref[at]
        )


def hidden_grad_kernel(same_ref, other_ref, first_ref, second_ref, out_ref, cot_ref):
    step = pl.program_id(0)
    rows = out_ref.shape[2]

    @pl.when(step == 0)
    def _():
        fill_plane(cot_ref, same_ref, other_ref)

    for dz in range(NZ):
        ref, at = ((first_ref, dz // 2), (second_ref, dz // 2))[dz % 2]

        @pl.when(step == dz)
        def _():
            out_ref[...] = (
                lax.dot_general(
                    cot_ref[...],
                    ref[at * rows : (at + 1) * rows],
                    (((1,), (1,)), ((), ())),
                    preferred_element_type=F32,
                )
                .astype(BF16)
                .reshape(out_ref.shape)
            )


def make_hidden_grad(same, other, first, second):
    tokens, inner = same.shape[0] // NY, same.shape[1]
    rows = first.shape[0] // 2
    cots = pl.BlockSpec((NY * tokens, inner), lambda i: (0, 0))
    weight = pl.BlockSpec((2 * rows, inner), lambda i: (0, 0))
    return pl.pallas_call(
        hidden_grad_kernel,
        grid=(NZ,),
        in_specs=[cots, cots, weight, weight],
        out_specs=pl.BlockSpec((PLANE, tokens, rows), lambda i: (0, 0, i)),
        out_shape=jax.ShapeDtypeStruct((PLANE, tokens, NZ * rows), BF16),
        scratch_shapes=[pltpu.VMEM((PLANE * tokens, inner), BF16)],
        cost_estimate=cost(
            2 * PLANE * tokens * inner * NZ * rows,
            2 * PLANE * tokens * (inner + NZ * rows) + 2 * NZ * rows * inner,
        ),
        name="hidden_grad",
    )(same, other, first, second)


def terms_kernel(same_ref, other_ref, first_ref, second_ref, *refs):
    hiddens, (weight_keep, weight_give, keep, give, cot_ref, hidden_ref) = refs[:PLANE], refs[PLANE:]
    _, y, c = place()
    tokens = cot_ref.shape[0] // PLANE
    rows = weight_keep.shape[1]
    fill_plane(cot_ref, same_ref, other_ref)
    for member, hidden in enumerate(hiddens):
        hidden_ref[member * tokens : (member + 1) * tokens] = hidden[0]
    for dz in (1, 3, 0, 2):
        out = weight_give if dz % 2 else weight_keep
        out[dz // 2] = lax.dot_general(
            hidden_ref[:, dz * rows : (dz + 1) * rows],
            cot_ref[...],
            (((0,), (0,)), ((), ())),
            preferred_element_type=F32,
        ).astype(out.dtype)
    first, second = first_ref[...], second_ref[...]
    weight = jnp.concatenate([first[:rows], second[:rows], first[rows:], second[rows:]], axis=0)
    for at, dy in enumerate(HALVES):
        for dc, out in enumerate((keep, give)):
            start = pl.multiple_of(((y ^ dy) * NC + (c ^ dc)) * tokens, tokens)
            out[at] = jnp.dot(
                hidden_ref[pl.ds(start, tokens)], weight, preferred_element_type=F32
            )


def make_terms(same, other, first, second, hidden):
    _, tokens, block = hidden.shape
    inner, rows = first.shape[1], first.shape[0] // 2
    members = [
        pl.BlockSpec((1, tokens, block), lambda i, member=member: (member, 0, 0))
        for member in range(PLANE)
    ]
    cots = pl.BlockSpec((NY * tokens, inner), lambda i: (0, 0))
    weight = pl.BlockSpec((2 * rows, inner), lambda i: (0, 0))
    weight_out = pl.BlockSpec((2, rows, inner), lambda i: (0, 0, 0))
    value_out = pl.BlockSpec((NY, tokens, inner), lambda i: (0, 0, 0))
    return pl.pallas_call(
        terms_kernel,
        grid=(1,),
        in_specs=[cots, cots, weight, weight] + members,
        out_specs=[weight_out] * 2 + [value_out] * 2,
        out_shape=[
            jax.ShapeDtypeStruct((2, rows, inner), F32),
            jax.ShapeDtypeStruct((2, rows, inner), BF16),
            jax.ShapeDtypeStruct((NY, tokens, inner), F32),
            jax.ShapeDtypeStruct((NY, tokens, inner), F32),
        ],
        scratch_shapes=[
            pltpu.VMEM((PLANE * tokens, inner), BF16),
            pltpu.VMEM((PLANE * tokens, block), BF16),
        ],
        cost_estimate=cost(
            4 * PLANE * tokens * inner * block,
            2 * PLANE * tokens * (3 * inner + block) + 2 * block * inner,
        ),
        name="weight_and_value_terms",
    )(same, other, first, second, *[hidden] * PLANE)


def input_grad_kernel(x_ref, gain_ref, scale_ref, grad_ref, out_ref):
    width = x_ref.shape[1]
    rows = width // (NZ * PLANE)
    scale = scale_ref[...]
    total = jnp.zeros((x_ref.shape[0], rows), F32)
    for dz in range(NZ):
        for member in range(PLANE):
            at = pl.ds(feature_start(member, dz, rows), rows)
            grad = grad_ref[member, :, dz * rows : (dz + 1) * rows].astype(F32)
            total += (grad * gain_ref[:, at]) * (x_ref[:, at].astype(F32) * scale)
    mean = jnp.sum(total, axis=-1, keepdims=True) * (1.0 / width)
    for dz in range(NZ):
        for member in range(PLANE):
            at = pl.ds(feature_start(member, dz, rows), rows)
            grad = grad_ref[member, :, dz * rows : (dz + 1) * rows].astype(F32)
            normed = x_ref[:, at].astype(F32) * scale
            out_ref[:, at] = scale * (grad * gain_ref[:, at] - normed * mean)


def make_input_grad(inputs, gain, scale, grads):
    tokens, width = inputs.shape
    step = 32
    block = width // PLANE
    return pl.pallas_call(
        input_grad_kernel,
        grid=(tokens // step,),
        in_specs=[
            pl.BlockSpec((step, width), lambda i: (i, 0)),
            pl.BlockSpec((1, width), lambda i: (0, 0)),
            pl.BlockSpec((step, 1), lambda i: (i, 0)),
            pl.BlockSpec((PLANE, step, block), lambda i: (0, i, 0)),
        ],
        out_specs=pl.BlockSpec((step, width), lambda i: (i, 0)),
        out_shape=jax.ShapeDtypeStruct((tokens, width), F32),
        cost_estimate=cost(12 * tokens * width, 8 * tokens * width),
        name="input_grad",
    )(inputs, gain, scale, grads)


def halve_columns(total, bits):
    half = total.shape[1] // 2
    mine = lax.axis_index("rep") // bits % 2
    give = lax.dynamic_slice_in_dim(total, (1 - mine) * half, half, 1)
    keep = lax.dynamic_slice_in_dim(total, mine * half, half, 1)
    return keep + swap(give, "rep", bits)


def outer_step(total, params, moment):
    average = total / lax.axis_size("rep")
    new_moment = 0.9 * moment + average
    new_params = params - 0.7 * (average + 0.9 * new_moment)
    return new_params, new_moment


def gather_pairs(array, bits):
    array = jnp.concatenate([array, swap(array, "fsdp", 2 * bits)], axis=0)
    return array, swap(array, "fsdp", bits)


def shards(inputs, cotangent, value_weight, norm_gain, outer_delta, outer_params, outer_moment):
    index = lax.axis_index("fsdp")
    gain = norm_gain.reshape(1, -1)
    rows = value_weight.shape[0]

    same = jnp.concatenate(gather_pairs(cotangent, NC), axis=0)
    other = swap(same, "fsdp", 1)
    first, second = gather_pairs(value_weight, PLANE)
    delta = halve_columns(outer_delta, 4)

    scale, blocks = make_hidden(inputs, gain)
    hidden = exchange_plane(after(blocks, same, first))

    delta = halve_columns(halve_columns(delta, 2), 1)
    new_params, new_moment = outer_step(delta, outer_params, outer_moment)

    grads = make_hidden_grad(after(same, same), other, first, second)
    back = exchange_plane(grads)

    weight_keep, weight_give, keep, give = make_terms(
        same, after(other, grads), first, second, hidden
    )
    weight_sums = weight_keep + swap(weight_give, "fsdp", PLANE).astype(F32)
    weight_sum = weight_sums[0] + swap(weight_sums[1].astype(BF16), "fsdp", 2 * PLANE).astype(F32)
    scale_grad = 1.0 / math.sqrt(inputs.shape[0] * lax.axis_size("fsdp"))
    weight_grad = weight_sum * scale_grad
    own_gain = lax.dynamic_slice_in_dim(norm_gain, index * rows, rows, 0)
    gain_grad = jnp.sum(weight_grad * value_weight.astype(F32), axis=1) / own_gain

    pair = keep + swap(give, "fsdp", 1)
    pair = pair[:2] + swap(pair[2:].astype(BF16), "fsdp", NC).astype(F32)
    values = pair[0] + swap(pair[1].astype(BF16), "fsdp", 2 * NC).astype(F32)
    input_grad = make_input_grad(inputs, gain, scale, after(back, weight_sums, pair))
    return values, input_grad, weight_grad, gain_grad, new_params, new_moment


def solution(mesh):
    rows = P(("rep", "fsdp"), None)
    in_specs = (rows, rows, rows, P("rep"), rows, P("fsdp", "rep"), P("fsdp", "rep"))
    out_specs = (rows, rows, rows, P(("rep", "fsdp")), P("fsdp", "rep"), P("fsdp", "rep"))
    return jax.shard_map(shards, mesh=mesh, in_specs=in_specs, out_specs=out_specs, check_vma=False)
```

time: 340 us -> 107 us (0.31)
  blocking collectives: 134 us -> 0 us
  waiting for transfers between devices: 157 us -> 30.3 us
  starting transfers between devices: 0.12 us -> 33.5 us
  matrix products: 22.9 us -> 0 us
  Pallas kernels: 0 us -> 20.5 us
  between operations: 16.2 us -> 0.84 us
  local copies, waits for them, and re-layouts: 1.25 us -> 8.26 us
    psum x1 -> x0, waiting for transfers between devices: 141 us -> none  [shards(): total = lax.psum(outer_delta, 'rep')]
    unnamed x1 -> x0, blocking collectives: 134 us -> none
    ppermute x0 -> x13, waiting for transfers between devices: none -> 27.8 us  [swap(): lax.ppermute(array, axis, [(source, source ^ bits) for source in range(si...]
    ppermute x0 -> x13, starting transfers between devices: none -> 26.3 us  [swap(): lax.ppermute(array, axis, [(source, source ^ bits) for source in range(si...]
    dot_general x3 -> x0, matrix products: 22.9 us -> none  [the longest x1 8.93 us: shards(): lax.dot_general(hidden, cotangent, (((0,), (0,)), ((), ())), preferred_el...]
    pallas_call x0 -> x4, Pallas kernels: none -> 20.5 us  [the longest x1 5.76 us: make_input_grad(): pl.pallas_call(input_grad_kernel, grid=(tokens // step,), in_specs=[pl.Bl...]
    reduce_scatter x1 -> x0, waiting for transfers between devices: 14.3 us -> none  [shards(): lax.psum_scatter(weight_term, 'fsdp', scatter_dimension=0, tiled=True)]
    all_to_all x0 -> x2, starting transfers between devices: none -> 7.23 us  [exchange_plane(): return lax.all_to_all(array, 'fsdp', 0, 0, axis_index_groups=planes)]
  transfers between devices with their start and end apart: 3 -> 15, of which waited for: 2 -> 6; matrix products, arithmetic and copies ran while one was open for 9% -> 15% of each run, Pallas kernels for 0% -> 19%
where the time goes in v2:
time: 107 us; the launch traced here: 106 us
  starting transfers between devices  33.5 us (31%)
  waiting for transfers between devices  30.3 us (28%)
  Pallas kernels  20.5 us (19%)
  other arithmetic  12.3 us (11%)
  local copies, waits for them, and re-layouts  8.26 us (8%)
    ppermute x13, waiting for transfers between devices, swap(): lax.ppermute(array, axis, [(source, source ^ bits) for source in range(si...  27.8 us
    ppermute x13, starting transfers between devices, swap(): lax.ppermute(array, axis, [(source, source ^ bits) for source in range(si...  26.3 us
    all_to_all x2, starting transfers between devices, exchange_plane(): return lax.all_to_all(array, 'fsdp', 0, 0, axis_index_groups=planes)  7.23 us
    pallas_call x1, Pallas kernels, make_input_grad(): pl.pallas_call(input_grad_kernel, grid=(tokens // step,), in_specs=[pl.Bl...  5.76 us
    pallas_call x1, Pallas kernels, make_terms(): pl.pallas_call(terms_kernel, grid=(1,), in_specs=[cots, cots, weight, wei...  5.75 us
    unnamed x19, local copies, waits for them, and re-layouts  5.51 us
    pallas_call x1, Pallas kernels, make_hidden_grad(): pl.pallas_call(hidden_grad_kernel, grid=(NZ,), in_specs=[cots, cots, weig...  4.69 us
    pallas_call x1, Pallas kernels, make_hidden(): pl.pallas_call(norm_kernel, grid=(tokens // step,), in_specs=[pl.BlockSpe...  4.3 us
  transfers between devices with their start and end apart: 15, of which 6 were waited for; matrix products, arithmetic and copies ran while one was open for 15% of the time, Pallas kernels for 19%

profile of v2, /device:TPU:2, one launch (start us, length us, event | category | flops | bytes accessed | tf_op | source)
XLA Modules:
  0.0 105.7 jit_solution(16879468765893085327)
XLA Ops:
  0.6 3.3 %collective-permute-start = (bf16[128,512]{1,0:T(8,128)(2,1)}, bf16[128,512]{1,0:T(8,128)(2,1)S(1)}, u32[]{:S(2)}, u32[]{:S(2)}) collective-permute-start(bf16[128,512]{1,0:T(8,128)(2,1)} %param.8), channel_id=1, source_target_pairs={{0,4},{1,5},{2,6},{3,7},{4,0},{5,1},{6,2},{7,3},{8,12},{9,13},{10,... | collective-permute-start | bytes 393224 | tf_op jit(solution)/shard_map/ppermute | solution.py:25
  3.9 3.3 %collective-permute-start.3 = (bf16[256,512]{1,0:T(8,128)(2,1)}, bf16[256,512]{1,0:T(8,128)(2,1)S(1)}, u32[]{:S(2)}, u32[]{:S(2)}) collective-permute-start(bf16[256,512]{1,0:T(8,128)(2,1)} %param.9), channel_id=1, source_target_pairs={{0,16},{1,17},{2,18},{3,19},{4,20},{5,21},{6,22},{7,23},{8,24},{9,... | collective-permute-start | bytes 786440 | tf_op jit(solution)/shard_map/ppermute | solution.py:25
  7.2 1.0 constant_dynamic-update-slice_fusion.4
  8.2 0.0 collective-permute-done
  8.2 0.9 pad_maximum_fusion
  9.1 1.1 %collective-permute-start.1 = (bf16[256,512]{1,0:T(8,128)(2,1)S(1)}, bf16[256,512]{1,0:T(8,128)(2,1)S(1)}, u32[]{:S(2)}, u32[]{:S(2)}) collective-permute-start(bf16[256,512]{1,0:T(8,128)(2,1)S(1)} %pad_maximum_fusion), channel_id=1, source_target_pairs={{0,2},{1,3},{2,0},{3,1},{4,6},{5,7},{6,4},{7,5},{8,10},{9,11},{10,... | collective-permute-start | bytes 786440 | tf_op jit(solution)/shard_map/ppermute | solution.py:25
  10.3 0.9 constant_dynamic-update-slice_fusion.2
  11.2 4.3 %norm.1 = (f32[128,1]{1,0:T(8,128)}, bf16[8,128,1024]{2,1,0:T(8,128)(2,1)}) custom-call(bf16[128,8192]{1,0:T(8,128)(2,1)} %x_ref.3, f32[1,8192]{1,0:T(1,128)} %bitcast.16), custom_call_target="tpu_custom_call" | custom-call | flops 6291456 | bytes 4194304 | tf_op jit(solution)/shard_map/norm/pallas_call | solution.py:64
  15.5 3.5 %collective-permute-done.3 = bf16[256,512]{1,0:T(8,128)(2,1)S(1)} collective-permute-done((bf16[256,512]{1,0:T(8,128)(2,1)}, bf16[256,512]{1,0:T(8,128)(2,1)S(1)}, u32[]{:S(2)}, u32[]{:S(2)}) %collective-permute-start.3) | collective-permute-done | bytes 262176 | tf_op jit(solution)/shard_map/ppermute | solution.py:25
  19.1 0.0 copy-start.3
  19.1 3.6 %all-to-all-start = ((bf16[8,128,1024]{2,1,0:T(8,128)(2,1)}), bf16[8,128,1024]{2,1,0:T(8,128)(2,1)S(1)}, u32[]{:S(2)}, u32[]{:S(2)}) async-start(bf16[8,128,1024]{2,1,0:T(8,128)(2,1)} %get-tuple-element.19), calls=%async_computation | async-start | bytes 4194304 | tf_op jit(solution)/shard_map/all_to_all | solution.py:30
  22.8 1.9 %constant_dynamic-slice_fusion.2 = f32[256,512]{1,0:T(8,128)} fusion(f32[256,1024]{1,0:T(8,128)} %param.11, s32[]{:T(128)S(6)} %select_n.48), kind=kLoop, calls=%fused_computation.26 | loop fusion | bytes 1048580 | tf_op jit(solution)/shard_map/dynamic_slice | solution.py:243
  24.7 2.1 %collective-permute-start.10 = (f32[256,512]{1,0:T(8,128)}, f32[256,512]{1,0:T(8,128)}, u32[]{:S(2)}, u32[]{:S(2)}) collective-permute-start(f32[256,512]{1,0:T(8,128)} %constant_dynamic-slice_fusion.2), channel_id=1, source_target_pairs={{0,128},{32,160},{64,192},{96,224},{128,0},{160,32},{192,64},{224,... | collective-permute-start | bytes 1572872 | tf_op jit(solution)/shard_map/ppermute | solution.py:25
  26.8 0.8 collective-permute-start.4
  27.6 13.0 %collective-permute-done.10 = f32[256,512]{1,0:T(8,128)} collective-permute-done((f32[256,512]{1,0:T(8,128)}, f32[256,512]{1,0:T(8,128)}, u32[]{:S(2)}, u32[]{:S(2)}) %collective-permute-start.10) | collective-permute-done | bytes 524320 | tf_op jit(solution)/shard_map/ppermute | solution.py:25
  40.7 1.3 %dynamic-slice_add_fusion = f32[256,512]{1,0:T(8,128)S(1)} fusion(f32[256,512]{1,0:T(8,128)} %collective-permute-done.10, f32[256,1024]{1,0:T(8,128)} %param.11, s32[]{:T(128)S(6)} %select_n.47), kind=kLoop, calls=%fused_computation.7 | loop fusion | flops 131072 | bytes 1572868 | tf_op jit(solution)/shard_map/add | solution.py:245
  42.0 0.6 collective-permute-start.11
  42.6 0.0 collective-permute-done.4.second_ref
  42.6 0.1 copy-done.4
  42.8 0.0 collective-permute-done.2.other_ref
  42.8 4.7 %hidden_grad.1 = bf16[8,128,1024]{2,1,0:T(8,128)(2,1)} custom-call(bf16[512,512]{1,0:T(8,128)(2,1)} %copy-done.3, bf16[512,512]{1,0:T(8,128)(2,1)} %collective-permute-done.2.other_ref, bf16[512,512]{1,0:T(8,128)(2,1)} %copy-done.2, bf16[512,512]{1,0:T(8,128)(2,1)} %collective-permute-done.4.second_ref), custom_call_target="tpu_custom_call" | custom-call | flops 1073741824 | bytes 4194304 | tf_op jit(solution)/shard_map/hidden_grad/pallas_call | solution.py:126
  47.4 2.4 %all-to-all-done.refs_0_.refs_1_.refs_2_.refs_3_.refs_4_.refs_5_.refs_6_.refs_7_ = bf16[8,128,1024]{2,1,0:T(8,128)(2,1)S(1)} async-done(((bf16[8,128,1024]{2,1,0:T(8,128)(2,1)}), bf16[8,128,1024]{2,1,0:T(8,128)(2,1)S(1)}, u32[]{:S(2)}, u32[]{:S(2)}) %all-to-all-start) | async-done | bytes 2097184 | tf_op jit(solution)/shard_map/all_to_all | solution.py:30
  49.9 1.3 %copy-done = bf16[8,128,1024]{2,1,0:T(8,128)(2,1)} copy-done((bf16[8,128,1024]{2,1,0:T(8,128)(2,1)}, bf16[8,128,1024]{2,1,0:T(8,128)(2,1)S(1)}, u32[]{:S(2)}) %copy-start) | copy-done | bytes 2097176
  51.2 5.8 %weight_and_value_terms.1 = (f32[2,256,512]{2,1,0:T(8,128)}, bf16[2,256,512]{2,1,0:T(8,128)(2,1)}, f32[4,128,512]{2,1,0:T(8,128)}, f32[4,128,512]{2,1,0:T(8,128)}) custom-call(bf16[512,512]{1,0:T(8,128)(2,1)} %copy-done.3, bf16[512,512]{1,0:T(8,128)(2,1)} %collective-permute-done.2.other_ref, bf16[512,512]{1,0:T(8,128)(2,1)} %copy-done.2, ...), custom_call_target="tpu_custom_call" | custom-call | flops 2147483648 | bytes 6291456 | tf_op jit(solution)/shard_map/weight_and_value_terms/pallas_call | solution.py:178
  56.9 0.8 collective-permute-start.8
  57.8 0.0 collective-permute-done.11
  57.8 1.0 dynamic-slice_add_fusion.1
  58.8 3.6 %all-to-all-start.1 = ((bf16[8,128,1024]{2,1,0:T(8,128)(2,1)}), bf16[8,128,1024]{2,1,0:T(8,128)(2,1)S(1)}, u32[]{:S(2)}, u32[]{:S(2)}) async-start(bf16[8,128,1024]{2,1,0:T(8,128)(2,1)} %hidden_grad.1), calls=%async_computation.1 | async-start | bytes 4194304 | tf_op jit(solution)/shard_map/all_to_all | solution.py:30
  62.4 5.9 %collective-permute-start.12 = (f32[256,128]{1,0:T(8,128)S(1)}, f32[256,128]{1,0:T(8,128)}, u32[]{:S(2)}, u32[]{:S(2)}) collective-permute-start(f32[256,128]{1,0:T(8,128)S(1)} %constant_dynamic-slice_fusion), channel_id=1, source_target_pairs={{0,32},{32,0},{64,96},{96,64},{128,160},{160,128},{192,224},{224,1... | collective-permute-start | bytes 393224 | tf_op jit(solution)/shard_map/ppermute | solution.py:25
  68.4 2.2 %collective-permute-done.8 = bf16[2,256,512]{2,1,0:T(8,128)(2,1)S(1)} collective-permute-done((bf16[2,256,512]{2,1,0:T(8,128)(2,1)}, bf16[2,256,512]{2,1,0:T(8,128)(2,1)S(1)}, u32[]{:S(2)}, u32[]{:S(2)}) %collective-permute-start.8) | collective-permute-done | bytes 524320 | tf_op jit(solution)/shard_map/ppermute | solution.py:25
  70.6 0.8 copy-done.7
  71.4 1.5 %convert_add_fusion = f32[2,256,512]{2,1,0:T(8,128)S(1)} fusion(f32[2,256,512]{2,1,0:T(8,128)} %get-tuple-element.23, bf16[2,256,512]{2,1,0:T(8,128)(2,1)} %copy-done.7), kind=kLoop, calls=%fused_computation | loop fusion | flops 524288 | bytes 2621440 | tf_op jit(solution)/shard_map/add | solution.py:282
  72.9 0.7 fusion.2
  73.7 5.4 %collective-permute-start.9 = (bf16[256,512]{1,0:T(8,128)(2,1)}, bf16[256,512]{1,0:T(8,128)(2,1)}, u32[]{:S(2)}, u32[]{:S(2)}) collective-permute-start(bf16[256,512]{1,0:T(8,128)(2,1)} %fusion.2), channel_id=1, source_target_pairs={{0,16},{1,17},{2,18},{3,19},{4,20},{5,21},{6,22},{7,23},{8,24},{9,... | collective-permute-start | bytes 786440 | tf_op jit(solution)/shard_map/ppermute | solution.py:25
  79.1 0.0 collective-permute-done.12
  79.1 1.8 %multiply_subtract_fusion = (f32[256,128]{1,0:T(8,128)}, f32[256,128]{1,0:T(8,128)}) fusion(f32[256,128]{1,0:T(8,128)} %param.12, f32[256,128]{1,0:T(8,128)} %collective-permute-done.12, f32[256,256]{1,0:T(8,128)S(1)} %dynamic-slice_add_fusion.1, s32[]{:T(128)S(6)} %select_n.54, f32[256,128]{1,0:T(8,128)} %param.13), kind=kLoop, calls=%fused_computation.16 | loop fusion | flops 262144 | bytes 786436 | tf_op jit(solution)/shard_map/sub | solution.py:251
  80.9 0.0 collective-permute-done.5
  80.9 1.7 %add.64 = f32[4,128,512]{2,1,0:T(8,128)S(1)} add(f32[4,128,512]{2,1,0:T(8,128)} %get-tuple-element.20, f32[4,128,512]{2,1,0:T(8,128)} %collective-permute-done.5) | non-fusion elementwise | flops 262144 | bytes 3145728 | tf_op jit(solution)/shard_map/add | solution.py:289
  82.7 0.1 collective-permute-start.6
  82.8 7.2 %collective-permute-done.9 = bf16[256,512]{1,0:T(8,128)(2,1)} collective-permute-done((bf16[256,512]{1,0:T(8,128)(2,1)}, bf16[256,512]{1,0:T(8,128)(2,1)}, u32[]{:S(2)}, u32[]{:S(2)}) %collective-permute-start.9) | collective-permute-done | bytes 262176 | tf_op jit(solution)/shard_map/ppermute | solution.py:25
  89.9 1.8 %multiply_reduce_fusion = (f32[256]{0:T(256)S(1)}, f32[256,512]{1,0:T(8,128)}) fusion(bf16[256,512]{1,0:T(8,128)(2,1)S(1)} %copy-done.6, bf16[256,512]{1,0:T(8,128)(2,1)} %collective-permute-done.9, f32[2,256,512]{2,1,0:T(8,128)S(1)} %convert_add_fusion), kind=kLoop, calls=%fused_computation.8 | loop fusion | flops 786176 | bytes 1573888 | tf_op jit(solution)/shard_map/reduce_sum | solution.py:287
  91.8 1.8 %collective-permute-done.6 = bf16[2,128,512]{2,1,0:T(8,128)(2,1)S(1)} collective-permute-done((bf16[2,128,512]{2,1,0:T(8,128)(2,1)S(1)}, bf16[2,128,512]{2,1,0:T(8,128)(2,1)S(1)}, u32[]{:S(2)}, u32[]{:S(2)}) %collective-permute-start.6) | collective-permute-done | bytes 262176 | tf_op jit(solution)/shard_map/ppermute | solution.py:25
  93.6 0.1 slice_add_fusion
  93.7 2.8 %collective-permute-start.7 = (bf16[128,512]{1,0:T(8,128)(2,1)S(1)}, bf16[128,512]{1,0:T(8,128)(2,1)S(1)}, u32[]{:S(2)}, u32[]{:S(2)}) collective-permute-start(bf16[128,512]{1,0:T(8,128)(2,1)S(1)} %fusion.4), channel_id=1, source_target_pairs={{0,4},{1,5},{2,6},{3,7},{4,0},{5,1},{6,2},{7,3},{8,12},{9,13},{10,... | collective-permute-start | bytes 393224 | tf_op jit(solution)/shard_map/ppermute | solution.py:25
  96.5 1.3 %dynamic-slice_divide_fusion = f32[256]{0:T(256)} fusion(f32[256]{0:T(256)S(1)} %get-tuple-element.28, f32[8192]{0:T(1024)} %param.10, s32[]{:T(128)S(6)} %select_n.44), kind=kLoop, calls=%fused_computation.27 | loop fusion | flops 256 | bytes 3076 | tf_op jit(solution)/shard_map/div | solution.py:287
  97.9 1.3 %copy-done.1 = bf16[8,128,1024]{2,1,0:T(8,128)(2,1)} copy-done((bf16[8,128,1024]{2,1,0:T(8,128)(2,1)}, bf16[8,128,1024]{2,1,0:T(8,128)(2,1)S(1)}, u32[]{:S(2)}) %copy-start.1) | copy-done | bytes 2097176
  99.2 5.8 %input_grad.1 = f32[128,8192]{1,0:T(8,128)} custom-call(bf16[128,8192]{1,0:T(8,128)(2,1)} %x_ref.3, f32[1,8192]{1,0:T(1,128)} %bitcast.17, f32[128,1]{1,0:T(8,128)} %get-tuple-element.22.scale_ref, bf16[8,128,1024]{2,1,0:T(8,128)(2,1)} %copy-done.1), custom_call_target="tpu_custom_call" | custom-call | flops 12582912 | bytes 8388608 | tf_op jit(solution)/shard_map/input_grad/pallas_call | solution.py:224
  104.9 0.7 fusion.3
  (23 shorter events, 0.2 us)
Async XLA Ops:
  0.6 7.6 %collective-permute-start = (bf16[128,512]{1,0:T(8,128)(2,1)}, bf16[128,512]{1,0:T(8,128)(2,1)S(1)}, u32[]{:S(2)}, u32[]{:S(2)}) collective-permute-start(bf16[128,512]{1,0:T(8,128)(2,1)} %param.8), channel_id=1, source_target_pairs={{0,4},{1,5},{2,6},{3,7},{4,0},{5,1},{6,2},{7,3},{8,12},{9,13},{10,... | collective-permute-start | bytes 393224 | tf_op jit(solution)/shard_map/ppermute | solution.py:25
  3.9 15.1 %collective-permute-start.3 = (bf16[256,512]{1,0:T(8,128)(2,1)}, bf16[256,512]{1,0:T(8,128)(2,1)S(1)}, u32[]{:S(2)}, u32[]{:S(2)}) collective-permute-start(bf16[256,512]{1,0:T(8,128)(2,1)} %param.9), channel_id=1, source_target_pairs={{0,16},{1,17},{2,18},{3,19},{4,20},{5,21},{6,22},{7,23},{8,24},{9,... | collective-permute-start | bytes 786440 | tf_op jit(solution)/shard_map/ppermute | solution.py:25
  9.1 9.9 %collective-permute-start.1 = (bf16[256,512]{1,0:T(8,128)(2,1)S(1)}, bf16[256,512]{1,0:T(8,128)(2,1)S(1)}, u32[]{:S(2)}, u32[]{:S(2)}) collective-permute-start(bf16[256,512]{1,0:T(8,128)(2,1)S(1)} %pad_maximum_fusion), channel_id=1, source_target_pairs={{0,2},{1,3},{2,0},{3,1},{4,6},{5,7},{6,4},{7,5},{8,10},{9,11},{10,... | collective-permute-start | bytes 786440 | tf_op jit(solution)/shard_map/ppermute | solution.py:25
  19.1 7.7 %copy-start.2 = (bf16[512,512]{1,0:T(8,128)(2,1)}, bf16[512,512]{1,0:T(8,128)(2,1)S(1)}, u32[]{:S(2)}) copy-start(bf16[512,512]{1,0:T(8,128)(2,1)S(1)} %constant_dynamic-update-slice_fusion.3.first_ref) | copy-start | bytes 1572868
  19.1 8.5 %copy-start.3 = (bf16[512,512]{1,0:T(8,128)(2,1)}, bf16[512,512]{1,0:T(8,128)(2,1)S(1)}, u32[]{:S(2)}) copy-start(bf16[512,512]{1,0:T(8,128)(2,1)S(1)} %constant_dynamic-update-slice_fusion.same_ref) | copy-start | bytes 1572868
  19.1 30.7 %all-to-all-start = ((bf16[8,128,1024]{2,1,0:T(8,128)(2,1)}), bf16[8,128,1024]{2,1,0:T(8,128)(2,1)S(1)}, u32[]{:S(2)}, u32[]{:S(2)}) async-start(bf16[8,128,1024]{2,1,0:T(8,128)(2,1)} %get-tuple-element.19), calls=%async_computation | async-start | bytes 4194304 | tf_op jit(solution)/shard_map/all_to_all | solution.py:30
  24.7 16.0 %collective-permute-start.10 = (f32[256,512]{1,0:T(8,128)}, f32[256,512]{1,0:T(8,128)}, u32[]{:S(2)}, u32[]{:S(2)}) collective-permute-start(f32[256,512]{1,0:T(8,128)} %constant_dynamic-slice_fusion.2), channel_id=1, source_target_pairs={{0,128},{32,160},{64,192},{96,224},{128,0},{160,32},{192,64},{224,... | collective-permute-start | bytes 1572872 | tf_op jit(solution)/shard_map/ppermute | solution.py:25
  26.8 15.8 %collective-permute-start.4 = (bf16[512,512]{1,0:T(8,128)(2,1)S(1)}, bf16[512,512]{1,0:T(8,128)(2,1)}, u32[]{:S(2)}, u32[]{:S(2)}) collective-permute-start(bf16[512,512]{1,0:T(8,128)(2,1)S(1)} %constant_dynamic-update-slice_fusion.3.first_ref), channel_id=1, source_target_pairs={{0,8},{1,9},{2,10},{3,11},{4,12},{5,13},{6,14},{7,15},{8,0},{9,1},... | collective-permute-start | bytes 1572872 | tf_op jit(solution)/shard_map/ppermute | solution.py:25
  27.6 15.1 %collective-permute-start.2 = (bf16[512,512]{1,0:T(8,128)(2,1)S(1)}, bf16[512,512]{1,0:T(8,128)(2,1)}, u32[]{:S(2)}, u32[]{:S(2)}) collective-permute-start(bf16[512,512]{1,0:T(8,128)(2,1)S(1)} %constant_dynamic-update-slice_fusion.same_ref), channel_id=1, source_target_pairs={{0,1},{1,0},{2,3},{3,2},{4,5},{5,4},{6,7},{7,6},{8,9},{9,8},{10,11... | collective-permute-start | bytes 1572872 | tf_op jit(solution)/shard_map/ppermute | solution.py:25
  42.0 0.8 copy-start.4
  42.0 15.8 %collective-permute-start.11 = (f32[256,256]{1,0:T(8,128)S(1)}, f32[256,256]{1,0:T(8,128)}, u32[]{:S(2)}, u32[]{:S(2)}) collective-permute-start(f32[256,256]{1,0:T(8,128)S(1)} %constant_dynamic-slice_fusion.1), channel_id=1, source_target_pairs={{0,64},{32,96},{64,0},{96,32},{128,192},{160,224},{192,128},{224,1... | collective-permute-start | bytes 786440 | tf_op jit(solution)/shard_map/ppermute | solution.py:25
  47.4 10.3 %copy-start.5 = (f32[256,512]{1,0:T(8,128)S(1)}, f32[256,512]{1,0:T(8,128)}, u32[]{:S(2)}) copy-start(f32[256,512]{1,0:T(8,128)} %copy-done.4) | copy-start | bytes 1572868
  49.9 1.3 %copy-start = (bf16[8,128,1024]{2,1,0:T(8,128)(2,1)}, bf16[8,128,1024]{2,1,0:T(8,128)(2,1)S(1)}, u32[]{:S(2)}) copy-start(bf16[8,128,1024]{2,1,0:T(8,128)(2,1)S(1)} %all-to-all-done.refs_0_.refs_1_.refs_2_.refs_3_.refs_4_.refs_5_.refs_6_.refs_7_) | copy-start | bytes 6291460
  56.9 13.7 %collective-permute-start.8 = (bf16[2,256,512]{2,1,0:T(8,128)(2,1)}, bf16[2,256,512]{2,1,0:T(8,128)(2,1)S(1)}, u32[]{:S(2)}, u32[]{:S(2)}) collective-permute-start(bf16[2,256,512]{2,1,0:T(8,128)(2,1)} %get-tuple-element.24), channel_id=1, source_target_pairs={{0,8},{1,9},{2,10},{3,11},{4,12},{5,13},{6,14},{7,15},{8,0},{9,1},... | collective-permute-start | bytes 1572872 | tf_op jit(solution)/shard_map/ppermute | solution.py:25
  57.8 23.1 %collective-permute-start.5 = (f32[4,128,512]{2,1,0:T(8,128)}, f32[4,128,512]{2,1,0:T(8,128)}, u32[]{:S(2)}, u32[]{:S(2)}) collective-permute-start(f32[4,128,512]{2,1,0:T(8,128)} %get-tuple-element.21), channel_id=1, source_target_pairs={{0,1},{1,0},{2,3},{3,2},{4,5},{5,4},{6,7},{7,6},{8,9},{9,8},{10,11... | collective-permute-start | bytes 3145736 | tf_op jit(solution)/shard_map/ppermute | solution.py:25
  58.8 39.1 %all-to-all-start.1 = ((bf16[8,128,1024]{2,1,0:T(8,128)(2,1)}), bf16[8,128,1024]{2,1,0:T(8,128)(2,1)S(1)}, u32[]{:S(2)}, u32[]{:S(2)}) async-start(bf16[8,128,1024]{2,1,0:T(8,128)(2,1)} %hidden_grad.1), calls=%async_computation.1 | async-start | bytes 4194304 | tf_op jit(solution)/shard_map/all_to_all | solution.py:30
  62.4 16.7 %collective-permute-start.12 = (f32[256,128]{1,0:T(8,128)S(1)}, f32[256,128]{1,0:T(8,128)}, u32[]{:S(2)}, u32[]{:S(2)}) collective-permute-start(f32[256,128]{1,0:T(8,128)S(1)} %constant_dynamic-slice_fusion), channel_id=1, source_target_pairs={{0,32},{32,0},{64,96},{96,64},{128,160},{160,128},{192,224},{224,1... | collective-permute-start | bytes 393224 | tf_op jit(solution)/shard_map/ppermute | solution.py:25
  70.6 0.8 copy-start.7
  73.7 16.3 %collective-permute-start.9 = (bf16[256,512]{1,0:T(8,128)(2,1)}, bf16[256,512]{1,0:T(8,128)(2,1)}, u32[]{:S(2)}, u32[]{:S(2)}) collective-permute-start(bf16[256,512]{1,0:T(8,128)(2,1)} %fusion.2), channel_id=1, source_target_pairs={{0,16},{1,17},{2,18},{3,19},{4,20},{5,21},{6,22},{7,23},{8,24},{9,... | collective-permute-start | bytes 786440 | tf_op jit(solution)/shard_map/ppermute | solution.py:25
  79.1 10.9 %copy-start.6 = (bf16[256,512]{1,0:T(8,128)(2,1)S(1)}, bf16[256,512]{1,0:T(8,128)(2,1)}, u32[]{:S(2)}) copy-start(bf16[256,512]{1,0:T(8,128)(2,1)} %param.9) | copy-start | bytes 786436
  82.7 10.9 %collective-permute-start.6 = (bf16[2,128,512]{2,1,0:T(8,128)(2,1)S(1)}, bf16[2,128,512]{2,1,0:T(8,128)(2,1)S(1)}, u32[]{:S(2)}, u32[]{:S(2)}) collective-permute-start(bf16[2,128,512]{2,1,0:T(8,128)(2,1)S(1)} %slice.49), channel_id=1, source_target_pairs={{0,2},{1,3},{2,0},{3,1},{4,6},{5,7},{6,4},{7,5},{8,10},{9,11},{10,... | collective-permute-start | bytes 786440 | tf_op jit(solution)/shard_map/ppermute | solution.py:25
  93.7 11.2 %collective-permute-start.7 = (bf16[128,512]{1,0:T(8,128)(2,1)S(1)}, bf16[128,512]{1,0:T(8,128)(2,1)S(1)}, u32[]{:S(2)}, u32[]{:S(2)}) collective-permute-start(bf16[128,512]{1,0:T(8,128)(2,1)S(1)} %fusion.4), channel_id=1, source_target_pairs={{0,4},{1,5},{2,6},{3,7},{4,0},{5,1},{6,2},{7,3},{8,12},{9,13},{10,... | collective-permute-start | bytes 393224 | tf_op jit(solution)/shard_map/ppermute | solution.py:25
  97.8 1.3 %copy-start.1 = (bf16[8,128,1024]{2,1,0:T(8,128)(2,1)}, bf16[8,128,1024]{2,1,0:T(8,128)(2,1)S(1)}, u32[]{:S(2)}) copy-start(bf16[8,128,1024]{2,1,0:T(8,128)(2,1)S(1)} %all-to-all-done.1.grad_ref) | copy-start | bytes 6291460

commit v3 on v2

--- a/solution.py
+++ b/solution.py
@@ -30,12 +30,16 @@
     return lax.all_to_all(array, "fsdp", 0, 0, axis_index_groups=planes)
 
 
-def after(value, *others):
-    return lax.optimization_barrier((value, *others))[0]
+def together(*values):
+    return lax.optimization_barrier(values)
 
 
 def cost(flops, bytes_accessed):
     return pl.CostEstimate(flops=flops, bytes_accessed=bytes_accessed, transcendentals=0)
+
+
+def roomy():
+    return pltpu.CompilerParams(vmem_limit_bytes=62 * 2**20)
 
 
 def feature_start(member, dz, rows):
@@ -139,16 +143,15 @@
 
 
 def terms_kernel(same_ref, other_ref, first_ref, second_ref, *refs):
-    hiddens, (weight_keep, weight_give, keep, give, cot_ref, hidden_ref) = refs[:PLANE], refs[PLANE:]
+    hiddens, (*outs, keep, give, cot_ref, hidden_ref) = refs[:PLANE], refs[PLANE:]
     _, y, c = place()
     tokens = cot_ref.shape[0] // PLANE
-    rows = weight_keep.shape[1]
+    rows = outs[0].shape[0]
     fill_plane(cot_ref, same_ref, other_ref)
     for member, hidden in enumerate(hiddens):
         hidden_ref[member * tokens : (member + 1) * tokens] = hidden[0]
-    for dz in (1, 3, 0, 2):
-        out = weight_give if dz % 2 else weight_keep
-        out[dz // 2] = lax.dot_general(
+    for dz, out in enumerate(outs):
+        out[...] = lax.dot_general(
             hidden_ref[:, dz * rows : (dz + 1) * rows],
             cot_ref[...],
             (((0,), (0,)), ((), ())),
@@ -166,30 +169,28 @@
 
 def make_terms(same, other, first, second, hidden):
     _, tokens, block = hidden.shape
-    inner, rows = first.shape[1], first.shape[0] // 2
+    inner, rows = same.shape[1], block // NZ
     members = [
         pl.BlockSpec((1, tokens, block), lambda i, member=member: (member, 0, 0))
         for member in range(PLANE)
     ]
     cots = pl.BlockSpec((NY * tokens, inner), lambda i: (0, 0))
     weight = pl.BlockSpec((2 * rows, inner), lambda i: (0, 0))
-    weight_out = pl.BlockSpec((2, rows, inner), lambda i: (0, 0, 0))
-    value_out = pl.BlockSpec((NY, tokens, inner), lambda i: (0, 0, 0))
     return pl.pallas_call(
         terms_kernel,
         grid=(1,),
         in_specs=[cots, cots, weight, weight] + members,
-        out_specs=[weight_out] * 2 + [value_out] * 2,
+        out_specs=[pl.BlockSpec((rows, inner), lambda i: (0, 0))] * NZ
+        + [pl.BlockSpec((NY, tokens, inner), lambda i: (0, 0, 0))] * NC,
         out_shape=[
-            jax.ShapeDtypeStruct((2, rows, inner), F32),
-            jax.ShapeDtypeStruct((2, rows, inner), BF16),
-            jax.ShapeDtypeStruct((NY, tokens, inner), F32),
-            jax.ShapeDtypeStruct((NY, tokens, inner), F32),
-        ],
+            jax.ShapeDtypeStruct((rows, inner), BF16 if dz else F32) for dz in range(NZ)
+        ]
+        + [jax.ShapeDtypeStruct((NY, tokens, inner), F32)] * NC,
         scratch_shapes=[
             pltpu.VMEM((PLANE * tokens, inner), BF16),
             pltpu.VMEM((PLANE * tokens, block), BF16),
         ],
+        compiler_params=roomy(),
         cost_estimate=cost(
             4 * PLANE * tokens * inner * block,
             2 * PLANE * tokens * (3 * inner + block) + 2 * block * inner,
@@ -232,17 +233,27 @@
         ],
         out_specs=pl.BlockSpec((step, width), lambda i: (i, 0)),
         out_shape=jax.ShapeDtypeStruct((tokens, width), F32),
+        compiler_params=roomy(),
         cost_estimate=cost(12 * tokens * width, 8 * tokens * width),
         name="input_grad",
     )(inputs, gain, scale, grads)
 
 
-def halve_columns(total, bits):
-    half = total.shape[1] // 2
-    mine = lax.axis_index("rep") // bits % 2
-    give = lax.dynamic_slice_in_dim(total, (1 - mine) * half, half, 1)
-    keep = lax.dynamic_slice_in_dim(total, mine * half, half, 1)
-    return keep + swap(give, "rep", bits)
+def sum_over_x(delta):
+    width = delta.shape[1] // 4
+    x = lax.axis_index("rep") // 2
+    total = lax.dynamic_slice_in_dim(delta, x * width, width, 1)
+    for dx in (2, 1, 3):
+        piece = lax.dynamic_slice_in_dim(delta, (x ^ dx) * width, width, 1)
+        total = total + swap(piece.astype(BF16), "rep", 2 * dx).astype(F32)
+    return total
+
+
+def sum_over_halves(delta):
+    width = delta.shape[1] // 2
+    half = lax.axis_index("rep") % 2
+    give = lax.dynamic_slice_in_dim(delta, (1 - half) * width, width, 1)
+    return lax.dynamic_slice_in_dim(delta, half * width, width, 1) + swap(give, "rep", 1)
 
 
 def outer_step(total, params, moment):
@@ -262,34 +273,39 @@
     gain = norm_gain.reshape(1, -1)
     rows = value_weight.shape[0]
 
+    first = jnp.concatenate([value_weight, swap(value_weight, "fsdp", 2 * PLANE)], axis=0)
     same = jnp.concatenate(gather_pairs(cotangent, NC), axis=0)
+    scale, blocks = make_hidden(inputs, gain)
+    blocks, same, first = together(blocks, same, first)
+
+    hidden = exchange_plane(blocks)
+    second = swap(first, "fsdp", PLANE)
     other = swap(same, "fsdp", 1)
-    first, second = gather_pairs(value_weight, PLANE)
-    delta = halve_columns(outer_delta, 4)
-
-    scale, blocks = make_hidden(inputs, gain)
-    hidden = exchange_plane(after(blocks, same, first))
-
-    delta = halve_columns(halve_columns(delta, 2), 1)
+    delta = sum_over_x(outer_delta)
+    same, delta = together(same, delta)
+    delta = sum_over_halves(delta)
     new_params, new_moment = outer_step(delta, outer_params, outer_moment)
-
-    grads = make_hidden_grad(after(same, same), other, first, second)
+    grads = make_hidden_grad(same, other, first, second)
+    hidden, new_moment = together(hidden, new_moment)
     back = exchange_plane(grads)
 
-    weight_keep, weight_give, keep, give = make_terms(
-        same, after(other, grads), first, second, hidden
-    )
-    weight_sums = weight_keep + swap(weight_give, "fsdp", PLANE).astype(F32)
-    weight_sum = weight_sums[0] + swap(weight_sums[1].astype(BF16), "fsdp", 2 * PLANE).astype(F32)
+    *terms, keep, give = make_terms(same, other, first, second, hidden)
+    got = [swap(terms[dz], "fsdp", dz * PLANE) for dz in (1, 2, 3)]
+    (pair,) = together(keep + swap(give, "fsdp", 1))
+    back, own = together(back, pair[0])
+    near = swap(pair[2:].astype(BF16), "fsdp", NC)
+    input_grad = make_input_grad(inputs, gain, scale, back)
+    input_grad, near, *got = together(input_grad, near, *got)
+    near = near.astype(F32)
+    far = swap((pair[1] + near[1]).astype(BF16), "fsdp", 2 * NC).astype(F32)
+    values = own + near[0] + far
+    weight_sum = terms[0]
+    for part in got:
+        weight_sum = weight_sum + part.astype(F32)
     scale_grad = 1.0 / math.sqrt(inputs.shape[0] * lax.axis_size("fsdp"))
     weight_grad = weight_sum * scale_grad
     own_gain = lax.dynamic_slice_in_dim(norm_gain, index * rows, rows, 0)
     gain_grad = jnp.sum(weight_grad * value_weight.astype(F32), axis=1) / own_gain
-
-    pair = keep + swap(give, "fsdp", 1)
-    pair = pair[:2] + swap(pair[2:].astype(BF16), "fsdp", NC).astype(F32)
-    values = pair[0] + swap(pair[1].astype(BF16), "fsdp", 2 * NC).astype(F32)
-    input_grad = make_input_grad(inputs, gain, scale, after(back, weight_sums, pair))
     return values, input_grad, weight_grad, gain_grad, new_params, new_moment
 
 

time: 107 us -> 96.9 us (0.906)
  local copies, waits for them, and re-layouts: 8.26 us -> 3.31 us
  waiting for transfers between devices: 30.3 us -> 26.9 us
  other arithmetic: 12.3 us -> 9.6 us
    ppermute x13 -> x15, waiting for transfers between devices: 27.8 us -> 13.9 us  [swap(): lax.ppermute(array, axis, [(source, source ^ bits) for source in range(si...]
    all_to_all x2, waiting for transfers between devices: 2.42 us -> 13 us  [exchange_plane(): return lax.all_to_all(array, 'fsdp', 0, 0, axis_index_groups=planes)]
    unnamed x19 -> x18, local copies, waits for them, and re-layouts: 5.51 us -> 0.69 us
    add x6 -> x3, other arithmetic: 6.36 us -> 3.32 us  [the longest x1 1.43 us: shards(): pair, = together(keep + swap(give, 'fsdp', 1))]
    dynamic_slice x3 -> x1, local copies, waits for them, and re-layouts: 1.92 us -> 0.02 us  [sum_over_halves(): give = lax.dynamic_slice_in_dim(delta, (1 - half) * width, width, 1)]
    convert_element_type x2 -> x1, local copies, waits for them, and re-layouts: 0.76 us -> 1.85 us  [sum_over_x(): total = total + swap(piece.astype(BF16), 'rep', 2 * dx).astype(F32)]
    ppermute x13 -> x15, starting transfers between devices: 26.3 us -> 26 us  [swap(): lax.ppermute(array, axis, [(source, source ^ bits) for source in range(si...]
  transfers between devices with their start and end apart: 15 -> 17, of which waited for: 6 -> 7; matrix products, arithmetic and copies ran while one was open for 15% -> 12% of each run, Pallas kernels for 19% -> 22%
where the time goes in v3:
time: 96.9 us; the launch traced here: 95.2 us
  starting transfers between devices  34 us (35%)
  waiting for transfers between devices  26.9 us (28%)
  Pallas kernels  20.5 us (21%)
  other arithmetic  9.6 us (10%)
  local copies, waits for them, and re-layouts  3.31 us (3%)
    ppermute x15, starting transfers between devices, swap(): lax.ppermute(array, axis, [(source, source ^ bits) for source in range(si...  26 us
    ppermute x15, waiting for transfers between devices, swap(): lax.ppermute(array, axis, [(source, source ^ bits) for source in range(si...  13.9 us
    all_to_all x2, waiting for transfers between devices, exchange_plane(): return lax.all_to_all(array, 'fsdp', 0, 0, axis_index_groups=planes)  13 us
    all_to_all x2, starting transfers between devices, exchange_plane(): return lax.all_to_all(array, 'fsdp', 0, 0, axis_index_groups=planes)  7.97 us
    pallas_call x1, Pallas kernels, make_input_grad(): pl.pallas_call(input_grad_kernel, grid=(tokens // step,), in_specs=[pl.Bl...  5.8 us
    pallas_call x1, Pallas kernels, make_terms(): pl.pallas_call(terms_kernel, grid=(1,), in_specs=[cots, cots, weight, wei...  5.77 us
    pallas_call x1, Pallas kernels, make_hidden_grad(): pl.pallas_call(hidden_grad_kernel, grid=(NZ,), in_specs=[cots, cots, weig...  4.64 us
    pallas_call x1, Pallas kernels, make_hidden(): pl.pallas_call(norm_kernel, grid=(tokens // step,), in_specs=[pl.BlockSpe...  4.28 us
  transfers between devices with their start and end apart: 17, of which 7 were waited for; matrix products, arithmetic and copies ran while one was open for 12% of the time, Pallas kernels for 22%

profile of v3, /device:TPU:2, one launch (start us, length us, event | category | flops | bytes accessed | tf_op | source)
XLA Modules:
  0.0 95.2 jit_solution(15487660028063791121)
XLA Ops:
  0.6 0.0 copy-start.3
  0.7 3.3 %collective-permute-start = (bf16[128,512]{1,0:T(8,128)(2,1)}, bf16[128,512]{1,0:T(8,128)(2,1)S(1)}, u32[]{:S(2)}, u32[]{:S(2)}) collective-permute-start(bf16[128,512]{1,0:T(8,128)(2,1)} %param.8), channel_id=1, source_target_pairs={{0,4},{1,5},{2,6},{3,7},{4,0},{5,1},{6,2},{7,3},{8,12},{9,13},{10,... | collective-permute-start | bytes 393224 | tf_op jit(solution)/shard_map/ppermute | solution.py:25
  3.9 3.3 %collective-permute-start.2 = (bf16[256,512]{1,0:T(8,128)(2,1)}, bf16[256,512]{1,0:T(8,128)(2,1)S(1)}, u32[]{:S(2)}, u32[]{:S(2)}) collective-permute-start(bf16[256,512]{1,0:T(8,128)(2,1)} %param.9), channel_id=1, source_target_pairs={{0,16},{1,17},{2,18},{3,19},{4,20},{5,21},{6,22},{7,23},{8,24},{9,... | collective-permute-start | bytes 786440 | tf_op jit(solution)/shard_map/ppermute | solution.py:25
  7.2 0.5 collective-permute-done
  7.7 0.9 pad_maximum_fusion.2
  8.6 1.7 %collective-permute-start.1 = (bf16[256,512]{1,0:T(8,128)(2,1)S(1)}, bf16[256,512]{1,0:T(8,128)(2,1)S(1)}, u32[]{:S(2)}, u32[]{:S(2)}) collective-permute-start(bf16[256,512]{1,0:T(8,128)(2,1)S(1)} %pad_maximum_fusion.2), channel_id=1, source_target_pairs={{0,2},{1,3},{2,0},{3,1},{4,6},{5,7},{6,4},{7,5},{8,10},{9,11},{10,... | collective-permute-start | bytes 786440 | tf_op jit(solution)/shard_map/ppermute | solution.py:25
  10.3 4.3 %norm.1 = (f32[128,1]{1,0:T(8,128)}, bf16[8,128,1024]{2,1,0:T(8,128)(2,1)}) custom-call(bf16[128,8192]{1,0:T(8,128)(2,1)} %x_ref.3, f32[1,8192]{1,0:T(1,128)} %bitcast.11), custom_call_target="tpu_custom_call" | custom-call | flops 6291456 | bytes 4194304 | tf_op jit(solution)/shard_map/norm/pallas_call | solution.py:68
  14.6 4.5 %collective-permute-done.2 = bf16[256,512]{1,0:T(8,128)(2,1)S(1)} collective-permute-done((bf16[256,512]{1,0:T(8,128)(2,1)}, bf16[256,512]{1,0:T(8,128)(2,1)S(1)}, u32[]{:S(2)}, u32[]{:S(2)}) %collective-permute-start.2) | collective-permute-done | bytes 262176 | tf_op jit(solution)/shard_map/ppermute | solution.py:25
  19.1 0.0 collective-permute-done.1
  19.2 0.0 copy-start.2
  19.2 3.6 %all-to-all-start.1 = ((bf16[8,128,1024]{2,1,0:T(8,128)(2,1)}), bf16[8,128,1024]{2,1,0:T(8,128)(2,1)S(1)}, u32[]{:S(2)}, u32[]{:S(2)}) async-start(bf16[8,128,1024]{2,1,0:T(8,128)(2,1)} %get-tuple-element.32), calls=%async_computation.1 | async-start | bytes 4194304 | tf_op jit(solution)/shard_map/all_to_all | solution.py:30
  22.9 0.9 collective-permute-start.7
  23.8 1.9 %dynamic-slice_convert_fusion.2 = (bf16[256,256]{1,0:T(8,128)(2,1)}, bf16[256,256]{1,0:T(8,128)(2,1)S(1)}, bf16[256,256]{1,0:T(8,128)(2,1)}) fusion(f32[256,1024]{1,0:T(8,128)} %param.11, s32[]{:T(128)S(6)} %select_n.34, s32[]{:T(128)S(6)} %select_n.36, s32[]{:T(128)S(6)} %select_n.35), kind=kLoop, calls=%fused_computation.15 | loop fusion | bytes 786444 | tf_op jit(solution)/shard_map/convert_element_type | solution.py:248
  25.6 2.1 %collective-permute-start.3 = (bf16[256,256]{1,0:T(8,128)(2,1)}, bf16[256,256]{1,0:T(8,128)(2,1)S(1)}, u32[]{:S(2)}, u32[]{:S(2)}) collective-permute-start(bf16[256,256]{1,0:T(8,128)(2,1)} %get-tuple-element.54), channel_id=1, source_target_pairs={{0,128},{32,160},{64,192},{96,224},{128,0},{160,32},{192,64},{224,... | collective-permute-start | bytes 393224 | tf_op jit(solution)/shard_map/ppermute | solution.py:25
  27.8 1.4 %collective-permute-start.4 = (bf16[256,256]{1,0:T(8,128)(2,1)}, bf16[256,256]{1,0:T(8,128)(2,1)S(1)}, u32[]{:S(2)}, u32[]{:S(2)}) collective-permute-start(bf16[256,256]{1,0:T(8,128)(2,1)} %get-tuple-element.56), channel_id=1, source_target_pairs={{0,64},{32,96},{64,0},{96,32},{128,192},{160,224},{192,128},{224,1... | collective-permute-start | bytes 393224 | tf_op jit(solution)/shard_map/ppermute | solution.py:25
  29.2 0.5 collective-permute-start.5
  29.7 3.9 %collective-permute-done.3 = bf16[256,256]{1,0:T(8,128)(2,1)S(1)} collective-permute-done((bf16[256,256]{1,0:T(8,128)(2,1)}, bf16[256,256]{1,0:T(8,128)(2,1)S(1)}, u32[]{:S(2)}, u32[]{:S(2)}) %collective-permute-start.3) | collective-permute-done | bytes 131104 | tf_op jit(solution)/shard_map/ppermute | solution.py:25
  33.6 2.5 %collective-permute-done.4 = bf16[256,256]{1,0:T(8,128)(2,1)S(1)} collective-permute-done((bf16[256,256]{1,0:T(8,128)(2,1)}, bf16[256,256]{1,0:T(8,128)(2,1)S(1)}, u32[]{:S(2)}, u32[]{:S(2)}) %collective-permute-start.4) | collective-permute-done | bytes 131104 | tf_op jit(solution)/shard_map/ppermute | solution.py:25
  36.1 0.7 copy-done.6
  36.8 0.0 collective-permute-done.5
  36.8 1.1 %convert_add_fusion = f32[256,256]{1,0:T(8,128)S(1)} fusion(bf16[256,256]{1,0:T(8,128)(2,1)} %collective-permute-done.5, bf16[256,256]{1,0:T(8,128)(2,1)} %copy-done.6, bf16[256,256]{1,0:T(8,128)(2,1)S(1)} %collective-permute-done.3, f32[256,1024]{1,0:T(8,128)} %param.11, s32[]{:T(128)S(6)} %select_n.33), kind=kLoop, calls=%fused_computation.12 | loop fusion | flops 393216 | bytes 917508 | tf_op jit(solution)/shard_map/add | solution.py:248
  38.0 5.9 %collective-permute-start.8 = (f32[256,128]{1,0:T(8,128)S(1)}, f32[256,128]{1,0:T(8,128)}, u32[]{:S(2)}, u32[]{:S(2)}) collective-permute-start(f32[256,128]{1,0:T(8,128)S(1)} %constant_dynamic-slice_fusion), channel_id=1, source_target_pairs={{0,32},{32,0},{64,96},{96,64},{128,160},{160,128},{192,224},{224,1... | collective-permute-start | bytes 393224 | tf_op jit(solution)/shard_map/ppermute | solution.py:25
  43.9 0.0 collective-permute-done.7.second_ref
  43.9 0.0 collective-permute-done.6.other_ref
  43.9 4.6 %hidden_grad.1 = bf16[8,128,1024]{2,1,0:T(8,128)(2,1)} custom-call(bf16[512,512]{1,0:T(8,128)(2,1)} %copy-done.2, bf16[512,512]{1,0:T(8,128)(2,1)} %collective-permute-done.6.other_ref, bf16[512,512]{1,0:T(8,128)(2,1)} %copy-done.1, bf16[512,512]{1,0:T(8,128)(2,1)} %collective-permute-done.7.second_ref), custom_call_target="tpu_custom_call" | custom-call | flops 1073741824 | bytes 4194304 | tf_op jit(solution)/shard_map/hidden_grad/pallas_call | solution.py:130
  48.5 1.4 %all-to-all-done.1.refs_0_.refs_1_.refs_2_.refs_3_.refs_4_.refs_5_.refs_6_.refs_7_ = bf16[8,128,1024]{2,1,0:T(8,128)(2,1)S(1)} async-done(((bf16[8,128,1024]{2,1,0:T(8,128)(2,1)}), bf16[8,128,1024]{2,1,0:T(8,128)(2,1)S(1)}, u32[]{:S(2)}, u32[]{:S(2)}) %all-to-all-start.1) | async-done | bytes 2097184 | tf_op jit(solution)/shard_map/all_to_all | solution.py:30
  49.9 4.4 %all-to-all-start = ((bf16[8,128,1024]{2,1,0:T(8,128)(2,1)}), bf16[8,128,1024]{2,1,0:T(8,128)(2,1)}, u32[]{:S(2)}, u32[]{:S(2)}) async-start(bf16[8,128,1024]{2,1,0:T(8,128)(2,1)} %hidden_grad.1), calls=%async_computation | async-start | bytes 4194304 | tf_op jit(solution)/shard_map/all_to_all | solution.py:30
  54.3 0.0 collective-permute-done.8
  54.3 1.6 %multiply_subtract_fusion = (f32[256,128]{1,0:T(8,128)}, f32[256,128]{1,0:T(8,128)}) fusion(f32[256,128]{1,0:T(8,128)S(1)} %copy-done.7, f32[256,128]{1,0:T(8,128)} %collective-permute-done.8, f32[256,256]{1,0:T(8,128)S(1)} %convert_add_fusion, s32[]{:T(128)S(6)} %select_n.38, f32[256,128]{1,0:T(8,128)S(1)} %copy-done.8), kind=kLoop, calls=%fused_computation.17 | loop fusion | flops 262144 | bytes 786436 | tf_op jit(solution)/shard_map/sub | solution.py:262
  56.0 5.8 %weight_and_value_terms.1 = (f32[256,512]{1,0:T(8,128)}, bf16[256,512]{1,0:T(8,128)(2,1)}, bf16[256,512]{1,0:T(8,128)(2,1)}, bf16[256,512]{1,0:T(8,128)(2,1)}, f...) custom-call(bf16[512,512]{1,0:T(8,128)(2,1)} %copy-done.2, bf16[512,512]{1,0:T(8,128)(2,1)} %collective-permute-done.6.other_ref, ...), custom_call_target="tpu_custom_call" | custom-call | flops 2147483648 | bytes 6291456 | tf_op jit(solution)/shard_map/weight_and_value_terms/pallas_call | solution.py:179
  61.8 0.4 collective-permute-start.9
  62.1 1.1 %collective-permute-start.11 = (bf16[256,512]{1,0:T(8,128)(2,1)}, bf16[256,512]{1,0:T(8,128)(2,1)}, u32[]{:S(2)}, u32[]{:S(2)}) collective-permute-start(bf16[256,512]{1,0:T(8,128)(2,1)} %get-tuple-element.40), channel_id=1, source_target_pairs={{0,8},{1,9},{2,10},{3,11},{4,12},{5,13},{6,14},{7,15},{8,0},{9,1},... | collective-permute-start | bytes 786440 | tf_op jit(solution)/shard_map/ppermute | solution.py:25
  63.2 3.0 %collective-permute-start.12 = (bf16[256,512]{1,0:T(8,128)(2,1)}, bf16[256,512]{1,0:T(8,128)(2,1)}, u32[]{:S(2)}, u32[]{:S(2)}) collective-permute-start(bf16[256,512]{1,0:T(8,128)(2,1)} %get-tuple-element.41), channel_id=1, source_target_pairs={{0,16},{1,17},{2,18},{3,19},{4,20},{5,21},{6,22},{7,23},{8,24},{9,... | collective-permute-start | bytes 786440 | tf_op jit(solution)/shard_map/ppermute | solution.py:25
  66.2 0.3 collective-permute-start.13
  66.5 1.4 %add.78 = f32[4,128,512]{2,1,0:T(8,128)S(1)} add(f32[4,128,512]{2,1,0:T(8,128)} %get-tuple-element.35, f32[4,128,512]{2,1,0:T(8,128)S(1)} %collective-permute-done.9) | non-fusion elementwise | flops 262144 | bytes 3145728 | tf_op jit(solution)/shard_map/add | solution.py:294
  67.9 0.7 slice.41
  68.7 1.7 %collective-permute-start.10 = (bf16[2,128,512]{2,1,0:T(8,128)(2,1)}, bf16[2,128,512]{2,1,0:T(8,128)(2,1)S(1)}, u32[]{:S(2)}, u32[]{:S(2)}) collective-permute-start(bf16[2,128,512]{2,1,0:T(8,128)(2,1)} %slice.41), channel_id=1, source_target_pairs={{0,2},{1,3},{2,0},{3,1},{4,6},{5,7},{6,4},{7,5},{8,10},{9,11},{10,... | collective-permute-start | bytes 786440 | tf_op jit(solution)/shard_map/ppermute | solution.py:25
  70.4 11.6 %all-to-all-done.grad_ref = bf16[8,128,1024]{2,1,0:T(8,128)(2,1)} async-done(((bf16[8,128,1024]{2,1,0:T(8,128)(2,1)}), bf16[8,128,1024]{2,1,0:T(8,128)(2,1)}, u32[]{:S(2)}, u32[]{:S(2)}) %all-to-all-start) | async-done | bytes 2097184 | tf_op jit(solution)/shard_map/all_to_all | solution.py:30
  82.0 5.8 %input_grad.1 = f32[128,8192]{1,0:T(8,128)} custom-call(bf16[128,8192]{1,0:T(8,128)(2,1)} %x_ref.3, f32[1,8192]{1,0:T(1,128)} %bitcast.12, f32[128,1]{1,0:T(8,128)} %get-tuple-element.38.scale_ref, bf16[8,128,1024]{2,1,0:T(8,128)(2,1)} %all-to-all-done.grad_ref), custom_call_target="tpu_custom_call" | custom-call | flops 12582912 | bytes 8388608 | tf_op jit(solution)/shard_map/input_grad/pallas_call | solution.py:225
  87.8 0.0 collective-permute-done.12
  87.8 0.0 collective-permute-done.13
  87.8 0.0 collective-permute-done.10
  87.8 0.1 convert_element_type.49
  87.9 0.5 collective-permute-start.14
  88.4 2.2 %multiply_reduce_fusion = (f32[256]{0:T(256)S(1)}, f32[256,512]{1,0:T(8,128)}) fusion(bf16[256,512]{1,0:T(8,128)(2,1)S(1)} %copy-done.4, bf16[256,512]{1,0:T(8,128)(2,1)} %collective-permute-done.13, bf16[256,512]{1,0:T(8,128)(2,1)} %collective-permute-done.12, f32[256,512]{1,0:T(8,128)} %get-tuple-element.45, bf16[256,512]{1,0:T(8,128)(2,1)} %collective-permute-done.11), kind=kLoop, calls=%fused_computation.3 | loop fusion | flops 1310464 | bytes 2098176 | tf_op jit(solution)/shard_map/reduce_sum | solution.py:308
  90.6 1.3 %dynamic-slice_divide_fusion = f32[256]{0:T(256)} fusion(f32[256]{0:T(256)S(1)} %get-tuple-element.52, f32[8192]{0:T(1024)} %param.10, s32[]{:T(128)S(6)} %select_n.40), kind=kLoop, calls=%fused_computation.21 | loop fusion | flops 256 | bytes 3076 | tf_op jit(solution)/shard_map/div | solution.py:308
  91.9 2.5 %collective-permute-done.14 = bf16[128,512]{1,0:T(8,128)(2,1)S(1)} collective-permute-done((bf16[128,512]{1,0:T(8,128)(2,1)S(1)}, bf16[128,512]{1,0:T(8,128)(2,1)S(1)}, u32[]{:S(2)}, u32[]{:S(2)}) %collective-permute-start.14) | collective-permute-done | bytes 131104 | tf_op jit(solution)/shard_map/ppermute | solution.py:25
  94.5 0.8 fusion.2
  (23 shorter events, 0.2 us)
Async XLA Ops:
  0.6 18.5 %copy-start.5 = (bf16[128,512]{1,0:T(8,128)(2,1)S(1)}, bf16[128,512]{1,0:T(8,128)(2,1)}, u32[]{:S(2)}) copy-start(bf16[128,512]{1,0:T(8,128)(2,1)} %param.8) | copy-start | bytes 393220
  0.6 18.4 %copy-start.3 = (bf16[256,512]{1,0:T(8,128)(2,1)S(1)}, bf16[256,512]{1,0:T(8,128)(2,1)}, u32[]{:S(2)}) copy-start(bf16[256,512]{1,0:T(8,128)(2,1)} %param.9) | copy-start | bytes 786436
  0.7 7.0 %collective-permute-start = (bf16[128,512]{1,0:T(8,128)(2,1)}, bf16[128,512]{1,0:T(8,128)(2,1)S(1)}, u32[]{:S(2)}, u32[]{:S(2)}) collective-permute-start(bf16[128,512]{1,0:T(8,128)(2,1)} %param.8), channel_id=1, source_target_pairs={{0,4},{1,5},{2,6},{3,7},{4,0},{5,1},{6,2},{7,3},{8,12},{9,13},{10,... | collective-permute-start | bytes 393224 | tf_op jit(solution)/shard_map/ppermute | solution.py:25
  3.9 15.1 %collective-permute-start.2 = (bf16[256,512]{1,0:T(8,128)(2,1)}, bf16[256,512]{1,0:T(8,128)(2,1)S(1)}, u32[]{:S(2)}, u32[]{:S(2)}) collective-permute-start(bf16[256,512]{1,0:T(8,128)(2,1)} %param.9), channel_id=1, source_target_pairs={{0,16},{1,17},{2,18},{3,19},{4,20},{5,21},{6,22},{7,23},{8,24},{9,... | collective-permute-start | bytes 786440 | tf_op jit(solution)/shard_map/ppermute | solution.py:25
  8.6 10.5 %collective-permute-start.1 = (bf16[256,512]{1,0:T(8,128)(2,1)S(1)}, bf16[256,512]{1,0:T(8,128)(2,1)S(1)}, u32[]{:S(2)}, u32[]{:S(2)}) collective-permute-start(bf16[256,512]{1,0:T(8,128)(2,1)S(1)} %pad_maximum_fusion.2), channel_id=1, source_target_pairs={{0,2},{1,3},{2,0},{3,1},{4,6},{5,7},{6,4},{7,5},{8,10},{9,11},{10,... | collective-permute-start | bytes 786440 | tf_op jit(solution)/shard_map/ppermute | solution.py:25
  19.1 3.7 %copy-start.1 = (bf16[512,512]{1,0:T(8,128)(2,1)}, bf16[512,512]{1,0:T(8,128)(2,1)S(1)}, u32[]{:S(2)}) copy-start(bf16[512,512]{1,0:T(8,128)(2,1)S(1)} %pad_maximum_fusion.1.first_ref) | copy-start | bytes 1572868
  19.2 4.6 %copy-start.2 = (bf16[512,512]{1,0:T(8,128)(2,1)}, bf16[512,512]{1,0:T(8,128)(2,1)S(1)}, u32[]{:S(2)}) copy-start(bf16[512,512]{1,0:T(8,128)(2,1)S(1)} %pad_maximum_fusion.same_ref) | copy-start | bytes 1572868
  19.2 30.7 %all-to-all-start.1 = ((bf16[8,128,1024]{2,1,0:T(8,128)(2,1)}), bf16[8,128,1024]{2,1,0:T(8,128)(2,1)S(1)}, u32[]{:S(2)}, u32[]{:S(2)}) async-start(bf16[8,128,1024]{2,1,0:T(8,128)(2,1)} %get-tuple-element.32), calls=%async_computation.1 | async-start | bytes 4194304 | tf_op jit(solution)/shard_map/all_to_all | solution.py:30
  22.9 21.0 %collective-permute-start.7 = (bf16[512,512]{1,0:T(8,128)(2,1)S(1)}, bf16[512,512]{1,0:T(8,128)(2,1)}, u32[]{:S(2)}, u32[]{:S(2)}) collective-permute-start(bf16[512,512]{1,0:T(8,128)(2,1)S(1)} %pad_maximum_fusion.1.first_ref), channel_id=1, source_target_pairs={{0,8},{1,9},{2,10},{3,11},{4,12},{5,13},{6,14},{7,15},{8,0},{9,1},... | collective-permute-start | bytes 1572872 | tf_op jit(solution)/shard_map/ppermute | solution.py:25
  23.8 20.1 %collective-permute-start.6 = (bf16[512,512]{1,0:T(8,128)(2,1)S(1)}, bf16[512,512]{1,0:T(8,128)(2,1)}, u32[]{:S(2)}, u32[]{:S(2)}) collective-permute-start(bf16[512,512]{1,0:T(8,128)(2,1)S(1)} %pad_maximum_fusion.same_ref), channel_id=1, source_target_pairs={{0,1},{1,0},{2,3},{3,2},{4,5},{5,4},{6,7},{7,6},{8,9},{9,8},{10,11... | collective-permute-start | bytes 1572872 | tf_op jit(solution)/shard_map/ppermute | solution.py:25
  25.6 8.0 %collective-permute-start.3 = (bf16[256,256]{1,0:T(8,128)(2,1)}, bf16[256,256]{1,0:T(8,128)(2,1)S(1)}, u32[]{:S(2)}, u32[]{:S(2)}) collective-permute-start(bf16[256,256]{1,0:T(8,128)(2,1)} %get-tuple-element.54), channel_id=1, source_target_pairs={{0,128},{32,160},{64,192},{96,224},{128,0},{160,32},{192,64},{224,... | collective-permute-start | bytes 393224 | tf_op jit(solution)/shard_map/ppermute | solution.py:25
  27.8 8.4 %collective-permute-start.4 = (bf16[256,256]{1,0:T(8,128)(2,1)}, bf16[256,256]{1,0:T(8,128)(2,1)S(1)}, u32[]{:S(2)}, u32[]{:S(2)}) collective-permute-start(bf16[256,256]{1,0:T(8,128)(2,1)} %get-tuple-element.56), channel_id=1, source_target_pairs={{0,64},{32,96},{64,0},{96,32},{128,192},{160,224},{192,128},{224,1... | collective-permute-start | bytes 393224 | tf_op jit(solution)/shard_map/ppermute | solution.py:25
  29.2 7.6 %collective-permute-start.5 = (bf16[256,256]{1,0:T(8,128)(2,1)S(1)}, bf16[256,256]{1,0:T(8,128)(2,1)}, u32[]{:S(2)}, u32[]{:S(2)}) collective-permute-start(bf16[256,256]{1,0:T(8,128)(2,1)S(1)} %get-tuple-element.55), channel_id=1, source_target_pairs={{0,192},{32,224},{64,128},{96,160},{128,64},{160,96},{192,0},{224,... | collective-permute-start | bytes 393224 | tf_op jit(solution)/shard_map/ppermute | solution.py:25
  36.1 0.7 copy-start.6
  38.0 16.4 %collective-permute-start.8 = (f32[256,128]{1,0:T(8,128)S(1)}, f32[256,128]{1,0:T(8,128)}, u32[]{:S(2)}, u32[]{:S(2)}) collective-permute-start(f32[256,128]{1,0:T(8,128)S(1)} %constant_dynamic-slice_fusion), channel_id=1, source_target_pairs={{0,32},{32,0},{64,96},{96,64},{128,160},{160,128},{192,224},{224,1... | collective-permute-start | bytes 393224 | tf_op jit(solution)/shard_map/ppermute | solution.py:25
  48.5 5.8 %copy-start.7 = (f32[256,128]{1,0:T(8,128)S(1)}, f32[256,128]{1,0:T(8,128)}, u32[]{:S(2)}) copy-start(f32[256,128]{1,0:T(8,128)} %param.12) | copy-start | bytes 393220
  48.5 5.8 %copy-start.8 = (f32[256,128]{1,0:T(8,128)S(1)}, f32[256,128]{1,0:T(8,128)}, u32[]{:S(2)}) copy-start(f32[256,128]{1,0:T(8,128)} %param.13) | copy-start | bytes 393220
  49.9 4.4 %copy-start = (bf16[8,128,1024]{2,1,0:T(8,128)(2,1)}, bf16[8,128,1024]{2,1,0:T(8,128)(2,1)S(1)}, u32[]{:S(2)}) copy-start(bf16[8,128,1024]{2,1,0:T(8,128)(2,1)S(1)} %all-to-all-done.1.refs_0_.refs_1_.refs_2_.refs_3_.refs_4_.refs_5_.refs_6_.refs_7_) | copy-start | bytes 6291460
  49.9 32.0 %all-to-all-start = ((bf16[8,128,1024]{2,1,0:T(8,128)(2,1)}), bf16[8,128,1024]{2,1,0:T(8,128)(2,1)}, u32[]{:S(2)}, u32[]{:S(2)}) async-start(bf16[8,128,1024]{2,1,0:T(8,128)(2,1)} %hidden_grad.1), calls=%async_computation | async-start | bytes 4194304 | tf_op jit(solution)/shard_map/all_to_all | solution.py:30
  61.8 4.8 %collective-permute-start.9 = (f32[4,128,512]{2,1,0:T(8,128)}, f32[4,128,512]{2,1,0:T(8,128)S(1)}, u32[]{:S(2)}, u32[]{:S(2)}) collective-permute-start(f32[4,128,512]{2,1,0:T(8,128)} %get-tuple-element.36), channel_id=1, source_target_pairs={{0,1},{1,0},{2,3},{3,2},{4,5},{5,4},{6,7},{7,6},{8,9},{9,8},{10,11... | collective-permute-start | bytes 3145736 | tf_op jit(solution)/shard_map/ppermute | solution.py:25
  62.1 25.6 %collective-permute-start.11 = (bf16[256,512]{1,0:T(8,128)(2,1)}, bf16[256,512]{1,0:T(8,128)(2,1)}, u32[]{:S(2)}, u32[]{:S(2)}) collective-permute-start(bf16[256,512]{1,0:T(8,128)(2,1)} %get-tuple-element.40), channel_id=1, source_target_pairs={{0,8},{1,9},{2,10},{3,11},{4,12},{5,13},{6,14},{7,15},{8,0},{9,1},... | collective-permute-start | bytes 786440 | tf_op jit(solution)/shard_map/ppermute | solution.py:25
  63.2 24.6 %collective-permute-start.12 = (bf16[256,512]{1,0:T(8,128)(2,1)}, bf16[256,512]{1,0:T(8,128)(2,1)}, u32[]{:S(2)}, u32[]{:S(2)}) collective-permute-start(bf16[256,512]{1,0:T(8,128)(2,1)} %get-tuple-element.41), channel_id=1, source_target_pairs={{0,16},{1,17},{2,18},{3,19},{4,20},{5,21},{6,22},{7,23},{8,24},{9,... | collective-permute-start | bytes 786440 | tf_op jit(solution)/shard_map/ppermute | solution.py:25
  66.2 21.6 %collective-permute-start.13 = (bf16[256,512]{1,0:T(8,128)(2,1)}, bf16[256,512]{1,0:T(8,128)(2,1)}, u32[]{:S(2)}, u32[]{:S(2)}) collective-permute-start(bf16[256,512]{1,0:T(8,128)(2,1)} %get-tuple-element.42), channel_id=1, source_target_pairs={{0,24},{1,25},{2,26},{3,27},{4,28},{5,29},{6,30},{7,31},{8,16},{9,... | collective-permute-start | bytes 786440 | tf_op jit(solution)/shard_map/ppermute | solution.py:25
  68.7 19.1 %collective-permute-start.10 = (bf16[2,128,512]{2,1,0:T(8,128)(2,1)}, bf16[2,128,512]{2,1,0:T(8,128)(2,1)S(1)}, u32[]{:S(2)}, u32[]{:S(2)}) collective-permute-start(bf16[2,128,512]{2,1,0:T(8,128)(2,1)} %slice.41), channel_id=1, source_target_pairs={{0,2},{1,3},{2,0},{3,1},{4,6},{5,7},{6,4},{7,5},{8,10},{9,11},{10,... | collective-permute-start | bytes 786440 | tf_op jit(solution)/shard_map/ppermute | solution.py:25
  82.0 6.4 %copy-start.4 = (bf16[256,512]{1,0:T(8,128)(2,1)S(1)}, bf16[256,512]{1,0:T(8,128)(2,1)}, u32[]{:S(2)}) copy-start(bf16[256,512]{1,0:T(8,128)(2,1)} %param.9) | copy-start | bytes 786436
  87.9 6.6 %collective-permute-start.14 = (bf16[128,512]{1,0:T(8,128)(2,1)S(1)}, bf16[128,512]{1,0:T(8,128)(2,1)S(1)}, u32[]{:S(2)}, u32[]{:S(2)}) collective-permute-start(bf16[128,512]{1,0:T(8,128)(2,1)S(1)} %fusion.3), channel_id=1, source_target_pairs={{0,4},{1,5},{2,6},{3,7},{4,0},{5,1},{6,2},{7,3},{8,12},{9,13},{10,... | collective-permute-start | bytes 393224 | tf_op jit(solution)/shard_map/ppermute | solution.py:25

commit v4 on v3

--- a/solution.py
+++ b/solution.py
@@ -159,10 +159,10 @@
         ).astype(out.dtype)
     first, second = first_ref[...], second_ref[...]
     weight = jnp.concatenate([first[:rows], second[:rows], first[rows:], second[rows:]], axis=0)
-    for at, dy in enumerate(HALVES):
+    for dy in range(NY):
         for dc, out in enumerate((keep, give)):
             start = pl.multiple_of(((y ^ dy) * NC + (c ^ dc)) * tokens, tokens)
-            out[at] = jnp.dot(
+            out[dy] = jnp.dot(
                 hidden_ref[pl.ds(start, tokens)], weight, preferred_element_type=F32
             )
 
@@ -199,7 +199,8 @@
     )(same, other, first, second, *[hidden] * PLANE)
 
 
-def input_grad_kernel(x_ref, gain_ref, scale_ref, grad_ref, out_ref):
+def input_grad_kernel(x_ref, gain_ref, scale_ref, *refs):
+    grads, out_ref = refs[:NY], refs[NY]
     width = x_ref.shape[1]
     rows = width // (NZ * PLANE)
     scale = scale_ref[...]
@@ -207,21 +208,24 @@
     for dz in range(NZ):
         for member in range(PLANE):
             at = pl.ds(feature_start(member, dz, rows), rows)
-            grad = grad_ref[member, :, dz * rows : (dz + 1) * rows].astype(F32)
-            total += (grad * gain_ref[:, at]) * (x_ref[:, at].astype(F32) * scale)
-    mean = jnp.sum(total, axis=-1, keepdims=True) * (1.0 / width)
-    for dz in range(NZ):
-        for member in range(PLANE):
-            at = pl.ds(feature_start(member, dz, rows), rows)
-            grad = grad_ref[member, :, dz * rows : (dz + 1) * rows].astype(F32)
-            normed = x_ref[:, at].astype(F32) * scale
-            out_ref[:, at] = scale * (grad * gain_ref[:, at] - normed * mean)
+            grad = grads[member // NC][member % NC, :, dz * rows : (dz + 1) * rows]
+            scaled = grad.astype(F32) * gain_ref[:, at]
+            out_ref[:, at] = scaled
+            total += scaled * x_ref[:, at].astype(F32)
+    mean = scale * jnp.sum(total, axis=-1, keepdims=True) * (1.0 / width)
+    factor = scale * scale * mean
+    for block in range(NZ * PLANE):
+        at = slice(block * rows, (block + 1) * rows)
+        out_ref[:, at] = scale * out_ref[:, at] - x_ref[:, at].astype(F32) * factor
 
 
 def make_input_grad(inputs, gain, scale, grads):
     tokens, width = inputs.shape
     step = 32
     block = width // PLANE
+    members = [
+        pl.BlockSpec((NC, step, block), lambda i, pair=pair: (pair, i, 0)) for pair in range(NY)
+    ]
     return pl.pallas_call(
         input_grad_kernel,
         grid=(tokens // step,),
@@ -229,14 +233,14 @@
             pl.BlockSpec((step, width), lambda i: (i, 0)),
             pl.BlockSpec((1, width), lambda i: (0, 0)),
             pl.BlockSpec((step, 1), lambda i: (i, 0)),
-            pl.BlockSpec((PLANE, step, block), lambda i: (0, i, 0)),
-        ],
+        ]
+        + members,
         out_specs=pl.BlockSpec((step, width), lambda i: (i, 0)),
         out_shape=jax.ShapeDtypeStruct((tokens, width), F32),
         compiler_params=roomy(),
-        cost_estimate=cost(12 * tokens * width, 8 * tokens * width),
+        cost_estimate=cost(9 * tokens * width, 8 * tokens * width),
         name="input_grad",
-    )(inputs, gain, scale, grads)
+    )(inputs, gain, scale, *[grads] * NY)
 
 
 def sum_over_x(delta):
@@ -274,38 +278,41 @@
     rows = value_weight.shape[0]
 
     first = jnp.concatenate([value_weight, swap(value_weight, "fsdp", 2 * PLANE)], axis=0)
-    same = jnp.concatenate(gather_pairs(cotangent, NC), axis=0)
+    same = jnp.concatenate(
+        [cotangent] + [swap(cotangent, "fsdp", dy * NC) for dy in HALVES[1:]], axis=0
+    )
     scale, blocks = make_hidden(inputs, gain)
     blocks, same, first = together(blocks, same, first)
 
     hidden = exchange_plane(blocks)
     second = swap(first, "fsdp", PLANE)
     other = swap(same, "fsdp", 1)
+    own_gain = lax.dynamic_slice_in_dim(norm_gain, index * rows, rows, 0)
+    weight_by_gain = value_weight.astype(F32) / own_gain[:, None]
     delta = sum_over_x(outer_delta)
     same, delta = together(same, delta)
     delta = sum_over_halves(delta)
     new_params, new_moment = outer_step(delta, outer_params, outer_moment)
     grads = make_hidden_grad(same, other, first, second)
-    hidden, new_moment = together(hidden, new_moment)
+    hidden, new_moment, weight_by_gain = together(hidden, new_moment, weight_by_gain)
     back = exchange_plane(grads)
 
     *terms, keep, give = make_terms(same, other, first, second, hidden)
     got = [swap(terms[dz], "fsdp", dz * PLANE) for dz in (1, 2, 3)]
     (pair,) = together(keep + swap(give, "fsdp", 1))
     back, own = together(back, pair[0])
-    near = swap(pair[2:].astype(BF16), "fsdp", NC)
+    far = swap(pair[2:].astype(BF16), "fsdp", 2 * NC)
     input_grad = make_input_grad(inputs, gain, scale, back)
-    input_grad, near, *got = together(input_grad, near, *got)
-    near = near.astype(F32)
-    far = swap((pair[1] + near[1]).astype(BF16), "fsdp", 2 * NC).astype(F32)
-    values = own + near[0] + far
+    input_grad, far, *got = together(input_grad, far, *got)
+    far = far.astype(F32)
+    near = swap((pair[1] + far[1]).astype(BF16), "fsdp", NC).astype(F32)
+    values = own + far[0] + near
     weight_sum = terms[0]
     for part in got:
         weight_sum = weight_sum + part.astype(F32)
     scale_grad = 1.0 / math.sqrt(inputs.shape[0] * lax.axis_size("fsdp"))
     weight_grad = weight_sum * scale_grad
-    own_gain = lax.dynamic_slice_in_dim(norm_gain, index * rows, rows, 0)
-    gain_grad = jnp.sum(weight_grad * value_weight.astype(F32), axis=1) / own_gain
+    gain_grad = jnp.sum(weight_grad * weight_by_gain, axis=1)
     return values, input_grad, weight_grad, gain_grad, new_params, new_moment
 
 

time: 96.9 us -> 94.3 us (0.973)
  the two profiles are of different devices: /device:TPU:2 before, /device:TPU:44 now
where the time goes in v4:
time: 94.3 us; the launch traced here: 93.7 us
  starting transfers between devices  36 us (38%)
  waiting for transfers between devices  23.7 us (25%)
  Pallas kernels  20.2 us (21%)
  other arithmetic  9.02 us (10%)
  local copies, waits for them, and re-layouts  4.07 us (4%)
    ppermute x16, starting transfers between devices, swap(): lax.ppermute(array, axis, [(source, source ^ bits) for source in range(si...  25.7 us
    ppermute x16, waiting for transfers between devices, swap(): lax.ppermute(array, axis, [(source, source ^ bits) for source in range(si...  13.3 us
    all_to_all x2, waiting for transfers between devices, exchange_plane(): return lax.all_to_all(array, 'fsdp', 0, 0, axis_index_groups=planes)  10.4 us
    all_to_all x2, starting transfers between devices, exchange_plane(): return lax.all_to_all(array, 'fsdp', 0, 0, axis_index_groups=planes)  10.3 us
    pallas_call x1, Pallas kernels, make_terms(): pl.pallas_call(terms_kernel, grid=(1,), in_specs=[cots, cots, weight, wei...  5.77 us
    pallas_call x1, Pallas kernels, make_input_grad(): pl.pallas_call(input_grad_kernel, grid=(tokens // step,), in_specs=[pl.Bl...  5.49 us
    pallas_call x1, Pallas kernels, make_hidden_grad(): pl.pallas_call(hidden_grad_kernel, grid=(NZ,), in_specs=[cots, cots, weig...  4.64 us
    pallas_call x1, Pallas kernels, make_hidden(): pl.pallas_call(norm_kernel, grid=(tokens // step,), in_specs=[pl.BlockSpe...  4.28 us
  transfers between devices with their start and end apart: 18, of which 8 were waited for; matrix products, arithmetic and copies ran while one was open for 11% of the time, Pallas kernels for 22%

profile of v4, /device:TPU:44, one launch (start us, length us, event | category | flops | bytes accessed | tf_op | source)
XLA Modules:
  0.0 93.7 jit_solution(474230745978758111)
XLA Ops:
  0.6 0.0 copy-start.3
  0.7 3.4 %collective-permute-start.3 = (bf16[256,512]{1,0:T(8,128)(2,1)}, bf16[256,512]{1,0:T(8,128)(2,1)S(1)}, u32[]{:S(2)}, u32[]{:S(2)}) collective-permute-start(bf16[256,512]{1,0:T(8,128)(2,1)} %param.9), channel_id=1, source_target_pairs={{0,16},{1,17},{2,18},{3,19},{4,20},{5,21},{6,22},{7,23},{8,24},{9,... | collective-permute-start | bytes 786440 | tf_op jit(solution)/shard_map/ppermute | solution.py:25
  4.0 2.3 %collective-permute-start = (bf16[128,512]{1,0:T(8,128)(2,1)}, bf16[128,512]{1,0:T(8,128)(2,1)S(1)}, u32[]{:S(2)}, u32[]{:S(2)}) collective-permute-start(bf16[128,512]{1,0:T(8,128)(2,1)} %param.8), channel_id=1, source_target_pairs={{0,4},{1,5},{2,6},{3,7},{4,0},{5,1},{6,2},{7,3},{8,12},{9,13},{10,... | collective-permute-start | bytes 393224 | tf_op jit(solution)/shard_map/ppermute | solution.py:25
  6.3 1.3 %collective-permute-start.1 = (bf16[128,512]{1,0:T(8,128)(2,1)}, bf16[128,512]{1,0:T(8,128)(2,1)S(1)}, u32[]{:S(2)}, u32[]{:S(2)}) collective-permute-start(bf16[128,512]{1,0:T(8,128)(2,1)} %param.8), channel_id=1, source_target_pairs={{0,2},{1,3},{2,0},{3,1},{4,6},{5,7},{6,4},{7,5},{8,10},{9,11},{10,... | collective-permute-start | bytes 393224 | tf_op jit(solution)/shard_map/ppermute | solution.py:25
  7.7 0.5 collective-permute-start.2
  8.1 4.3 %norm.1 = (f32[128,1]{1,0:T(8,128)}, bf16[8,128,1024]{2,1,0:T(8,128)(2,1)}) custom-call(bf16[128,8192]{1,0:T(8,128)(2,1)} %x_ref.3, f32[1,8192]{1,0:T(1,128)} %bitcast.11), custom_call_target="tpu_custom_call" | custom-call | flops 6291456 | bytes 4194304 | tf_op jit(solution)/shard_map/norm/pallas_call | solution.py:68
  12.4 0.0 collective-permute-done
  12.4 1.2 %collective-permute-done.1 = bf16[128,512]{1,0:T(8,128)(2,1)S(1)} collective-permute-done((bf16[128,512]{1,0:T(8,128)(2,1)}, bf16[128,512]{1,0:T(8,128)(2,1)S(1)}, u32[]{:S(2)}, u32[]{:S(2)}) %collective-permute-start.1) | collective-permute-done | bytes 131104 | tf_op jit(solution)/shard_map/ppermute | solution.py:25
  13.6 0.0 collective-permute-done.2
  13.7 0.0 copy-start.1
  13.7 1.4 %collective-permute-done.3 = bf16[256,512]{1,0:T(8,128)(2,1)S(1)} collective-permute-done((bf16[256,512]{1,0:T(8,128)(2,1)}, bf16[256,512]{1,0:T(8,128)(2,1)S(1)}, u32[]{:S(2)}, u32[]{:S(2)}) %collective-permute-start.3) | collective-permute-done | bytes 262176 | tf_op jit(solution)/shard_map/ppermute | solution.py:25
  15.1 4.9 %all-to-all-start.1 = ((bf16[8,128,1024]{2,1,0:T(8,128)(2,1)}), bf16[8,128,1024]{2,1,0:T(8,128)(2,1)S(1)}, u32[]{:S(2)}, u32[]{:S(2)}) async-start(bf16[8,128,1024]{2,1,0:T(8,128)(2,1)} %get-tuple-element.33), calls=%async_computation.1 | async-start | bytes 4194304 | tf_op jit(solution)/shard_map/all_to_all | solution.py:30
  20.0 1.2 %collective-permute-start.8 = (bf16[512,512]{1,0:T(8,128)(2,1)S(1)}, bf16[512,512]{1,0:T(8,128)(2,1)}, u32[]{:S(2)}, u32[]{:S(2)}) collective-permute-start(bf16[512,512]{1,0:T(8,128)(2,1)S(1)} %pad_maximum_fusion.1.first_ref), channel_id=1, source_target_pairs={{0,8},{1,9},{2,10},{3,11},{4,12},{5,13},{6,14},{7,15},{8,0},{9,1},... | collective-permute-start | bytes 1572872 | tf_op jit(solution)/shard_map/ppermute | solution.py:25
  21.2 0.0 collective-permute-start.7
  21.2 1.9 %dynamic-slice_convert_fusion.2 = (bf16[256,256]{1,0:T(8,128)(2,1)}, bf16[256,256]{1,0:T(8,128)(2,1)S(1)}, bf16[256,256]{1,0:T(8,128)(2,1)}) fusion(f32[256,1024]{1,0:T(8,128)} %param.11, s32[]{:T(128)S(6)} %select_n.34, s32[]{:T(128)S(6)} %select_n.36, s32[]{:T(128)S(6)} %select_n.35), kind=kLoop, calls=%fused_computation.15 | loop fusion | bytes 786444 | tf_op jit(solution)/shard_map/convert_element_type | solution.py:252
  23.1 0.5 collective-permute-start.4
  23.6 2.1 %collective-permute-start.5 = (bf16[256,256]{1,0:T(8,128)(2,1)}, bf16[256,256]{1,0:T(8,128)(2,1)S(1)}, u32[]{:S(2)}, u32[]{:S(2)}) collective-permute-start(bf16[256,256]{1,0:T(8,128)(2,1)} %get-tuple-element.58), channel_id=1, source_target_pairs={{0,64},{32,96},{64,0},{96,32},{128,192},{160,224},{192,128},{224,1... | collective-permute-start | bytes 393224 | tf_op jit(solution)/shard_map/ppermute | solution.py:25
  25.7 1.5 %collective-permute-start.6 = (bf16[256,256]{1,0:T(8,128)(2,1)S(1)}, bf16[256,256]{1,0:T(8,128)(2,1)}, u32[]{:S(2)}, u32[]{:S(2)}) collective-permute-start(bf16[256,256]{1,0:T(8,128)(2,1)S(1)} %get-tuple-element.57), channel_id=1, source_target_pairs={{0,192},{32,224},{64,128},{96,160},{128,64},{160,96},{192,0},{224,... | collective-permute-start | bytes 393224 | tf_op jit(solution)/shard_map/ppermute | solution.py:25
  27.2 0.8 dynamic_slice.27
  27.9 3.2 %collective-permute-done.4 = bf16[256,256]{1,0:T(8,128)(2,1)S(1)} collective-permute-done((bf16[256,256]{1,0:T(8,128)(2,1)}, bf16[256,256]{1,0:T(8,128)(2,1)S(1)}, u32[]{:S(2)}, u32[]{:S(2)}) %collective-permute-start.4) | collective-permute-done | bytes 131104 | tf_op jit(solution)/shard_map/ppermute | solution.py:25
  31.1 1.5 %collective-permute-done.5 = bf16[256,256]{1,0:T(8,128)(2,1)S(1)} collective-permute-done((bf16[256,256]{1,0:T(8,128)(2,1)}, bf16[256,256]{1,0:T(8,128)(2,1)S(1)}, u32[]{:S(2)}, u32[]{:S(2)}) %collective-permute-start.5) | collective-permute-done | bytes 131104 | tf_op jit(solution)/shard_map/ppermute | solution.py:25
  32.6 0.7 copy-done.5
  33.3 0.4 collective-permute-done.6
  33.6 1.1 %convert_add_fusion = f32[256,256]{1,0:T(8,128)S(1)} fusion(bf16[256,256]{1,0:T(8,128)(2,1)} %collective-permute-done.6, bf16[256,256]{1,0:T(8,128)(2,1)} %copy-done.5, bf16[256,256]{1,0:T(8,128)(2,1)S(1)} %collective-permute-done.4, f32[256,1024]{1,0:T(8,128)} %param.11, s32[]{:T(128)S(6)} %select_n.33), kind=kLoop, calls=%fused_computation.12 | loop fusion | flops 393216 | bytes 917508 | tf_op jit(solution)/shard_map/add | solution.py:252
  34.8 6.6 %collective-permute-start.9 = (f32[256,128]{1,0:T(8,128)S(1)}, f32[256,128]{1,0:T(8,128)}, u32[]{:S(2)}, u32[]{:S(2)}) collective-permute-start(f32[256,128]{1,0:T(8,128)S(1)} %constant_dynamic-slice_fusion), channel_id=1, source_target_pairs={{0,32},{32,0},{64,96},{96,64},{128,160},{160,128},{192,224},{224,1... | collective-permute-start | bytes 393224 | tf_op jit(solution)/shard_map/ppermute | solution.py:25
  41.4 0.0 collective-permute-done.8.second_ref
  41.4 0.0 collective-permute-done.7.other_ref
  41.4 4.6 %hidden_grad.1 = bf16[8,128,1024]{2,1,0:T(8,128)(2,1)} custom-call(bf16[512,512]{1,0:T(8,128)(2,1)} %copy-done.1, bf16[512,512]{1,0:T(8,128)(2,1)} %collective-permute-done.7.other_ref, bf16[512,512]{1,0:T(8,128)(2,1)} %copy-done.2, bf16[512,512]{1,0:T(8,128)(2,1)} %collective-permute-done.8.second_ref), custom_call_target="tpu_custom_call" | custom-call | flops 1073741824 | bytes 4194304 | tf_op jit(solution)/shard_map/hidden_grad/pallas_call | solution.py:130
  46.1 0.0 copy-start
  46.1 5.4 %all-to-all-start = ((bf16[8,128,1024]{2,1,0:T(8,128)(2,1)}), bf16[8,128,1024]{2,1,0:T(8,128)(2,1)}, u32[]{:S(2)}, u32[]{:S(2)}) async-start(bf16[8,128,1024]{2,1,0:T(8,128)(2,1)} %hidden_grad.1), calls=%async_computation | async-start | bytes 4194304 | tf_op jit(solution)/shard_map/all_to_all | solution.py:30
  51.5 0.1 convert_divide_fusion
  51.6 1.7 %multiply_subtract_fusion = (f32[256,128]{1,0:T(8,128)}, f32[256,128]{1,0:T(8,128)}) fusion(f32[256,128]{1,0:T(8,128)S(1)} %copy-done.6, f32[256,128]{1,0:T(8,128)} %collective-permute-done.9, f32[256,256]{1,0:T(8,128)S(1)} %convert_add_fusion, s32[]{:T(128)S(6)} %select_n.38, f32[256,128]{1,0:T(8,128)} %param.13), kind=kLoop, calls=%fused_computation.17 | loop fusion | flops 262144 | bytes 786436 | tf_op jit(solution)/shard_map/sub | solution.py:266
  53.3 5.8 %weight_and_value_terms.1 = (f32[256,512]{1,0:T(8,128)}, bf16[256,512]{1,0:T(8,128)(2,1)}, bf16[256,512]{1,0:T(8,128)(2,1)}, bf16[256,512]{1,0:T(8,128)(2,1)}, f...) custom-call(bf16[512,512]{1,0:T(8,128)(2,1)} %copy-done.1, bf16[512,512]{1,0:T(8,128)(2,1)} %collective-permute-done.7.other_ref, ...), custom_call_target="tpu_custom_call" | custom-call | flops 2147483648 | bytes 6291456 | tf_op jit(solution)/shard_map/weight_and_value_terms/pallas_call | solution.py:179
  59.1 0.2 collective-permute-start.10
  59.3 1.2 %collective-permute-start.12 = (bf16[256,512]{1,0:T(8,128)(2,1)}, bf16[256,512]{1,0:T(8,128)(2,1)}, u32[]{:S(2)}, u32[]{:S(2)}) collective-permute-start(bf16[256,512]{1,0:T(8,128)(2,1)} %get-tuple-element.41), channel_id=1, source_target_pairs={{0,8},{1,9},{2,10},{3,11},{4,12},{5,13},{6,14},{7,15},{8,0},{9,1},... | collective-permute-start | bytes 786440 | tf_op jit(solution)/shard_map/ppermute | solution.py:25
  60.5 2.1 %collective-permute-start.13 = (bf16[256,512]{1,0:T(8,128)(2,1)}, bf16[256,512]{1,0:T(8,128)(2,1)}, u32[]{:S(2)}, u32[]{:S(2)}) collective-permute-start(bf16[256,512]{1,0:T(8,128)(2,1)} %get-tuple-element.42), channel_id=1, source_target_pairs={{0,16},{1,17},{2,18},{3,19},{4,20},{5,21},{6,22},{7,23},{8,24},{9,... | collective-permute-start | bytes 786440 | tf_op jit(solution)/shard_map/ppermute | solution.py:25
  62.6 0.5 collective-permute-start.14
  63.1 1.4 %add.79 = f32[4,128,512]{2,1,0:T(8,128)S(1)} add(f32[4,128,512]{2,1,0:T(8,128)} %get-tuple-element.36, f32[4,128,512]{2,1,0:T(8,128)S(1)} %collective-permute-done.10) | non-fusion elementwise | flops 262144 | bytes 3145728 | tf_op jit(solution)/shard_map/add | solution.py:302
  64.6 0.7 slice.41
  65.3 2.1 %collective-permute-start.11 = (bf16[2,128,512]{2,1,0:T(8,128)(2,1)}, bf16[2,128,512]{2,1,0:T(8,128)(2,1)}, u32[]{:S(2)}, u32[]{:S(2)}) collective-permute-start(bf16[2,128,512]{2,1,0:T(8,128)(2,1)} %slice.41), channel_id=1, source_target_pairs={{0,4},{1,5},{2,6},{3,7},{4,0},{5,1},{6,2},{7,3},{8,12},{9,13},{10,... | collective-permute-start | bytes 786440 | tf_op jit(solution)/shard_map/ppermute | solution.py:25
  67.4 10.4 %all-to-all-done.refs_0_.refs_1_.refs_2_.refs_3_ = bf16[8,128,1024]{2,1,0:T(8,128)(2,1)} async-done(((bf16[8,128,1024]{2,1,0:T(8,128)(2,1)}), bf16[8,128,1024]{2,1,0:T(8,128)(2,1)}, u32[]{:S(2)}, u32[]{:S(2)}) %all-to-all-start) | async-done | bytes 2097184 | tf_op jit(solution)/shard_map/all_to_all | solution.py:30
  77.8 5.5 %input_grad.1 = f32[128,8192]{1,0:T(8,128)} custom-call(bf16[128,8192]{1,0:T(8,128)(2,1)} %x_ref.3, f32[1,8192]{1,0:T(1,128)} %bitcast.12, f32[128,1]{1,0:T(8,128)} %get-tuple-element.39.scale_ref, bf16[8,128,1024]{2,1,0:T(8,128)(2,1)} %all-to-all-done.refs_0_.refs_1_.refs_2_.refs_3_, bf16[8,128,1024]{2,1,0:T(8,128)(2,1)} %all-to-all-done.refs_0_.refs_1_.refs_2_.refs_3_, ...), custom_call_target="tpu_custom_call" | custom-call | flops 9437184 | bytes 8388608 | tf_op jit(solution)/shard_map/input_grad/pallas_call | solution.py:229
  83.3 3.6 %collective-permute-done.14 = bf16[256,512]{1,0:T(8,128)(2,1)} collective-permute-done((bf16[256,512]{1,0:T(8,128)(2,1)}, bf16[256,512]{1,0:T(8,128)(2,1)}, u32[]{:S(2)}, u32[]{:S(2)}) %collective-permute-start.14) | collective-permute-done | bytes 262176 | tf_op jit(solution)/shard_map/ppermute | solution.py:25
  86.9 1.0 %convert_element_type.50 = f32[2,128,512]{2,1,0:T(8,128)S(1)} convert(bf16[2,128,512]{2,1,0:T(8,128)(2,1)} %collective-permute-done.11) | non-fusion elementwise | flops 131072 | bytes 786432 | tf_op jit(solution)/shard_map/convert_element_type | solution.py:307
  87.9 0.2 collective-permute-start.15
  88.2 2.8 %multiply_reduce_fusion = (f32[256]{0:T(256)}, f32[256,512]{1,0:T(8,128)}) fusion(f32[256,512]{1,0:T(8,128)S(1)} %convert_divide_fusion, bf16[256,512]{1,0:T(8,128)(2,1)} %collective-permute-done.14, bf16[256,512]{1,0:T(8,128)(2,1)} %collective-permute-done.13, f32[256,512]{1,0:T(8,128)} %get-tuple-element.46, bf16[256,512]{1,0:T(8,128)(2,1)} %collective-permute-done.12), kind=kLoop, calls=%fused_computation.3 | loop fusion | flops 1179392 | bytes 2360320 | tf_op jit(solution)/shard_map/reduce_sum | solution.py:315
  90.9 2.1 %collective-permute-done.15 = bf16[128,512]{1,0:T(8,128)(2,1)S(1)} collective-permute-done((bf16[128,512]{1,0:T(8,128)(2,1)S(1)}, bf16[128,512]{1,0:T(8,128)(2,1)S(1)}, u32[]{:S(2)}, u32[]{:S(2)}) %collective-permute-start.15) | collective-permute-done | bytes 131104 | tf_op jit(solution)/shard_map/ppermute | solution.py:25
  93.0 0.8 fusion.2
  (23 shorter events, 0.2 us)
Async XLA Ops:
  0.6 14.4 %copy-start.3 = (bf16[256,512]{1,0:T(8,128)(2,1)S(1)}, bf16[256,512]{1,0:T(8,128)(2,1)}, u32[]{:S(2)}) copy-start(bf16[256,512]{1,0:T(8,128)(2,1)} %param.9) | copy-start | bytes 786436
  0.6 13.0 %copy-start.7 = (bf16[128,512]{1,0:T(8,128)(2,1)S(1)}, bf16[128,512]{1,0:T(8,128)(2,1)}, u32[]{:S(2)}) copy-start(bf16[128,512]{1,0:T(8,128)(2,1)} %param.8) | copy-start | bytes 393220
  0.7 14.4 %collective-permute-start.3 = (bf16[256,512]{1,0:T(8,128)(2,1)}, bf16[256,512]{1,0:T(8,128)(2,1)S(1)}, u32[]{:S(2)}, u32[]{:S(2)}) collective-permute-start(bf16[256,512]{1,0:T(8,128)(2,1)} %param.9), channel_id=1, source_target_pairs={{0,16},{1,17},{2,18},{3,19},{4,20},{5,21},{6,22},{7,23},{8,24},{9,... | collective-permute-start | bytes 786440 | tf_op jit(solution)/shard_map/ppermute | solution.py:25
  4.0 8.4 %collective-permute-start = (bf16[128,512]{1,0:T(8,128)(2,1)}, bf16[128,512]{1,0:T(8,128)(2,1)S(1)}, u32[]{:S(2)}, u32[]{:S(2)}) collective-permute-start(bf16[128,512]{1,0:T(8,128)(2,1)} %param.8), channel_id=1, source_target_pairs={{0,4},{1,5},{2,6},{3,7},{4,0},{5,1},{6,2},{7,3},{8,12},{9,13},{10,... | collective-permute-start | bytes 393224 | tf_op jit(solution)/shard_map/ppermute | solution.py:25
  6.3 7.3 %collective-permute-start.1 = (bf16[128,512]{1,0:T(8,128)(2,1)}, bf16[128,512]{1,0:T(8,128)(2,1)S(1)}, u32[]{:S(2)}, u32[]{:S(2)}) collective-permute-start(bf16[128,512]{1,0:T(8,128)(2,1)} %param.8), channel_id=1, source_target_pairs={{0,2},{1,3},{2,0},{3,1},{4,6},{5,7},{6,4},{7,5},{8,10},{9,11},{10,... | collective-permute-start | bytes 393224 | tf_op jit(solution)/shard_map/ppermute | solution.py:25
  7.7 6.0 %collective-permute-start.2 = (bf16[128,512]{1,0:T(8,128)(2,1)}, bf16[128,512]{1,0:T(8,128)(2,1)S(1)}, u32[]{:S(2)}, u32[]{:S(2)}) collective-permute-start(bf16[128,512]{1,0:T(8,128)(2,1)} %param.8), channel_id=1, source_target_pairs={{0,6},{1,7},{2,4},{3,5},{4,2},{5,3},{6,0},{7,1},{8,14},{9,15},{10,... | collective-permute-start | bytes 393224 | tf_op jit(solution)/shard_map/ppermute | solution.py:25
  13.7 7.6 %copy-start.1 = (bf16[512,512]{1,0:T(8,128)(2,1)}, bf16[512,512]{1,0:T(8,128)(2,1)S(1)}, u32[]{:S(2)}) copy-start(bf16[512,512]{1,0:T(8,128)(2,1)S(1)} %pad_maximum_fusion.same_ref) | copy-start | bytes 1572868
  15.1 4.9 %copy-start.2 = (bf16[512,512]{1,0:T(8,128)(2,1)}, bf16[512,512]{1,0:T(8,128)(2,1)S(1)}, u32[]{:S(2)}) copy-start(bf16[512,512]{1,0:T(8,128)(2,1)S(1)} %pad_maximum_fusion.1.first_ref) | copy-start | bytes 1572868
  15.1 31.0 %all-to-all-start.1 = ((bf16[8,128,1024]{2,1,0:T(8,128)(2,1)}), bf16[8,128,1024]{2,1,0:T(8,128)(2,1)S(1)}, u32[]{:S(2)}, u32[]{:S(2)}) async-start(bf16[8,128,1024]{2,1,0:T(8,128)(2,1)} %get-tuple-element.33), calls=%async_computation.1 | async-start | bytes 4194304 | tf_op jit(solution)/shard_map/all_to_all | solution.py:30
  20.0 21.4 %collective-permute-start.8 = (bf16[512,512]{1,0:T(8,128)(2,1)S(1)}, bf16[512,512]{1,0:T(8,128)(2,1)}, u32[]{:S(2)}, u32[]{:S(2)}) collective-permute-start(bf16[512,512]{1,0:T(8,128)(2,1)S(1)} %pad_maximum_fusion.1.first_ref), channel_id=1, source_target_pairs={{0,8},{1,9},{2,10},{3,11},{4,12},{5,13},{6,14},{7,15},{8,0},{9,1},... | collective-permute-start | bytes 1572872 | tf_op jit(solution)/shard_map/ppermute | solution.py:25
  21.2 20.2 %collective-permute-start.7 = (bf16[512,512]{1,0:T(8,128)(2,1)S(1)}, bf16[512,512]{1,0:T(8,128)(2,1)}, u32[]{:S(2)}, u32[]{:S(2)}) collective-permute-start(bf16[512,512]{1,0:T(8,128)(2,1)S(1)} %pad_maximum_fusion.same_ref), channel_id=1, source_target_pairs={{0,1},{1,0},{2,3},{3,2},{4,5},{5,4},{6,7},{7,6},{8,9},{9,8},{10,11... | collective-permute-start | bytes 1572872 | tf_op jit(solution)/shard_map/ppermute | solution.py:25
  23.1 8.1 %collective-permute-start.4 = (bf16[256,256]{1,0:T(8,128)(2,1)}, bf16[256,256]{1,0:T(8,128)(2,1)S(1)}, u32[]{:S(2)}, u32[]{:S(2)}) collective-permute-start(bf16[256,256]{1,0:T(8,128)(2,1)} %get-tuple-element.56), channel_id=1, source_target_pairs={{0,128},{32,160},{64,192},{96,224},{128,0},{160,32},{192,64},{224,... | collective-permute-start | bytes 393224 | tf_op jit(solution)/shard_map/ppermute | solution.py:25
  23.6 9.0 %collective-permute-start.5 = (bf16[256,256]{1,0:T(8,128)(2,1)}, bf16[256,256]{1,0:T(8,128)(2,1)S(1)}, u32[]{:S(2)}, u32[]{:S(2)}) collective-permute-start(bf16[256,256]{1,0:T(8,128)(2,1)} %get-tuple-element.58), channel_id=1, source_target_pairs={{0,64},{32,96},{64,0},{96,32},{128,192},{160,224},{192,128},{224,1... | collective-permute-start | bytes 393224 | tf_op jit(solution)/shard_map/ppermute | solution.py:25
  25.7 7.9 %collective-permute-start.6 = (bf16[256,256]{1,0:T(8,128)(2,1)S(1)}, bf16[256,256]{1,0:T(8,128)(2,1)}, u32[]{:S(2)}, u32[]{:S(2)}) collective-permute-start(bf16[256,256]{1,0:T(8,128)(2,1)S(1)} %get-tuple-element.57), channel_id=1, source_target_pairs={{0,192},{32,224},{64,128},{96,160},{128,64},{160,96},{192,0},{224,... | collective-permute-start | bytes 393224 | tf_op jit(solution)/shard_map/ppermute | solution.py:25
  32.6 0.7 copy-start.5
  34.8 16.8 %collective-permute-start.9 = (f32[256,128]{1,0:T(8,128)S(1)}, f32[256,128]{1,0:T(8,128)}, u32[]{:S(2)}, u32[]{:S(2)}) collective-permute-start(f32[256,128]{1,0:T(8,128)S(1)} %constant_dynamic-slice_fusion), channel_id=1, source_target_pairs={{0,32},{32,0},{64,96},{96,64},{128,160},{160,128},{192,224},{224,1... | collective-permute-start | bytes 393224 | tf_op jit(solution)/shard_map/ppermute | solution.py:25
  46.1 5.4 %copy-start.4 = (bf16[256,512]{1,0:T(8,128)(2,1)S(1)}, bf16[256,512]{1,0:T(8,128)(2,1)}, u32[]{:S(2)}) copy-start(bf16[256,512]{1,0:T(8,128)(2,1)} %param.9) | copy-start | bytes 786436
  46.1 5.5 %copy-start.6 = (f32[256,128]{1,0:T(8,128)S(1)}, f32[256,128]{1,0:T(8,128)}, u32[]{:S(2)}) copy-start(f32[256,128]{1,0:T(8,128)} %param.12) | copy-start | bytes 393220
  46.1 5.5 %copy-start = (bf16[8,128,1024]{2,1,0:T(8,128)(2,1)}, bf16[8,128,1024]{2,1,0:T(8,128)(2,1)S(1)}, u32[]{:S(2)}) copy-start(bf16[8,128,1024]{2,1,0:T(8,128)(2,1)S(1)} %all-to-all-done.1.refs_0_.refs_1_.refs_2_.refs_3_.refs_4_.refs_5_.refs_6_.refs_7_) | copy-start | bytes 6291460
  46.1 31.7 %all-to-all-start = ((bf16[8,128,1024]{2,1,0:T(8,128)(2,1)}), bf16[8,128,1024]{2,1,0:T(8,128)(2,1)}, u32[]{:S(2)}, u32[]{:S(2)}) async-start(bf16[8,128,1024]{2,1,0:T(8,128)(2,1)} %hidden_grad.1), calls=%async_computation | async-start | bytes 4194304 | tf_op jit(solution)/shard_map/all_to_all | solution.py:30
  59.1 4.0 %collective-permute-start.10 = (f32[4,128,512]{2,1,0:T(8,128)}, f32[4,128,512]{2,1,0:T(8,128)S(1)}, u32[]{:S(2)}, u32[]{:S(2)}) collective-permute-start(f32[4,128,512]{2,1,0:T(8,128)} %get-tuple-element.37), channel_id=1, source_target_pairs={{0,1},{1,0},{2,3},{3,2},{4,5},{5,4},{6,7},{7,6},{8,9},{9,8},{10,11... | collective-permute-start | bytes 3145736 | tf_op jit(solution)/shard_map/ppermute | solution.py:25
  59.3 24.0 %collective-permute-start.12 = (bf16[256,512]{1,0:T(8,128)(2,1)}, bf16[256,512]{1,0:T(8,128)(2,1)}, u32[]{:S(2)}, u32[]{:S(2)}) collective-permute-start(bf16[256,512]{1,0:T(8,128)(2,1)} %get-tuple-element.41), channel_id=1, source_target_pairs={{0,8},{1,9},{2,10},{3,11},{4,12},{5,13},{6,14},{7,15},{8,0},{9,1},... | collective-permute-start | bytes 786440 | tf_op jit(solution)/shard_map/ppermute | solution.py:25
  60.5 22.9 %collective-permute-start.13 = (bf16[256,512]{1,0:T(8,128)(2,1)}, bf16[256,512]{1,0:T(8,128)(2,1)}, u32[]{:S(2)}, u32[]{:S(2)}) collective-permute-start(bf16[256,512]{1,0:T(8,128)(2,1)} %get-tuple-element.42), channel_id=1, source_target_pairs={{0,16},{1,17},{2,18},{3,19},{4,20},{5,21},{6,22},{7,23},{8,24},{9,... | collective-permute-start | bytes 786440 | tf_op jit(solution)/shard_map/ppermute | solution.py:25
  62.6 24.3 %collective-permute-start.14 = (bf16[256,512]{1,0:T(8,128)(2,1)}, bf16[256,512]{1,0:T(8,128)(2,1)}, u32[]{:S(2)}, u32[]{:S(2)}) collective-permute-start(bf16[256,512]{1,0:T(8,128)(2,1)} %get-tuple-element.43), channel_id=1, source_target_pairs={{0,24},{1,25},{2,26},{3,27},{4,28},{5,29},{6,30},{7,31},{8,16},{9,... | collective-permute-start | bytes 786440 | tf_op jit(solution)/shard_map/ppermute | solution.py:25
  65.3 21.6 %collective-permute-start.11 = (bf16[2,128,512]{2,1,0:T(8,128)(2,1)}, bf16[2,128,512]{2,1,0:T(8,128)(2,1)}, u32[]{:S(2)}, u32[]{:S(2)}) collective-permute-start(bf16[2,128,512]{2,1,0:T(8,128)(2,1)} %slice.41), channel_id=1, source_target_pairs={{0,4},{1,5},{2,6},{3,7},{4,0},{5,1},{6,2},{7,3},{8,12},{9,13},{10,... | collective-permute-start | bytes 786440 | tf_op jit(solution)/shard_map/ppermute | solution.py:25
  87.9 5.1 %collective-permute-start.15 = (bf16[128,512]{1,0:T(8,128)(2,1)S(1)}, bf16[128,512]{1,0:T(8,128)(2,1)S(1)}, u32[]{:S(2)}, u32[]{:S(2)}) collective-permute-start(bf16[128,512]{1,0:T(8,128)(2,1)S(1)} %fusion.3), channel_id=1, source_target_pairs={{0,2},{1,3},{2,0},{3,1},{4,6},{5,7},{6,4},{7,5},{8,10},{9,11},{10,... | collective-permute-start | bytes 393224 | tf_op jit(solution)/shard_map/ppermute | solution.py:25

commit v5 on v4

--- a/solution.py
+++ b/solution.py
@@ -38,8 +38,8 @@
     return pl.CostEstimate(flops=flops, bytes_accessed=bytes_accessed, transcendentals=0)
 
 
-def roomy():
-    return pltpu.CompilerParams(vmem_limit_bytes=62 * 2**20)
+def roomy(mib=62):
+    return pltpu.CompilerParams(vmem_limit_bytes=mib * 2**20)
 
 
 def feature_start(member, dz, rows):
@@ -199,48 +199,84 @@
     )(same, other, first, second, *[hidden] * PLANE)
 
 
-def input_grad_kernel(x_ref, gain_ref, scale_ref, *refs):
-    grads, out_ref = refs[:NY], refs[NY]
-    width = x_ref.shape[1]
+def input_grad_kernel(
+    x_ref, gain_ref, scale_ref, grad_hbm, out_hbm, grad_ref, out_ref, grad_sems, out_sems
+):
+    tokens, width = x_ref.shape
     rows = width // (NZ * PLANE)
-    scale = scale_ref[...]
-    total = jnp.zeros((x_ref.shape[0], rows), F32)
-    for dz in range(NZ):
-        for member in range(PLANE):
-            at = pl.ds(feature_start(member, dz, rows), rows)
-            grad = grads[member // NC][member % NC, :, dz * rows : (dz + 1) * rows]
-            scaled = grad.astype(F32) * gain_ref[:, at]
-            out_ref[:, at] = scaled
-            total += scaled * x_ref[:, at].astype(F32)
-    mean = scale * jnp.sum(total, axis=-1, keepdims=True) * (1.0 / width)
-    factor = scale * scale * mean
-    for block in range(NZ * PLANE):
-        at = slice(block * rows, (block + 1) * rows)
-        out_ref[:, at] = scale * out_ref[:, at] - x_ref[:, at].astype(F32) * factor
+    steps = grad_sems.shape[0]
+    step = tokens // steps
+    tile = step // out_sems.shape[1]
+    half = PLANE // 2
+
+    def fetches(i):
+        at = pl.ds(i * step, step)
+        copies = []
+        for part in range(2):
+            members = pl.ds(part * half, half)
+            copies.append(
+                pltpu.make_async_copy(
+                    grad_hbm.at[members, at], grad_ref.at[members, at], grad_sems.at[i, part]
+                )
+            )
+        return copies
+
+    def stores(i):
+        copies = []
+        for part in range(step // tile):
+            at = pl.ds(i * step + part * tile, tile)
+            copies.append(
+                pltpu.make_async_copy(out_ref.at[at], out_hbm.at[at], out_sems.at[i, part])
+            )
+        return copies
+
+    for i in range(steps):
+        for copy in fetches(i):
+            copy.start()
+    for i in range(steps):
+        for copy in fetches(i):
+            copy.wait()
+        here = slice(i * step, (i + 1) * step)
+        scale = scale_ref[here]
+        total = jnp.zeros((step, rows), F32)
+        for dz in range(NZ):
+            for member in range(PLANE):
+                at = pl.ds(feature_start(member, dz, rows), rows)
+                grad = grad_ref[member, here, dz * rows : (dz + 1) * rows]
+                scaled = grad.astype(F32) * gain_ref[:, at]
+                out_ref[here, at] = scaled
+                total += scaled * x_ref[here, at].astype(F32)
+        mean = scale * jnp.sum(total, axis=-1, keepdims=True) * (1.0 / width)
+        factor = scale * scale * mean
+        for block in range(NZ * PLANE):
+            at = slice(block * rows, (block + 1) * rows)
+            out_ref[here, at] = scale * out_ref[here, at] - x_ref[here, at].astype(F32) * factor
+        for copy in stores(i):
+            copy.start()
+    for i in range(steps):
+        for copy in stores(i):
+            copy.wait()
 
 
 def make_input_grad(inputs, gain, scale, grads):
     tokens, width = inputs.shape
-    step = 32
-    block = width // PLANE
-    members = [
-        pl.BlockSpec((NC, step, block), lambda i, pair=pair: (pair, i, 0)) for pair in range(NY)
-    ]
+    steps = 4
+    hbm, vmem = pl.BlockSpec(memory_space=pltpu.HBM), pl.BlockSpec(memory_space=pltpu.VMEM)
     return pl.pallas_call(
         input_grad_kernel,
-        grid=(tokens // step,),
-        in_specs=[
-            pl.BlockSpec((step, width), lambda i: (i, 0)),
-            pl.BlockSpec((1, width), lambda i: (0, 0)),
-            pl.BlockSpec((step, 1), lambda i: (i, 0)),
-        ]
-        + members,
-        out_specs=pl.BlockSpec((step, width), lambda i: (i, 0)),
+        in_specs=[vmem, vmem, vmem, hbm],
+        out_specs=hbm,
         out_shape=jax.ShapeDtypeStruct((tokens, width), F32),
-        compiler_params=roomy(),
+        scratch_shapes=[
+            pltpu.VMEM(grads.shape, grads.dtype),
+            pltpu.VMEM((tokens, width), F32),
+            pltpu.SemaphoreType.DMA((steps, 2)),
+            pltpu.SemaphoreType.DMA((steps, 4)),
+        ],
+        compiler_params=roomy(24),
         cost_estimate=cost(9 * tokens * width, 8 * tokens * width),
         name="input_grad",
-    )(inputs, gain, scale, *[grads] * NY)
+    )(inputs, gain, scale, grads)
 
 
 def sum_over_x(delta):
@@ -300,13 +336,13 @@
     *terms, keep, give = make_terms(same, other, first, second, hidden)
     got = [swap(terms[dz], "fsdp", dz * PLANE) for dz in (1, 2, 3)]
     (pair,) = together(keep + swap(give, "fsdp", 1))
-    back, own = together(back, pair[0])
-    far = swap(pair[2:].astype(BF16), "fsdp", 2 * NC)
+    back, values = together(back, pair[0])
+    parts = [swap(pair[dy].astype(BF16), "fsdp", dy * NC) for dy in (1, 2, 3)]
     input_grad = make_input_grad(inputs, gain, scale, back)
-    input_grad, far, *got = together(input_grad, far, *got)
-    far = far.astype(F32)
-    near = swap((pair[1] + far[1]).astype(BF16), "fsdp", NC).astype(F32)
-    values = own + far[0] + near
+    input_grad, *got = together(input_grad, *got)
+    input_grad, *parts = together(input_grad, *parts)
+    for part in parts:
+        values = values + part.astype(F32)
     weight_sum = terms[0]
     for part in got:
         weight_sum = weight_sum + part.astype(F32)

time: 94.3 us -> 92.8 us (0.984)
  the two profiles are of different devices: /device:TPU:44 before, /device:TPU:2 now
where the time goes in v5:
time: 92.8 us; the launch traced here: 92.2 us
  starting transfers between devices  37.6 us (41%)
  waiting for transfers between devices  23.7 us (26%)
  Pallas kernels  18.8 us (20%)
  other arithmetic  7.97 us (9%)
  local copies, waits for them, and re-layouts  3.37 us (4%)
    ppermute x17, starting transfers between devices, swap(): lax.ppermute(array, axis, [(source, source ^ bits) for source in range(si...  29 us
    all_to_all x2, waiting for transfers between devices, exchange_plane(): return lax.all_to_all(array, 'fsdp', 0, 0, axis_index_groups=planes)  14.2 us
    ppermute x17, waiting for transfers between devices, swap(): lax.ppermute(array, axis, [(source, source ^ bits) for source in range(si...  9.46 us
    all_to_all x2, starting transfers between devices, exchange_plane(): return lax.all_to_all(array, 'fsdp', 0, 0, axis_index_groups=planes)  8.57 us
    pallas_call x1, Pallas kernels, make_terms(): pl.pallas_call(terms_kernel, grid=(1,), in_specs=[cots, cots, weight, wei...  5.81 us
    pallas_call x1, Pallas kernels, make_hidden_grad(): pl.pallas_call(hidden_grad_kernel, grid=(NZ,), in_specs=[cots, cots, weig...  4.65 us
    pallas_call x1, Pallas kernels, make_hidden(): pl.pallas_call(norm_kernel, grid=(tokens // step,), in_specs=[pl.BlockSpe...  4.28 us
    pallas_call x1, Pallas kernels, make_input_grad(): pl.pallas_call(input_grad_kernel, in_specs=[vmem, vmem, vmem, hbm], out_s...  4.03 us
  transfers between devices with their start and end apart: 19, of which 7 were waited for; matrix products, arithmetic and copies ran while one was open for 11% of the time, Pallas kernels for 20%

profile of v5, /device:TPU:2, one launch (start us, length us, event | category | flops | bytes accessed | tf_op | source)
XLA Modules:
  0.0 92.2 jit_solution(15768203231812437491)
XLA Ops:
  0.6 0.0 copy-start.6
  0.7 3.4 %collective-permute-start.3 = (bf16[256,512]{1,0:T(8,128)(2,1)}, bf16[256,512]{1,0:T(8,128)(2,1)S(1)}, u32[]{:S(2)}, u32[]{:S(2)}) collective-permute-start(bf16[256,512]{1,0:T(8,128)(2,1)} %param.9), channel_id=1, source_target_pairs={{0,16},{1,17},{2,18},{3,19},{4,20},{5,21},{6,22},{7,23},{8,24},{9,... | collective-permute-start | bytes 786440 | tf_op jit(solution)/shard_map/ppermute | solution.py:25
  4.0 1.6 %collective-permute-start.1 = (bf16[128,512]{1,0:T(8,128)(2,1)}, bf16[128,512]{1,0:T(8,128)(2,1)S(1)}, u32[]{:S(2)}, u32[]{:S(2)}) collective-permute-start(bf16[128,512]{1,0:T(8,128)(2,1)} %param.8), channel_id=1, source_target_pairs={{0,2},{1,3},{2,0},{3,1},{4,6},{5,7},{6,4},{7,5},{8,10},{9,11},{10,... | collective-permute-start | bytes 393224 | tf_op jit(solution)/shard_map/ppermute | solution.py:25
  5.6 2.9 %collective-permute-start = (bf16[128,512]{1,0:T(8,128)(2,1)}, bf16[128,512]{1,0:T(8,128)(2,1)S(1)}, u32[]{:S(2)}, u32[]{:S(2)}) collective-permute-start(bf16[128,512]{1,0:T(8,128)(2,1)} %param.8), channel_id=1, source_target_pairs={{0,4},{1,5},{2,6},{3,7},{4,0},{5,1},{6,2},{7,3},{8,12},{9,13},{10,... | collective-permute-start | bytes 393224 | tf_op jit(solution)/shard_map/ppermute | solution.py:25
  8.5 0.2 collective-permute-start.2
  8.7 4.3 %norm.1 = (f32[128,1]{1,0:T(8,128)}, bf16[8,128,1024]{2,1,0:T(8,128)(2,1)}) custom-call(bf16[128,8192]{1,0:T(8,128)(2,1)} %x_ref.3, f32[1,8192]{1,0:T(1,128)} %bitcast.9), custom_call_target="tpu_custom_call" | custom-call | flops 6291456 | bytes 4194304 | tf_op jit(solution)/shard_map/norm/pallas_call | solution.py:68
  13.0 0.0 collective-permute-done.1
  13.0 1.5 %collective-permute-done = bf16[128,512]{1,0:T(8,128)(2,1)S(1)} collective-permute-done((bf16[128,512]{1,0:T(8,128)(2,1)}, bf16[128,512]{1,0:T(8,128)(2,1)S(1)}, u32[]{:S(2)}, u32[]{:S(2)}) %collective-permute-start) | collective-permute-done | bytes 131104 | tf_op jit(solution)/shard_map/ppermute | solution.py:25
  14.5 1.9 %collective-permute-done.2 = bf16[128,512]{1,0:T(8,128)(2,1)S(1)} collective-permute-done((bf16[128,512]{1,0:T(8,128)(2,1)}, bf16[128,512]{1,0:T(8,128)(2,1)S(1)}, u32[]{:S(2)}, u32[]{:S(2)}) %collective-permute-start.2) | collective-permute-done | bytes 131104 | tf_op jit(solution)/shard_map/ppermute | solution.py:25
  16.5 0.0 copy-start.4
  16.6 0.0 copy-start.1
  16.6 4.2 %all-to-all-start.1 = ((bf16[8,128,1024]{2,1,0:T(8,128)(2,1)}), bf16[8,128,1024]{2,1,0:T(8,128)(2,1)S(1)}, u32[]{:S(2)}, u32[]{:S(2)}) async-start(bf16[8,128,1024]{2,1,0:T(8,128)(2,1)} %get-tuple-element.36), calls=%async_computation.1 | async-start | bytes 4194304 | tf_op jit(solution)/shard_map/all_to_all | solution.py:30
  20.8 0.5 collective-permute-start.7
  21.3 1.3 %collective-permute-start.8 = (bf16[512,512]{1,0:T(8,128)(2,1)S(1)}, bf16[512,512]{1,0:T(8,128)(2,1)}, u32[]{:S(2)}, u32[]{:S(2)}) collective-permute-start(bf16[512,512]{1,0:T(8,128)(2,1)S(1)} %pad_maximum_fusion.1.first_ref), channel_id=1, source_target_pairs={{0,8},{1,9},{2,10},{3,11},{4,12},{5,13},{6,14},{7,15},{8,0},{9,1},... | collective-permute-start | bytes 1572872 | tf_op jit(solution)/shard_map/ppermute | solution.py:25
  22.7 1.9 %dynamic-slice_convert_fusion.2 = (bf16[256,256]{1,0:T(8,128)(2,1)}, bf16[256,256]{1,0:T(8,128)(2,1)}, bf16[256,256]{1,0:T(8,128)(2,1)}) fusion(f32[256,1024]{1,0:T(8,128)} %param.11, s32[]{:T(128)S(6)} %select_n.34, s32[]{:T(128)S(6)} %select_n.36, s32[]{:T(128)S(6)} %select_n.35), kind=kLoop, calls=%fused_computation.10 | loop fusion | bytes 786444 | tf_op jit(solution)/shard_map/convert_element_type | solution.py:288
  24.5 2.1 %collective-permute-start.4 = (bf16[256,256]{1,0:T(8,128)(2,1)}, bf16[256,256]{1,0:T(8,128)(2,1)S(1)}, u32[]{:S(2)}, u32[]{:S(2)}) collective-permute-start(bf16[256,256]{1,0:T(8,128)(2,1)} %get-tuple-element.62), channel_id=1, source_target_pairs={{0,128},{32,160},{64,192},{96,224},{128,0},{160,32},{192,64},{224,... | collective-permute-start | bytes 393224 | tf_op jit(solution)/shard_map/ppermute | solution.py:25
  26.7 2.6 %collective-permute-start.5 = (bf16[256,256]{1,0:T(8,128)(2,1)}, bf16[256,256]{1,0:T(8,128)(2,1)}, u32[]{:S(2)}, u32[]{:S(2)}) collective-permute-start(bf16[256,256]{1,0:T(8,128)(2,1)} %get-tuple-element.64), channel_id=1, source_target_pairs={{0,64},{32,96},{64,0},{96,32},{128,192},{160,224},{192,128},{224,1... | collective-permute-start | bytes 393224 | tf_op jit(solution)/shard_map/ppermute | solution.py:25
  29.2 0.1 dynamic_slice.27
  29.3 3.3 %collective-permute-done.4 = bf16[256,256]{1,0:T(8,128)(2,1)S(1)} collective-permute-done((bf16[256,256]{1,0:T(8,128)(2,1)}, bf16[256,256]{1,0:T(8,128)(2,1)S(1)}, u32[]{:S(2)}, u32[]{:S(2)}) %collective-permute-start.4) | collective-permute-done | bytes 131104 | tf_op jit(solution)/shard_map/ppermute | solution.py:25
  32.6 1.8 %collective-permute-done.6 = bf16[256,256]{1,0:T(8,128)(2,1)S(1)} collective-permute-done((bf16[256,256]{1,0:T(8,128)(2,1)}, bf16[256,256]{1,0:T(8,128)(2,1)S(1)}, u32[]{:S(2)}, u32[]{:S(2)}) %collective-permute-start.6) | collective-permute-done | bytes 131104 | tf_op jit(solution)/shard_map/ppermute | solution.py:25
  34.4 0.7 copy-done.10
  35.1 1.2 %convert_add_fusion.1 = f32[256,256]{1,0:T(8,128)S(1)} fusion(bf16[256,256]{1,0:T(8,128)(2,1)} %copy-done.10, bf16[256,256]{1,0:T(8,128)(2,1)} %collective-permute-done.5, bf16[256,256]{1,0:T(8,128)(2,1)} %copy-done.9, f32[256,1024]{1,0:T(8,128)} %param.11, s32[]{:T(128)S(6)} %select_n.33), kind=kLoop, calls=%fused_computation.7 | loop fusion | flops 393216 | bytes 917508 | tf_op jit(solution)/shard_map/add | solution.py:288
  36.3 0.7 constant_dynamic-slice_fusion
  37.0 5.4 %collective-permute-start.9 = (f32[256,128]{1,0:T(8,128)}, f32[256,128]{1,0:T(8,128)}, u32[]{:S(2)}, u32[]{:S(2)}) collective-permute-start(f32[256,128]{1,0:T(8,128)} %constant_dynamic-slice_fusion), channel_id=1, source_target_pairs={{0,32},{32,0},{64,96},{96,64},{128,160},{160,128},{192,224},{224,1... | collective-permute-start | bytes 393224 | tf_op jit(solution)/shard_map/ppermute | solution.py:25
  42.4 0.0 collective-permute-done.8.second_ref
  42.4 4.7 %hidden_grad.1 = bf16[8,128,1024]{2,1,0:T(8,128)(2,1)} custom-call(bf16[512,512]{1,0:T(8,128)(2,1)} %copy-done.4, bf16[512,512]{1,0:T(8,128)(2,1)} %collective-permute-done.7.other_ref, bf16[512,512]{1,0:T(8,128)(2,1)} %copy-done.5, bf16[512,512]{1,0:T(8,128)(2,1)} %collective-permute-done.8.second_ref), custom_call_target="tpu_custom_call" | custom-call | flops 1073741824 | bytes 4194304 | tf_op jit(solution)/shard_map/hidden_grad/pallas_call | solution.py:130
  47.0 1.0 %all-to-all-done.1.refs_0_.refs_1_.refs_2_.refs_3_.refs_4_.refs_5_.refs_6_.refs_7_ = bf16[8,128,1024]{2,1,0:T(8,128)(2,1)S(1)} async-done(((bf16[8,128,1024]{2,1,0:T(8,128)(2,1)}), bf16[8,128,1024]{2,1,0:T(8,128)(2,1)S(1)}, u32[]{:S(2)}, u32[]{:S(2)}) %all-to-all-start.1) | async-done | bytes 2097184 | tf_op jit(solution)/shard_map/all_to_all | solution.py:30
  48.0 4.3 %all-to-all-start = ((bf16[8,128,1024]{2,1,0:T(8,128)(2,1)}), bf16[8,128,1024]{2,1,0:T(8,128)(2,1)}, u32[]{:S(2)}, u32[]{:S(2)}) async-start(bf16[8,128,1024]{2,1,0:T(8,128)(2,1)} %hidden_grad.1), calls=%async_computation | async-start | bytes 4194304 | tf_op jit(solution)/shard_map/all_to_all | solution.py:30
  52.4 0.1 convert_divide_fusion
  52.5 1.7 %multiply_subtract_fusion = (f32[256,128]{1,0:T(8,128)}, f32[256,128]{1,0:T(8,128)}) fusion(f32[256,128]{1,0:T(8,128)S(1)} %copy-done.11, f32[256,128]{1,0:T(8,128)} %collective-permute-done.9, f32[256,256]{1,0:T(8,128)S(1)} %convert_add_fusion.1, s32[]{:T(128)S(6)} %select_n.38, f32[256,128]{1,0:T(8,128)} %param.13), kind=kLoop, calls=%fused_computation.14 | loop fusion | flops 262144 | bytes 786436 | tf_op jit(solution)/shard_map/sub | solution.py:302
  54.2 5.8 %weight_and_value_terms.1 = (f32[256,512]{1,0:T(8,128)}, bf16[256,512]{1,0:T(8,128)(2,1)}, bf16[256,512]{1,0:T(8,128)(2,1)}, bf16[256,512]{1,0:T(8,128)(2,1)}, f...) custom-call(bf16[512,512]{1,0:T(8,128)(2,1)} %copy-done.4, bf16[512,512]{1,0:T(8,128)(2,1)} %collective-permute-done.7.other_ref, ...), custom_call_target="tpu_custom_call" | custom-call | flops 2147483648 | bytes 6291456 | tf_op jit(solution)/shard_map/weight_and_value_terms/pallas_call | solution.py:179
  60.1 0.4 collective-permute-start.10
  60.4 1.3 %collective-permute-start.11 = (bf16[256,512]{1,0:T(8,128)(2,1)}, bf16[256,512]{1,0:T(8,128)(2,1)}, u32[]{:S(2)}, u32[]{:S(2)}) collective-permute-start(bf16[256,512]{1,0:T(8,128)(2,1)} %get-tuple-element.44), channel_id=1, source_target_pairs={{0,8},{1,9},{2,10},{3,11},{4,12},{5,13},{6,14},{7,15},{8,0},{9,1},... | collective-permute-start | bytes 786440 | tf_op jit(solution)/shard_map/ppermute | solution.py:25
  61.8 2.8 %collective-permute-start.12 = (bf16[256,512]{1,0:T(8,128)(2,1)}, bf16[256,512]{1,0:T(8,128)(2,1)}, u32[]{:S(2)}, u32[]{:S(2)}) collective-permute-start(bf16[256,512]{1,0:T(8,128)(2,1)} %get-tuple-element.45), channel_id=1, source_target_pairs={{0,16},{1,17},{2,18},{3,19},{4,20},{5,21},{6,22},{7,23},{8,24},{9,... | collective-permute-start | bytes 786440 | tf_op jit(solution)/shard_map/ppermute | solution.py:25
  64.5 0.3 collective-permute-start.13
  64.8 0.0 collective-permute-done.10
  64.8 1.4 %add.78 = f32[4,128,512]{2,1,0:T(8,128)S(1)} add(f32[4,128,512]{2,1,0:T(8,128)} %get-tuple-element.39, f32[4,128,512]{2,1,0:T(8,128)S(1)} %collective-permute-done.10) | non-fusion elementwise | flops 262144 | bytes 3145728 | tf_op jit(solution)/shard_map/add | solution.py:338
  66.2 0.0 copy-start
  66.3 0.1 convert.5
  66.4 13.2 %all-to-all-done.grad_hbm = bf16[8,128,1024]{2,1,0:T(8,128)(2,1)} async-done(((bf16[8,128,1024]{2,1,0:T(8,128)(2,1)}), bf16[8,128,1024]{2,1,0:T(8,128)(2,1)}, u32[]{:S(2)}, u32[]{:S(2)}) %all-to-all-start) | async-done | bytes 2097184 | tf_op jit(solution)/shard_map/all_to_all | solution.py:30
  79.6 1.2 %collective-permute-start.16 = (bf16[128,512]{1,0:T(8,128)(2,1)S(1)}, bf16[128,512]{1,0:T(8,128)(2,1)S(1)}, u32[]{:S(2)}, u32[]{:S(2)}) collective-permute-start(bf16[128,512]{1,0:T(8,128)(2,1)S(1)} %get-tuple-element.65), channel_id=1, source_target_pairs={{0,6},{1,7},{2,4},{3,5},{4,2},{5,3},{6,0},{7,1},{8,14},{9,15},{10,... | collective-permute-start | bytes 393224 | tf_op jit(solution)/shard_map/ppermute | solution.py:25
  80.8 1.5 %collective-permute-start.15 = (bf16[128,512]{1,0:T(8,128)(2,1)S(1)}, bf16[128,512]{1,0:T(8,128)(2,1)S(1)}, u32[]{:S(2)}, u32[]{:S(2)}) collective-permute-start(bf16[128,512]{1,0:T(8,128)(2,1)S(1)} %get-tuple-element.66), channel_id=1, source_target_pairs={{0,4},{1,5},{2,6},{3,7},{4,0},{5,1},{6,2},{7,3},{8,12},{9,13},{10,... | collective-permute-start | bytes 393224 | tf_op jit(solution)/shard_map/ppermute | solution.py:25
  82.3 4.0 %input_grad.1 = f32[128,8192]{1,0:T(8,128)} custom-call(bf16[128,8192]{1,0:T(8,128)(2,1)S(1)} %copy-done, f32[1,8192]{1,0:T(1,128)S(1)} %bitcast.10, f32[128,1]{1,0:T(8,128)S(1)} %copy-done.2, bf16[8,128,1024]{2,1,0:T(8,128)(2,1)} %all-to-all-done.grad_hbm), custom_call_target="tpu_custom_call" | custom-call | flops 9437184 | bytes 8388608 | tf_op jit(solution)/shard_map/input_grad/pallas_call | solution.py:265
  86.4 0.0 collective-permute-done.11
  86.4 1.5 %collective-permute-start.14 = (bf16[128,512]{1,0:T(8,128)(2,1)S(1)}, bf16[128,512]{1,0:T(8,128)(2,1)S(1)}, u32[]{:S(2)}, u32[]{:S(2)}) collective-permute-start(bf16[128,512]{1,0:T(8,128)(2,1)S(1)} %get-tuple-element.67), channel_id=1, source_target_pairs={{0,2},{1,3},{2,0},{3,1},{4,6},{5,7},{6,4},{7,5},{8,10},{9,11},{10,... | collective-permute-start | bytes 393224 | tf_op jit(solution)/shard_map/ppermute | solution.py:25
  87.9 2.6 %multiply_reduce_fusion = (f32[256]{0:T(256)}, f32[256,512]{1,0:T(8,128)}) fusion(f32[256,512]{1,0:T(8,128)S(1)} %convert_divide_fusion, bf16[256,512]{1,0:T(8,128)(2,1)} %collective-permute-done.13, bf16[256,512]{1,0:T(8,128)(2,1)} %collective-permute-done.12, f32[256,512]{1,0:T(8,128)S(1)} %copy-done.8, bf16[256,512]{1,0:T(8,128)(2,1)} %collective-permute-done.11), kind=kLoop, calls=%fused_computation.2 | loop fusion | flops 1179392 | bytes 2360320 | tf_op jit(solution)/shard_map/reduce_sum | solution.py:351
  90.6 0.9 collective-permute-done.14
  91.4 0.8 convert_add_fusion
  (34 shorter events, 0.2 us)
Async XLA Ops:
  0.6 15.9 %copy-start.6 = (bf16[256,512]{1,0:T(8,128)(2,1)S(1)}, bf16[256,512]{1,0:T(8,128)(2,1)}, u32[]{:S(2)}) copy-start(bf16[256,512]{1,0:T(8,128)(2,1)} %param.9) | copy-start | bytes 786436
  0.6 15.8 %copy-start.12 = (bf16[128,512]{1,0:T(8,128)(2,1)S(1)}, bf16[128,512]{1,0:T(8,128)(2,1)}, u32[]{:S(2)}) copy-start(bf16[128,512]{1,0:T(8,128)(2,1)} %param.8) | copy-start | bytes 393220
  0.7 15.8 %collective-permute-start.3 = (bf16[256,512]{1,0:T(8,128)(2,1)}, bf16[256,512]{1,0:T(8,128)(2,1)S(1)}, u32[]{:S(2)}, u32[]{:S(2)}) collective-permute-start(bf16[256,512]{1,0:T(8,128)(2,1)} %param.9), channel_id=1, source_target_pairs={{0,16},{1,17},{2,18},{3,19},{4,20},{5,21},{6,22},{7,23},{8,24},{9,... | collective-permute-start | bytes 786440 | tf_op jit(solution)/shard_map/ppermute | solution.py:25
  4.0 9.0 %collective-permute-start.1 = (bf16[128,512]{1,0:T(8,128)(2,1)}, bf16[128,512]{1,0:T(8,128)(2,1)S(1)}, u32[]{:S(2)}, u32[]{:S(2)}) collective-permute-start(bf16[128,512]{1,0:T(8,128)(2,1)} %param.8), channel_id=1, source_target_pairs={{0,2},{1,3},{2,0},{3,1},{4,6},{5,7},{6,4},{7,5},{8,10},{9,11},{10,... | collective-permute-start | bytes 393224 | tf_op jit(solution)/shard_map/ppermute | solution.py:25
  5.6 9.0 %collective-permute-start = (bf16[128,512]{1,0:T(8,128)(2,1)}, bf16[128,512]{1,0:T(8,128)(2,1)S(1)}, u32[]{:S(2)}, u32[]{:S(2)}) collective-permute-start(bf16[128,512]{1,0:T(8,128)(2,1)} %param.8), channel_id=1, source_target_pairs={{0,4},{1,5},{2,6},{3,7},{4,0},{5,1},{6,2},{7,3},{8,12},{9,13},{10,... | collective-permute-start | bytes 393224 | tf_op jit(solution)/shard_map/ppermute | solution.py:25
  8.5 8.0 %collective-permute-start.2 = (bf16[128,512]{1,0:T(8,128)(2,1)}, bf16[128,512]{1,0:T(8,128)(2,1)S(1)}, u32[]{:S(2)}, u32[]{:S(2)}) collective-permute-start(bf16[128,512]{1,0:T(8,128)(2,1)} %param.8), channel_id=1, source_target_pairs={{0,6},{1,7},{2,4},{3,5},{4,2},{5,3},{6,0},{7,1},{8,14},{9,15},{10,... | collective-permute-start | bytes 393224 | tf_op jit(solution)/shard_map/ppermute | solution.py:25
  16.5 4.3 %copy-start.4 = (bf16[512,512]{1,0:T(8,128)(2,1)}, bf16[512,512]{1,0:T(8,128)(2,1)S(1)}, u32[]{:S(2)}) copy-start(bf16[512,512]{1,0:T(8,128)(2,1)S(1)} %pad_maximum_fusion.same_ref) | copy-start | bytes 1572868
  16.6 4.8 %copy-start.5 = (bf16[512,512]{1,0:T(8,128)(2,1)}, bf16[512,512]{1,0:T(8,128)(2,1)S(1)}, u32[]{:S(2)}) copy-start(bf16[512,512]{1,0:T(8,128)(2,1)S(1)} %pad_maximum_fusion.1.first_ref) | copy-start | bytes 1572868
  16.6 12.7 %copy-start.1 = (f32[8192]{0:T(1024)S(1)}, f32[8192]{0:T(1024)}, u32[]{:S(2)}) copy-start(f32[8192]{0:T(1024)} %param.10) | copy-start | bytes 98308
  16.6 31.4 %all-to-all-start.1 = ((bf16[8,128,1024]{2,1,0:T(8,128)(2,1)}), bf16[8,128,1024]{2,1,0:T(8,128)(2,1)S(1)}, u32[]{:S(2)}, u32[]{:S(2)}) async-start(bf16[8,128,1024]{2,1,0:T(8,128)(2,1)} %get-tuple-element.36), calls=%async_computation.1 | async-start | bytes 4194304 | tf_op jit(solution)/shard_map/all_to_all | solution.py:30
  20.8 21.5 %collective-permute-start.7 = (bf16[512,512]{1,0:T(8,128)(2,1)S(1)}, bf16[512,512]{1,0:T(8,128)(2,1)}, u32[]{:S(2)}, u32[]{:S(2)}) collective-permute-start(bf16[512,512]{1,0:T(8,128)(2,1)S(1)} %pad_maximum_fusion.same_ref), channel_id=1, source_target_pairs={{0,1},{1,0},{2,3},{3,2},{4,5},{5,4},{6,7},{7,6},{8,9},{9,8},{10,11... | collective-permute-start | bytes 1572872 | tf_op jit(solution)/shard_map/ppermute | solution.py:25
  21.3 21.0 %collective-permute-start.8 = (bf16[512,512]{1,0:T(8,128)(2,1)S(1)}, bf16[512,512]{1,0:T(8,128)(2,1)}, u32[]{:S(2)}, u32[]{:S(2)}) collective-permute-start(bf16[512,512]{1,0:T(8,128)(2,1)S(1)} %pad_maximum_fusion.1.first_ref), channel_id=1, source_target_pairs={{0,8},{1,9},{2,10},{3,11},{4,12},{5,13},{6,14},{7,15},{8,0},{9,1},... | collective-permute-start | bytes 1572872 | tf_op jit(solution)/shard_map/ppermute | solution.py:25
  24.5 8.1 %collective-permute-start.4 = (bf16[256,256]{1,0:T(8,128)(2,1)}, bf16[256,256]{1,0:T(8,128)(2,1)S(1)}, u32[]{:S(2)}, u32[]{:S(2)}) collective-permute-start(bf16[256,256]{1,0:T(8,128)(2,1)} %get-tuple-element.62), channel_id=1, source_target_pairs={{0,128},{32,160},{64,192},{96,224},{128,0},{160,32},{192,64},{224,... | collective-permute-start | bytes 393224 | tf_op jit(solution)/shard_map/ppermute | solution.py:25
  26.7 7.8 %collective-permute-start.6 = (bf16[256,256]{1,0:T(8,128)(2,1)}, bf16[256,256]{1,0:T(8,128)(2,1)S(1)}, u32[]{:S(2)}, u32[]{:S(2)}) collective-permute-start(bf16[256,256]{1,0:T(8,128)(2,1)} %get-tuple-element.63), channel_id=1, source_target_pairs={{0,192},{32,224},{64,128},{96,160},{128,64},{160,96},{192,0},{224,... | collective-permute-start | bytes 393224 | tf_op jit(solution)/shard_map/ppermute | solution.py:25
  26.7 8.4 %collective-permute-start.5 = (bf16[256,256]{1,0:T(8,128)(2,1)}, bf16[256,256]{1,0:T(8,128)(2,1)}, u32[]{:S(2)}, u32[]{:S(2)}) collective-permute-start(bf16[256,256]{1,0:T(8,128)(2,1)} %get-tuple-element.64), channel_id=1, source_target_pairs={{0,64},{32,96},{64,0},{96,32},{128,192},{160,224},{192,128},{224,1... | collective-permute-start | bytes 393224 | tf_op jit(solution)/shard_map/ppermute | solution.py:25
  32.6 1.8 %copy-start.9 = (bf16[256,256]{1,0:T(8,128)(2,1)}, bf16[256,256]{1,0:T(8,128)(2,1)S(1)}, u32[]{:S(2)}) copy-start(bf16[256,256]{1,0:T(8,128)(2,1)S(1)} %collective-permute-done.4) | copy-start | bytes 393220
  34.4 0.7 copy-start.10
  37.0 15.6 %collective-permute-start.9 = (f32[256,128]{1,0:T(8,128)}, f32[256,128]{1,0:T(8,128)}, u32[]{:S(2)}, u32[]{:S(2)}) collective-permute-start(f32[256,128]{1,0:T(8,128)} %constant_dynamic-slice_fusion), channel_id=1, source_target_pairs={{0,32},{32,0},{64,96},{96,64},{128,160},{160,128},{192,224},{224,1... | collective-permute-start | bytes 393224 | tf_op jit(solution)/shard_map/ppermute | solution.py:25
  47.0 5.4 %copy-start.7 = (bf16[256,512]{1,0:T(8,128)(2,1)S(1)}, bf16[256,512]{1,0:T(8,128)(2,1)}, u32[]{:S(2)}) copy-start(bf16[256,512]{1,0:T(8,128)(2,1)} %param.9) | copy-start | bytes 786436
  47.0 5.5 %copy-start.11 = (f32[256,128]{1,0:T(8,128)S(1)}, f32[256,128]{1,0:T(8,128)}, u32[]{:S(2)}) copy-start(f32[256,128]{1,0:T(8,128)} %param.12) | copy-start | bytes 393220
  48.0 4.5 %copy-start.3 = (bf16[8,128,1024]{2,1,0:T(8,128)(2,1)}, bf16[8,128,1024]{2,1,0:T(8,128)(2,1)S(1)}, u32[]{:S(2)}) copy-start(bf16[8,128,1024]{2,1,0:T(8,128)(2,1)S(1)} %all-to-all-done.1.refs_0_.refs_1_.refs_2_.refs_3_.refs_4_.refs_5_.refs_6_.refs_7_) | copy-start | bytes 6291460
  48.0 31.5 %all-to-all-start = ((bf16[8,128,1024]{2,1,0:T(8,128)(2,1)}), bf16[8,128,1024]{2,1,0:T(8,128)(2,1)}, u32[]{:S(2)}, u32[]{:S(2)}) async-start(bf16[8,128,1024]{2,1,0:T(8,128)(2,1)} %hidden_grad.1), calls=%async_computation | async-start | bytes 4194304 | tf_op jit(solution)/shard_map/all_to_all | solution.py:30
  60.1 4.8 %collective-permute-start.10 = (f32[4,128,512]{2,1,0:T(8,128)}, f32[4,128,512]{2,1,0:T(8,128)S(1)}, u32[]{:S(2)}, u32[]{:S(2)}) collective-permute-start(f32[4,128,512]{2,1,0:T(8,128)} %get-tuple-element.40), channel_id=1, source_target_pairs={{0,1},{1,0},{2,3},{3,2},{4,5},{5,4},{6,7},{7,6},{8,9},{9,8},{10,11... | collective-permute-start | bytes 3145736 | tf_op jit(solution)/shard_map/ppermute | solution.py:25
  60.4 26.0 %collective-permute-start.11 = (bf16[256,512]{1,0:T(8,128)(2,1)}, bf16[256,512]{1,0:T(8,128)(2,1)}, u32[]{:S(2)}, u32[]{:S(2)}) collective-permute-start(bf16[256,512]{1,0:T(8,128)(2,1)} %get-tuple-element.44), channel_id=1, source_target_pairs={{0,8},{1,9},{2,10},{3,11},{4,12},{5,13},{6,14},{7,15},{8,0},{9,1},... | collective-permute-start | bytes 786440 | tf_op jit(solution)/shard_map/ppermute | solution.py:25
  61.8 26.2 %collective-permute-start.12 = (bf16[256,512]{1,0:T(8,128)(2,1)}, bf16[256,512]{1,0:T(8,128)(2,1)}, u32[]{:S(2)}, u32[]{:S(2)}) collective-permute-start(bf16[256,512]{1,0:T(8,128)(2,1)} %get-tuple-element.45), channel_id=1, source_target_pairs={{0,16},{1,17},{2,18},{3,19},{4,20},{5,21},{6,22},{7,23},{8,24},{9,... | collective-permute-start | bytes 786440 | tf_op jit(solution)/shard_map/ppermute | solution.py:25
  64.5 23.4 %collective-permute-start.13 = (bf16[256,512]{1,0:T(8,128)(2,1)}, bf16[256,512]{1,0:T(8,128)(2,1)}, u32[]{:S(2)}, u32[]{:S(2)}) collective-permute-start(bf16[256,512]{1,0:T(8,128)(2,1)} %get-tuple-element.46), channel_id=1, source_target_pairs={{0,24},{1,25},{2,26},{3,27},{4,28},{5,29},{6,30},{7,31},{8,16},{9,... | collective-permute-start | bytes 786440 | tf_op jit(solution)/shard_map/ppermute | solution.py:25
  66.2 16.1 %copy-start = (bf16[128,8192]{1,0:T(8,128)(2,1)S(1)}, bf16[128,8192]{1,0:T(8,128)(2,1)}, u32[]{:S(2)}) copy-start(bf16[128,8192]{1,0:T(8,128)(2,1)} %x_ref.3) | copy-start | bytes 6291460
  66.3 16.1 %copy-start.2 = (f32[128,1]{1,0:T(8,128)S(1)}, f32[128,1]{1,0:T(8,128)}, u32[]{:S(2)}) copy-start(f32[128,1]{1,0:T(8,128)} %get-tuple-element.42.scale_ref) | copy-start | bytes 1540
  79.6 11.0 %collective-permute-start.16 = (bf16[128,512]{1,0:T(8,128)(2,1)S(1)}, bf16[128,512]{1,0:T(8,128)(2,1)S(1)}, u32[]{:S(2)}, u32[]{:S(2)}) collective-permute-start(bf16[128,512]{1,0:T(8,128)(2,1)S(1)} %get-tuple-element.65), channel_id=1, source_target_pairs={{0,6},{1,7},{2,4},{3,5},{4,2},{5,3},{6,0},{7,1},{8,14},{9,15},{10,... | collective-permute-start | bytes 393224 | tf_op jit(solution)/shard_map/ppermute | solution.py:25
  80.8 9.7 %collective-permute-start.15 = (bf16[128,512]{1,0:T(8,128)(2,1)S(1)}, bf16[128,512]{1,0:T(8,128)(2,1)S(1)}, u32[]{:S(2)}, u32[]{:S(2)}) collective-permute-start(bf16[128,512]{1,0:T(8,128)(2,1)S(1)} %get-tuple-element.66), channel_id=1, source_target_pairs={{0,4},{1,5},{2,6},{3,7},{4,0},{5,1},{6,2},{7,3},{8,12},{9,13},{10,... | collective-permute-start | bytes 393224 | tf_op jit(solution)/shard_map/ppermute | solution.py:25
  82.3 5.6 %copy-start.8 = (f32[256,512]{1,0:T(8,128)S(1)}, f32[256,512]{1,0:T(8,128)}, u32[]{:S(2)}) copy-start(f32[256,512]{1,0:T(8,128)} %get-tuple-element.52) | copy-start | bytes 1572868
  86.4 5.1 %collective-permute-start.14 = (bf16[128,512]{1,0:T(8,128)(2,1)S(1)}, bf16[128,512]{1,0:T(8,128)(2,1)S(1)}, u32[]{:S(2)}, u32[]{:S(2)}) collective-permute-start(bf16[128,512]{1,0:T(8,128)(2,1)S(1)} %get-tuple-element.67), channel_id=1, source_target_pairs={{0,2},{1,3},{2,0},{3,1},{4,6},{5,7},{6,4},{7,5},{8,10},{9,11},{10,... | collective-permute-start | bytes 393224 | tf_op jit(solution)/shard_map/ppermute | solution.py:25
